TPU v7x, 32 devices: a whole 2x2x4 slice. The times are simulated.
32 devices in a mesh: row: 2 (over y), col: 16 (over z, x, core).
Axes of the slice: x: 2, y: 2, z: 4, core: 2. Of those that a mesh axis runs over, the one named last changes fastest.
Arguments:
- left_emb: float32 [2, 1536, 400], P('row', 'col'), may hold values from -2 to 2
- left_state: float32 [2, 1536], P('row', 'col'), may hold values from 0.001 to 1
- right_emb: float32 [16, 512, 400], P('col', 'row'), may hold values from -2 to 2
- right_state: float32 [16, 512], P('col', 'row'), may hold values from 0.001 to 1
- relation: float32 [64, 400], replicated, may hold values from -2 to 2
- rel_state: float32 [64], replicated, may hold values from 0.001 to 1
- left_ids: int32 [2, 16, 4000], P('row', 'col'), may hold values from 0 to 1535
- rel_ids: int32 [2, 16, 4000], P('row', 'col'), may hold values from 0 to 63
- right_ids: int32 [2, 16, 4000], P('row', 'col'), may hold values from 0 to 511
- neg_ids: int32 [2, 16, 4, 1000], P('row', 'col'), may hold values from 0 to 511
- counts: int32 [2, 16], P('row', 'col'), may hold values from 2000 to 4000, as said below
Outputs:
- new_left: float32 [2, 1536, 400], P('row', 'col')
- new_left_state: float32 [2, 1536], P('row', 'col')
- new_right: float32 [16, 512, 400], P('col', 'row')
- new_right_state: float32 [16, 512], P('col', 'row')
- new_rel: float32 [64, 400], replicated
- new_rel_state: float32 [64], replicated
Inputs may be any that keep to these rules, and one draw needn't show every extreme that they name: `counts`: slots at or beyond a bucket's count are padding. Some bucket is full and some bucket holds exactly 2000 edges in every draw.
All inputs are finite; a program needn't handle non-finite values.
Results may differ from a plain program's by a relative error of at most 0.0003.
The roundings to bfloat16 on the way count: a program that leaves them out, or rounds other values in their place, can miss the bound.
Values may be sent and summed in bfloat16 or wider, within the bound.
No kernel may reach another device: no remote copies, remote signals or barrier semaphores. Data moves between devices by JAX's collectives and lax.ppermute only.
A program may use at most 128 MiB of HBM per device.

v0:
```python
import jax
import jax.numpy as jnp
from jax import lax
from jax.sharding import PartitionSpec as P

CH = 1000


learn_rate = 0.1
epsilon = 1e-10


def complex_mul(first, second):
    half_width = first.shape[-1] // 2
    first_re, first_im = (first[..., :half_width], first[..., half_width:])
    second_re, second_im = (second[..., :half_width], second[..., half_width:])
    return jnp.concatenate(
        [first_re * second_re - first_im * second_im, first_re * second_im + first_im * second_re],
        axis=-1,
    )


def complex_back(upstream, other):
    half_width = upstream.shape[-1] // 2
    up_re, up_im = (upstream[..., :half_width], upstream[..., half_width:])
    other_re, other_im = (other[..., :half_width], other[..., half_width:])
    return jnp.concatenate(
        [up_re * other_re + up_im * other_im, up_im * other_re - up_re * other_im], axis=-1
    )


def group_update(
    gradients,
    left_part,
    right_part,
    relation,
    left_slots,
    rel_slots,
    right_slots,
    neg_slots,
    valid_rows,
):
    grad_left, grad_right, grad_rel = gradients
    rel_table = (
        rel_slots[:, None] == jnp.arange(relation.shape[0], dtype=jnp.int32)[None, :]
    ).astype(jnp.float32)
    left_vec = left_part[left_slots].astype(jnp.float32)
    rel_vec = jnp.dot(
        rel_table, relation, precision=lax.Precision.HIGHEST, preferred_element_type=jnp.float32
    )
    target = right_part[right_slots]
    negative = right_part[neg_slots]
    queries = complex_mul(left_vec, rel_vec).astype(jnp.bfloat16)
    scores = jnp.dot(queries, negative.T, preferred_element_type=jnp.float32)
    positive = jnp.sum(queries.astype(jnp.float32) * target.astype(jnp.float32), axis=-1)
    highest = jnp.maximum(jnp.max(scores, axis=-1), positive)
    expo = jnp.exp(scores - highest[:, None])
    expo_pos = jnp.exp(positive - highest)
    totals = expo_pos + jnp.sum(expo, axis=-1)
    mask_value = valid_rows.astype(jnp.float32)
    probability = (expo * (mask_value / totals)[:, None]).astype(jnp.bfloat16)
    pos_coeff = (expo_pos / totals - 1.0) * mask_value
    d_query = pos_coeff[:, None] * target.astype(jnp.float32) + jnp.dot(
        probability, negative, preferred_element_type=jnp.float32
    )
    d_negative = jnp.dot(probability.T, queries, preferred_element_type=jnp.float32)
    d_target = pos_coeff[:, None] * queries.astype(jnp.float32)
    d_left = complex_back(d_query, rel_vec)
    d_rel = complex_back(d_query, left_vec)
    grad_left = grad_left.at[left_slots].add(d_left)
    grad_right = grad_right.at[right_slots].add(d_target).at[neg_slots].add(d_negative)
    grad_rel = grad_rel + jnp.dot(
        rel_table.T, d_rel, precision=lax.Precision.HIGHEST, preferred_element_type=jnp.float32
    )
    return (grad_left, grad_right, grad_rel)


def row_adagrad(embedding, accumulator, gradient):
    new_accum = accumulator + jnp.mean(gradient * gradient, axis=-1)
    return (
        embedding - learn_rate * gradient / (jnp.sqrt(new_accum)[..., None] + epsilon),
        new_accum,
    )


def body(
    left_emb,
    left_state,
    right_emb,
    right_state,
    relation,
    rel_state,
    left_ids,
    rel_ids,
    right_ids,
    neg_ids,
    counts,
):
    left_part = lax.all_gather(left_emb[0].astype(jnp.bfloat16), "col", axis=0, tiled=True)
    right_part = lax.all_gather(right_emb[0].astype(jnp.bfloat16), "row", axis=0, tiled=True)
    edge_count = counts[0, 0]
    width = relation.shape[1]
    my_left = left_ids[0, 0]
    my_rel = rel_ids[0, 0]
    my_right = right_ids[0, 0]
    my_neg = neg_ids[0, 0]

    def group_step(group_index, gradients):
        group_start = group_index * CH
        left_slots = lax.dynamic_slice_in_dim(my_left, group_start, CH, 0)
        rel_slots = lax.dynamic_slice_in_dim(my_rel, group_start, CH, 0)
        right_slots = lax.dynamic_slice_in_dim(my_right, group_start, CH, 0)
        neg_slots = lax.dynamic_index_in_dim(my_neg, group_index, 0, keepdims=False)
        valid_rows = group_start + jnp.arange(CH, dtype=jnp.int32) < edge_count
        return group_update(
            gradients,
            left_part,
            right_part,
            relation,
            left_slots,
            rel_slots,
            right_slots,
            neg_slots,
            valid_rows,
        )

    start_grads = (
        jnp.zeros((left_part.shape[0], width), jnp.float32),
        jnp.zeros((right_part.shape[0], width), jnp.float32),
        jnp.zeros(relation.shape, jnp.float32),
    )
    group_total = (edge_count + CH - 1) // CH
    grad_left, grad_right, grad_rel = lax.fori_loop(0, group_total, group_step, start_grads)
    rel_grad = lax.psum(grad_rel, ("row", "col"))
    share_rows = left_emb.shape[1]
    left_whole = lax.psum(grad_left, "col")
    left_grad = lax.dynamic_slice_in_dim(
        left_whole, lax.axis_index("col") * share_rows, share_rows, 0
    )
    right_grad = lax.psum_scatter(grad_right, "row", scatter_dimension=0, tiled=True)
    new_left, new_left_state = row_adagrad(left_emb[0], left_state[0], left_grad)
    new_right, new_right_state = row_adagrad(right_emb[0], right_state[0], right_grad)
    new_rel, new_rel_state = row_adagrad(relation, rel_state, rel_grad)
    return (
        new_left[None],
        new_left_state[None],
        new_right[None],
        new_right_state[None],
        new_rel,
        new_rel_state,
    )


def solution(mesh):
    return jax.shard_map(
        body,
        mesh=mesh,
        in_specs=(
            P("row", "col", None),
            P("row", "col"),
            P("col", "row", None),
            P("col", "row"),
            P(),
            P(),
            P("row", "col", None),
            P("row", "col", None),
            P("row", "col", None),
            P("row", "col", None, None),
            P("row", "col"),
        ),
        out_specs=(
            P("row", "col", None),
            P("row", "col"),
            P("col", "row", None),
            P("col", "row"),
            P(),
            P(),
        ),
        check_vma=False,
    )
```

profile of v0, /device:TPU:0, one launch (start us, length us, event | category | flops | bytes accessed | tf_op | source)
XLA Modules:
  0.0 603.7 jit_solution(2458668032158724540)
XLA Ops:
  10.6 8.7 %all_gather.7 = bf16[512,400]{0,1:T(8,128)(2,1)S(1)} all-gather(bf16[256,400]{0,1:T(8,128)(2,1)S(1)} %bitcast_convert_fusion), channel_id=1, replica_groups=mesh['row'=2,'col'=16] {'row'}, dimensions={0}, use_global_device_ids=true | all-gather | bytes 614400 | tf_op jit(solution)/shard_map/all_gather | solution.py:100
  19.5 33.8 %all-gather.2.cloned.1.call-done = bf16[1536,400]{1,0:T(8,128)(2,1)} async-done(((bf16[96,400]{1,0:T(8,128)(2,1)}), bf16[1536,400]{1,0:T(8,128)(2,1)}) %all-gather.2.cloned.1.call-update) | async-done | bytes 1228816 | tf_op jit(solution)/shard_map/all_gather | solution.py:99
  56.1 291.0 %while.16 = (s32[]{:T(128)}, f32[1536,400]{1,0:T(8,128)}, f32[512,400]{1,0:T(8,128)S(1)}, f32[64,400]{1,0:T(8,128)}, s32[]{:T(128)}, /*index=5*/s32[4000]{0:T(10...) while((s32[]{:T(128)}, f32[1536,400]{1,0:T(8,128)}, ...), condition=%wide.region_7.8_spmd, body=%wide.region_0.7_spmd.sunk | while | flops 3039236608 | bytes 85821752 | solution.py:133
  64.1 5.1 gather_fusion
  71.4 5.1 gather_fusion.2
  102.7 7.7 %scatter_fusion.1 = f32[512,400]{1,0:T(8,128)S(1)} fusion(f32[512,400]{1,0:T(8,128)S(1)} %get-tuple-element.369, s32[1000]{0:T(1024)S(1)} %copy-done.14, f32[1000,400]{1,0:T(8,128)} %copy.36), kind=kCustom, calls=%fused_computation.4.clone.1 | custom fusion | flops 400000 | bytes 4804000 | tf_op jit(solution)/shard_map/while/body/scatter-add | solution.py:71
  110.4 7.7 %scatter_fusion.2 = f32[512,400]{1,0:T(8,128)S(1)} fusion(f32[512,400]{1,0:T(8,128)S(1)} %scatter_fusion.1, s32[1000]{0:T(1024)S(1)} %bitcast.47, f32[1000,400]{1,0:T(8,128)} %fusion.48), kind=kCustom, calls=%fused_computation.5.clone.1 | custom fusion | flops 400000 | bytes 4804000 | tf_op jit(solution)/shard_map/while/body/scatter-add | solution.py:71
  118.1 10.8 %scatter_fusion = f32[1536,400]{1,0:T(8,128)} fusion(f32[1536,400]{1,0:T(8,128)} %get-tuple-element.368, s32[1000]{0:T(1024)S(1)} %copy-done.12, f32[1000,400]{1,0:T(8,128)} %copy.35), kind=kCustom, calls=%fused_computation.3.clone.1 | custom fusion | flops 400000 | bytes 4804000 | tf_op jit(solution)/shard_map/while/body/scatter-add | solution.py:70
  136.9 5.1 gather_fusion
  144.2 5.1 gather_fusion.2
  175.5 7.7 %scatter_fusion.1 = f32[512,400]{1,0:T(8,128)S(1)} fusion(f32[512,400]{1,0:T(8,128)S(1)} %get-tuple-element.369, s32[1000]{0:T(1024)S(1)} %copy-done.14, f32[1000,400]{1,0:T(8,128)} %copy.36), kind=kCustom, calls=%fused_computation.4.clone.1 | custom fusion | flops 400000 | bytes 4804000 | tf_op jit(solution)/shard_map/while/body/scatter-add | solution.py:71
  183.1 7.7 %scatter_fusion.2 = f32[512,400]{1,0:T(8,128)S(1)} fusion(f32[512,400]{1,0:T(8,128)S(1)} %scatter_fusion.1, s32[1000]{0:T(1024)S(1)} %bitcast.47, f32[1000,400]{1,0:T(8,128)} %fusion.48), kind=kCustom, calls=%fused_computation.5.clone.1 | custom fusion | flops 400000 | bytes 4804000 | tf_op jit(solution)/shard_map/while/body/scatter-add | solution.py:71
  190.8 10.8 %scatter_fusion = f32[1536,400]{1,0:T(8,128)} fusion(f32[1536,400]{1,0:T(8,128)} %get-tuple-element.368, s32[1000]{0:T(1024)S(1)} %copy-done.12, f32[1000,400]{1,0:T(8,128)} %copy.35), kind=kCustom, calls=%fused_computation.3.clone.1 | custom fusion | flops 400000 | bytes 4804000 | tf_op jit(solution)/shard_map/while/body/scatter-add | solution.py:70
  209.6 5.1 gather_fusion
  248.2 7.7 %scatter_fusion.1 = f32[512,400]{1,0:T(8,128)S(1)} fusion(f32[512,400]{1,0:T(8,128)S(1)} %get-tuple-element.369, s32[1000]{0:T(1024)S(1)} %copy-done.14, f32[1000,400]{1,0:T(8,128)} %copy.36), kind=kCustom, calls=%fused_computation.4.clone.1 | custom fusion | flops 400000 | bytes 4804000 | tf_op jit(solution)/shard_map/while/body/scatter-add | solution.py:71
  255.9 7.7 %scatter_fusion.2 = f32[512,400]{1,0:T(8,128)S(1)} fusion(f32[512,400]{1,0:T(8,128)S(1)} %scatter_fusion.1, s32[1000]{0:T(1024)S(1)} %bitcast.47, f32[1000,400]{1,0:T(8,128)} %fusion.48), kind=kCustom, calls=%fused_computation.5.clone.1 | custom fusion | flops 400000 | bytes 4804000 | tf_op jit(solution)/shard_map/while/body/scatter-add | solution.py:71
  263.6 10.8 %scatter_fusion = f32[1536,400]{1,0:T(8,128)} fusion(f32[1536,400]{1,0:T(8,128)} %get-tuple-element.368, s32[1000]{0:T(1024)S(1)} %copy-done.12, f32[1000,400]{1,0:T(8,128)} %copy.35), kind=kCustom, calls=%fused_computation.3.clone.1 | custom fusion | flops 400000 | bytes 4804000 | tf_op jit(solution)/shard_map/while/body/scatter-add | solution.py:70
  282.4 5.1 gather_fusion
  321.0 7.7 %scatter_fusion.1 = f32[512,400]{1,0:T(8,128)S(1)} fusion(f32[512,400]{1,0:T(8,128)S(1)} %get-tuple-element.369, s32[1000]{0:T(1024)S(1)} %copy-done.14, f32[1000,400]{1,0:T(8,128)} %copy.36), kind=kCustom, calls=%fused_computation.4.clone.1 | custom fusion | flops 400000 | bytes 4804000 | tf_op jit(solution)/shard_map/while/body/scatter-add | solution.py:71
  328.7 7.7 %scatter_fusion.2 = f32[512,400]{1,0:T(8,128)S(1)} fusion(f32[512,400]{1,0:T(8,128)S(1)} %scatter_fusion.1, s32[1000]{0:T(1024)S(1)} %bitcast.47, f32[1000,400]{1,0:T(8,128)} %fusion.48), kind=kCustom, calls=%fused_computation.5.clone.1 | custom fusion | flops 400000 | bytes 4804000 | tf_op jit(solution)/shard_map/while/body/scatter-add | solution.py:71
  336.4 10.8 %scatter_fusion = f32[1536,400]{1,0:T(8,128)} fusion(f32[1536,400]{1,0:T(8,128)} %get-tuple-element.368, s32[1000]{0:T(1024)S(1)} %copy-done.12, f32[1000,400]{1,0:T(8,128)} %copy.35), kind=kCustom, calls=%fused_computation.3.clone.1 | custom fusion | flops 400000 | bytes 4804000 | tf_op jit(solution)/shard_map/while/body/scatter-add | solution.py:70
  349.2 119.4 %all-reduce.5.cloned.1.call-done = f32[64,400]{1,0:T(8,128)} async-done(((f32[64,400]{1,0:T(8,128)}), f32[64,400]{1,0:T(8,128)}) %all-reduce.5.cloned.1.call-update) | async-done | bytes 102416 | tf_op jit(solution)/shard_map/psum | solution.py:134
  471.8 102.9 %all-reduce.3.cloned.1.call-done = f32[1536,400]{1,0:T(8,128)} async-done(((f32[1536,400]{1,0:T(8,128)}), f32[1536,400]{1,0:T(8,128)}) %all-reduce.3.cloned.1.call-update) | async-done | bytes 2457616 | tf_op jit(solution)/shard_map/psum | solution.py:136
  578.0 15.7 %reduce-scatter.2.cloned.1.call-done = f32[256,400]{0,1:T(8,128)} async-done(((f32[512,400]{0,1:T(8,128)}), f32[256,400]{0,1:T(8,128)}) %reduce-scatter.2.cloned.1.call-update) | async-done | bytes 409616 | tf_op jit(solution)/shard_map/reduce_scatter | solution.py:140
  (246 shorter events, 172.9 us)
Async XLA Ops:
  7.2 46.1 %all-gather.2.cloned.1.call-start = ((), (), s32[]{:S(2)}) async-start(), calls=%async_computation.1 | async-start | bytes 1671168 | tf_op jit(solution)/shard_map/all_gather | solution.py:99
  8.8 459.8 %all-reduce.5.cloned.1.call-start = ((), (), s32[]{:S(2)}) async-start(), calls=%async_computation.4 | async-start | bytes 262144 | tf_op jit(solution)/shard_map/psum | solution.py:134
  57.6 22.5 %copy-start.7 = (s32[1000]{0:T(1024)}, s32[1000]{0:T(1024)S(1)}, u32[]{:S(2)}) copy-start(s32[1000]{0:T(1024)S(1)} %dynamic_slice.39) | copy-start | bytes 12004 | tf_op jit(solution)/shard_map/while
  102.7 7.7 %copy-start.10 = (s32[1000,1]{0,1:T(1,128)S(1)}, s32[1000,1]{0,1:T(1,128)}, u32[]{:S(2)}) copy-start(s32[1000,1]{0,1:T(1,128)} %copy-done.9) | copy-start | bytes 12004 | tf_op jit(solution)/shard_map/while
  110.4 7.7 %copy-start.12 = (s32[1000]{0:T(1024)S(1)}, s32[1000]{0:T(1024)}, u32[]{:S(2)}) copy-start(s32[1000]{0:T(1024)} %copy-done.11) | copy-start | bytes 12004 | tf_op jit(solution)/shard_map/while
  118.1 10.8 %copy-start.5 = (f32[64,400]{1,0:T(8,128)S(1)}, f32[64,400]{1,0:T(8,128)}, u32[]{:S(2)}) copy-start(f32[64,400]{1,0:T(8,128)} %get-tuple-element.428) | copy-start | bytes 307204 | tf_op jit(solution)/shard_map/while
  130.4 22.5 %copy-start.7 = (s32[1000]{0:T(1024)}, s32[1000]{0:T(1024)S(1)}, u32[]{:S(2)}) copy-start(s32[1000]{0:T(1024)S(1)} %dynamic_slice.39) | copy-start | bytes 12004 | tf_op jit(solution)/shard_map/while
  175.5 7.7 %copy-start.10 = (s32[1000,1]{0,1:T(1,128)S(1)}, s32[1000,1]{0,1:T(1,128)}, u32[]{:S(2)}) copy-start(s32[1000,1]{0,1:T(1,128)} %copy-done.9) | copy-start | bytes 12004 | tf_op jit(solution)/shard_map/while
  183.1 7.7 %copy-start.12 = (s32[1000]{0:T(1024)S(1)}, s32[1000]{0:T(1024)}, u32[]{:S(2)}) copy-start(s32[1000]{0:T(1024)} %copy-done.11) | copy-start | bytes 12004 | tf_op jit(solution)/shard_map/while
  190.8 10.8 %copy-start.5 = (f32[64,400]{1,0:T(8,128)S(1)}, f32[64,400]{1,0:T(8,128)}, u32[]{:S(2)}) copy-start(f32[64,400]{1,0:T(8,128)} %get-tuple-element.428) | copy-start | bytes 307204 | tf_op jit(solution)/shard_map/while
  203.1 22.5 %copy-start.7 = (s32[1000]{0:T(1024)}, s32[1000]{0:T(1024)S(1)}, u32[]{:S(2)}) copy-start(s32[1000]{0:T(1024)S(1)} %dynamic_slice.39) | copy-start | bytes 12004 | tf_op jit(solution)/shard_map/while
  248.2 7.7 %copy-start.10 = (s32[1000,1]{0,1:T(1,128)S(1)}, s32[1000,1]{0,1:T(1,128)}, u32[]{:S(2)}) copy-start(s32[1000,1]{0,1:T(1,128)} %copy-done.9) | copy-start | bytes 12004 | tf_op jit(solution)/shard_map/while
  255.9 7.7 %copy-start.12 = (s32[1000]{0:T(1024)S(1)}, s32[1000]{0:T(1024)}, u32[]{:S(2)}) copy-start(s32[1000]{0:T(1024)} %copy-done.11) | copy-start | bytes 12004 | tf_op jit(solution)/shard_map/while
  263.6 10.8 %copy-start.5 = (f32[64,400]{1,0:T(8,128)S(1)}, f32[64,400]{1,0:T(8,128)}, u32[]{:S(2)}) copy-start(f32[64,400]{1,0:T(8,128)} %get-tuple-element.428) | copy-start | bytes 307204 | tf_op jit(solution)/shard_map/while
  275.9 22.5 %copy-start.7 = (s32[1000]{0:T(1024)}, s32[1000]{0:T(1024)S(1)}, u32[]{:S(2)}) copy-start(s32[1000]{0:T(1024)S(1)} %dynamic_slice.39) | copy-start | bytes 12004 | tf_op jit(solution)/shard_map/while
  328.7 7.7 %copy-start.12 = (s32[1000]{0:T(1024)S(1)}, s32[1000]{0:T(1024)}, u32[]{:S(2)}) copy-start(s32[1000]{0:T(1024)} %copy-done.11) | copy-start | bytes 12004 | tf_op jit(solution)/shard_map/while
  336.3 10.8 %copy-start.5 = (f32[64,400]{1,0:T(8,128)S(1)}, f32[64,400]{1,0:T(8,128)}, u32[]{:S(2)}) copy-start(f32[64,400]{1,0:T(8,128)} %get-tuple-element.428) | copy-start | bytes 307204 | tf_op jit(solution)/shard_map/while
  347.2 227.5 %all-reduce.3.cloned.1.call-start = ((), (), s32[]{:S(2)}) async-start(), calls=%async_computation.2 | async-start | bytes 6291456 | tf_op jit(solution)/shard_map/psum | solution.py:136
  347.9 121.7 %copy-start.18 = (f32[64]{0:T(128)S(1)}, f32[64]{0:T(128)}, u32[]{:S(2)}) copy-start(f32[64]{0:T(128)} %param.18) | copy-start | bytes 772
  347.9 227.8 %copy-start.19 = (f32[1,96]{1,0:T(1,128)S(1)}, f32[1,96]{1,0:T(1,128)}, u32[]{:S(2)}) copy-start(f32[1,96]{1,0:T(1,128)} %param.14) | copy-start | bytes 1156
  347.9 228.4 %copy-start.15 = (f32[1,96,400]{2,1,0:T(8,128)S(1)}, f32[1,96,400]{2,1,0:T(8,128)}, u32[]{:S(2)}) copy-start(f32[1,96,400]{2,1,0:T(8,128)} %param.13) | copy-start | bytes 460804
  347.9 245.8 %reduce-scatter.2.cloned.1.call-start = ((), (), s32[]{:S(2)}) async-start(), calls=%async_computation.3 | async-start | bytes 1228800 | tf_op jit(solution)/shard_map/reduce_scatter | solution.py:140
  348.0 246.8 %copy-start.17 = (f32[1,256]{1,0:T(1,128)S(1)}, f32[1,256]{1,0:T(1,128)}, u32[]{:S(2)}) copy-start(f32[1,256]{1,0:T(1,128)} %param.16) | copy-start | bytes 3076
  348.0 247.4 %copy-start.6 = (f32[1,256,400]{1,2,0:T(8,128)S(1)}, f32[1,256,400]{1,2,0:T(8,128)}, u32[]{:S(2)}) copy-start(f32[1,256,400]{1,2,0:T(8,128)} %param.15) | copy-start | bytes 1228804
  (39 other events, 72.4 us)
Sparse Core Ops, SparseCore 0:
  10.9 42.3 all-gather.1
  347.3 121.2 all-reduce.4
  472.2 102.4 all-reduce.2
  576.8 16.8 reduce-scatter.1
where the time goes:
time: 606 us; the launch traced here: 604 us
  waiting for transfers between devices  272 us (45%)
  other arithmetic  155 us (26%)
  local copies, waits for them, and re-layouts  117 us (19%)
  matrix products  34.6 us (6%)
  between operations  14.5 us (2%)
  blocking collectives  8.71 us (1%)
    psum x1, waiting for transfers between devices, body(): rel_grad = lax.psum(grad_rel, ('row', 'col'))  119 us
    psum x1, waiting for transfers between devices, body(): left_whole = lax.psum(grad_left, 'col')  103 us
    scatter-add x8, other arithmetic, group_update(): grad_right.at[right_slots].add(d_target).at[neg_slots].add(d_negative)  61.3 us
    scatter-add x4, other arithmetic, group_update(): grad_left = grad_left.at[left_slots].add(d_left)  43.1 us
    all_gather x1, waiting for transfers between devices, body(): lax.all_gather(left_emb[0].astype(jnp.bfloat16), 'col', axis=0, tiled=True)  33.8 us
    gather x8, local copies, waits for them, and re-layouts, group_update(): target = right_part[right_slots]  29.4 us
    gather x8, local copies, waits for them, and re-layouts, group_update(): left_vec = left_part[left_slots].astype(jnp.float32)  29.3 us
    gather x4, local copies, waits for them, and re-layouts, group_update(): negative = right_part[neg_slots]  20.2 us
  transfers between devices with their start and end apart: 4, of which 4 were waited for; matrix products, arithmetic and copies ran while one was open for 1% of the time, Pallas kernels for 0%

commit v1 on v0

v1 whole, which is shorter than its diff:
```python
import functools

import jax
import jax.numpy as jnp
from jax import lax
from jax.experimental import pallas as pl
from jax.experimental.pallas import tpu as pltpu
from jax.sharding import PartitionSpec as P

CH = 1000
LANES = 128
TILE = 256

learn_rate = 0.1
epsilon = 1e-10
bf16 = jnp.bfloat16
f32 = jnp.float32


def round_up(value, step):
    return (value + step - 1) // step * step


def to_halves(array, half_pad):
    half = array.shape[-1] // 2
    pad = [(0, 0)] * (array.ndim - 1) + [(0, half_pad - half)]
    return jnp.concatenate([jnp.pad(array[..., :half], pad), jnp.pad(array[..., half:], pad)], axis=-1)


def from_halves(array, width):
    half_pad = array.shape[-1] // 2
    return jnp.concatenate([array[..., : width // 2], array[..., half_pad : half_pad + width // 2]], axis=-1)


def bits_of(size):
    return [1 << b for b in range(size.bit_length() - 1)]


def swap(array, axis, size, bit):
    return lax.ppermute(array, axis, [(i, i ^ bit) for i in range(size)])


def gather_chunks(array, axis, size):
    for bit in reversed(bits_of(size)):
        array = jnp.concatenate([array, swap(array, axis, size, bit)], axis=0)
    return array


def reduce_chunks(array, axis, size):
    for bit in bits_of(size):
        half = array.shape[0] // 2
        array = array[:half] + swap(array[half:], axis, size, bit)
    return array


def relative_ids(ids, axis, size, share):
    owner = ids // share
    within = ids - owner * share
    apart = owner ^ lax.axis_index(axis)
    place = jnp.zeros_like(apart)
    top = size.bit_length() - 2
    for b in range(top + 1):
        place = place | (((apart >> b) & 1) << (top - b))
    return place * share + within


def split_two(value):
    high = value.astype(bf16)
    return high, (value - high.astype(f32)).astype(bf16)


def dot(a, b):
    return jnp.dot(a, b, preferred_element_type=f32)


def edge_kernel(
    count_ref, ids_ref, mult_ref, left_ref, right_ref, rel_ref,
    query_ref, c_hi_ref, c_lo_ref, d_hi_ref, d_lo_ref, grad_rel_ref,
    rel_parts, right_t,
):
    step = pl.program_id(0)
    tile = ids_ref.shape[2]
    tiles_in_group = pl.num_programs(0) // mult_ref.shape[0]
    n_rel, wide = rel_ref.shape
    half = wide // 2
    n_left, n_right = left_ref.shape[0], right_ref.shape[0]
    rel_rows = rel_parts.shape[0]

    @pl.when(step == 0)
    def _():
        grad_rel_ref[...] = jnp.zeros_like(grad_rel_ref)
        rel_parts[...] = jnp.zeros_like(rel_parts)
        rest = rel_ref[...]
        for part in range(3):
            piece = rest.astype(bf16)
            rel_parts[part * n_rel : (part + 1) * n_rel, :] = piece
            rest = rest - piece.astype(f32)
        right_t[...] = right_ref[...].T

    group = step // tiles_in_group
    start = group * CH + (step - group * tiles_in_group) * tile

    @pl.when(start >= count_ref[0])
    def _():
        for ref in (query_ref, c_hi_ref, c_lo_ref, d_hi_ref, d_lo_ref):
            ref[...] = jnp.zeros_like(ref)

    @pl.when(start < count_ref[0])
    def _():
        ids = ids_ref[0]
        cols = ids.T
        left_col, rel_col, right_col = cols[:, 0:1], cols[:, 1:2], cols[:, 2:3]
        valid = cols[:, 3:4].astype(f32)
        rel_iota = lax.broadcasted_iota(jnp.int32, (tile, rel_rows), 1) % n_rel
        rel_hot = jnp.where(rel_iota == rel_col, 1.0, 0.0).astype(bf16)
        rel_vec = dot(rel_hot, rel_parts[...])
        left_iota = lax.broadcasted_iota(jnp.int32, (tile, n_left), 1)
        left_hot = jnp.where(left_iota == left_col, 1.0, 0.0).astype(bf16)
        left_vec = dot(left_hot, left_ref[...])
        a_re, a_im = left_vec[:, :half], left_vec[:, half:]
        b_re, b_im = rel_vec[:, :half], rel_vec[:, half:]
        query = jnp.concatenate([a_re * b_re - a_im * b_im, a_re * b_im + a_im * b_re], axis=1).astype(bf16)
        query_ref[...] = query
        scores = dot(query, right_t[...])
        mult = mult_ref[group]
        right_iota = lax.broadcasted_iota(jnp.int32, (tile, n_right), 1)
        is_target = right_iota == right_col
        positive = jnp.sum(jnp.where(is_target, scores, 0.0), axis=1, keepdims=True)
        masked = jnp.where(mult > 0.0, scores, -jnp.inf)
        highest = jnp.maximum(jnp.max(masked, axis=1, keepdims=True), positive)
        expo = jnp.exp(masked - highest)
        expo_pos = jnp.exp(positive - highest)
        totals = expo_pos + jnp.sum(expo * mult, axis=1, keepdims=True)
        probability = (expo * (valid / totals)).astype(bf16)
        pos_coeff = (expo_pos / totals - 1.0) * valid
        coeff = mult * probability.astype(f32) + jnp.where(is_target, pos_coeff, 0.0)
        c_hi, c_lo = split_two(coeff)
        c_hi_ref[...] = c_hi
        c_lo_ref[...] = c_lo
        d_query = dot(c_hi, right_ref[...]) + dot(c_lo, right_ref[...])
        g_re, g_im = d_query[:, :half], d_query[:, half:]
        d_left = jnp.concatenate([g_re * b_re + g_im * b_im, g_im * b_re - g_re * b_im], axis=1)
        d_hi, d_lo = split_two(d_left)
        d_hi_ref[...] = d_hi
        d_lo_ref[...] = d_lo
        d_rel = jnp.concatenate([g_re * a_re + g_im * a_im, g_im * a_re - g_re * a_im], axis=1)
        r_hi, r_lo = split_two(d_rel)
        row_iota = lax.broadcasted_iota(jnp.int32, (n_rel, tile), 0)
        rel_hot_t = jnp.where(row_iota == ids[1:2, :], 1.0, 0.0).astype(bf16)
        grad_rel_ref[...] += dot(rel_hot_t, r_hi) + dot(rel_hot_t, r_lo)


def left_kernel(groups_ref, ids_ref, d_hi_ref, d_lo_ref, out_ref):
    rows = out_ref.shape[0]
    edges = ids_ref.shape[2]
    out_ref[...] = jnp.zeros_like(out_ref)
    row_iota = lax.broadcasted_iota(jnp.int32, (rows, edges), 0) + pl.program_id(0) * rows

    def group_step(g, carry):
        hot = jnp.where(row_iota == ids_ref[g, 0:1, :], 1.0, 0.0).astype(bf16)
        here = pl.ds(pl.multiple_of(g * edges, edges), edges)
        out_ref[...] += dot(hot, d_hi_ref[here, :]) + dot(hot, d_lo_ref[here, :])
        return carry

    lax.fori_loop(0, groups_ref[0], group_step, 0)


def right_kernel(query_ref, c_hi_ref, c_lo_ref, out_ref, total):
    step = pl.program_id(0)

    @pl.when(step == 0)
    def _():
        total[...] = jnp.zeros_like(total)

    dims = (((0,), (0,)), ((), ()))
    query = query_ref[...]
    total[...] += lax.dot_general(query, c_hi_ref[...], dims, preferred_element_type=f32) + lax.dot_general(
        query, c_lo_ref[...], dims, preferred_element_type=f32
    )

    @pl.when(step == pl.num_programs(0) - 1)
    def _():
        out_ref[...] = total[...].T


def whole(shape):
    return pl.BlockSpec(shape, lambda *_: (0,) * len(shape))


def body(n_row, n_col, left_emb, left_state, right_emb, right_state, relation, rel_state, left_ids, rel_ids, right_ids, neg_ids, counts):
    width = relation.shape[1]
    half_pad = round_up(width // 2, LANES)
    wide = 2 * half_pad
    left_share, right_share = left_emb.shape[1], right_emb.shape[1]
    n_left, n_right, n_rel = left_share * n_col, right_share * n_row, relation.shape[0]
    groups = neg_ids.shape[2]
    edges = round_up(CH, TILE)
    slots = groups * edges
    tiles = edges // TILE

    right_part = gather_chunks(to_halves(right_emb[0].astype(bf16), half_pad), "row", n_row)
    left_part = gather_chunks(to_halves(left_emb[0].astype(bf16), half_pad), "col", n_col)
    edge_count = counts[0, 0]
    my_left = relative_ids(left_ids[0, 0], "col", n_col, left_share).reshape(groups, CH)
    my_right = relative_ids(right_ids[0, 0], "row", n_row, right_share).reshape(groups, CH)
    my_neg = relative_ids(neg_ids[0, 0], "row", n_row, right_share)
    my_rel = rel_ids[0, 0].reshape(groups, CH)
    valid = (jnp.arange(groups * CH, dtype=jnp.int32) < edge_count).astype(jnp.int32).reshape(groups, CH)
    ids = jnp.stack([my_left, my_rel, my_right, valid] + [jnp.zeros_like(valid)] * 4, axis=1)
    ids = jnp.pad(ids, ((0, 0), (0, 0), (0, edges - CH)))
    hot = jnp.arange(n_right, dtype=jnp.int32)[None, :, None] == my_neg[:, None, :]
    mult = jnp.sum(hot.astype(f32), axis=2)[:, None, :]
    count_arg = edge_count.reshape(1)
    group_arg = (count_arg + CH - 1) // CH

    smem = pl.BlockSpec(memory_space=pltpu.SMEM)
    tile_block = lambda lanes: pl.BlockSpec((TILE, lanes), lambda i: (i, 0))
    query, c_hi, c_lo, d_hi, d_lo, grad_rel = pl.pallas_call(
        edge_kernel,
        grid=(groups * tiles,),
        in_specs=[
            smem,
            pl.BlockSpec((1, 8, TILE), lambda i: (i // tiles, 0, i % tiles)),
            whole((groups, 1, n_right)),
            whole((n_left, wide)),
            whole((n_right, wide)),
            whole((n_rel, wide)),
        ],
        out_specs=[
            tile_block(wide),
            tile_block(n_right),
            tile_block(n_right),
            tile_block(wide),
            tile_block(wide),
            whole((n_rel, wide)),
        ],
        out_shape=[
            jax.ShapeDtypeStruct((slots, wide), bf16),
            jax.ShapeDtypeStruct((slots, n_right), bf16),
            jax.ShapeDtypeStruct((slots, n_right), bf16),
            jax.ShapeDtypeStruct((slots, wide), bf16),
            jax.ShapeDtypeStruct((slots, wide), bf16),
            jax.ShapeDtypeStruct((n_rel, wide), f32),
        ],
        scratch_shapes=[
            pltpu.VMEM((round_up(3 * n_rel, LANES), wide), bf16),
            pltpu.VMEM((wide, n_right), bf16),
        ],
        compiler_params=pltpu.CompilerParams(vmem_limit_bytes=48 << 20),
        name="edges",
    )(count_arg, ids, mult, left_part, right_part, to_halves(relation, half_pad))

    row_block = 256 if n_left % 256 == 0 else left_share
    grad_left = pl.pallas_call(
        left_kernel,
        grid=(n_left // row_block,),
        in_specs=[smem, whole((groups, 8, edges)), whole((slots, wide)), whole((slots, wide))],
        out_specs=pl.BlockSpec((row_block, wide), lambda i: (i, 0)),
        out_shape=jax.ShapeDtypeStruct((n_left, wide), f32),
        compiler_params=pltpu.CompilerParams(vmem_limit_bytes=48 << 20),
        name="left_sum",
    )(group_arg, ids, d_hi, d_lo)

    group_block = lambda lanes: pl.BlockSpec((edges, lanes), lambda i: (i, 0))
    grad_right = pl.pallas_call(
        right_kernel,
        grid=(groups,),
        in_specs=[group_block(wide), group_block(n_right), group_block(n_right)],
        out_specs=whole((n_right, wide)),
        out_shape=jax.ShapeDtypeStruct((n_right, wide), f32),
        scratch_shapes=[pltpu.VMEM((wide, n_right), f32)],
        compiler_params=pltpu.CompilerParams(vmem_limit_bytes=48 << 20),
        cost_estimate=pl.CostEstimate(flops=4 * slots * wide * n_right, bytes_accessed=6 * slots * wide, transcendentals=0),
        name="right_sum",
    )(query, c_hi, c_lo)

    for bit in bits_of(n_col):
        grad_rel = grad_rel + swap(grad_rel, "col", n_col, bit)
    for bit in bits_of(n_row):
        grad_rel = grad_rel + swap(grad_rel, "row", n_row, bit)
    grad_left = reduce_chunks(grad_left, "col", n_col)
    grad_right = reduce_chunks(grad_right, "row", n_row)

    def adagrad(embedding, accumulator, gradient):
        new_accum = accumulator + jnp.sum(gradient * gradient, axis=-1) / width
        gradient = from_halves(gradient, width)
        return embedding - learn_rate * gradient / (jnp.sqrt(new_accum)[..., None] + epsilon), new_accum

    new_left, new_left_state = adagrad(left_emb[0], left_state[0], grad_left)
    new_right, new_right_state = adagrad(right_emb[0], right_state[0], grad_right)
    new_rel, new_rel_state = adagrad(relation, rel_state, grad_rel)
    return new_left[None], new_left_state[None], new_right[None], new_right_state[None], new_rel, new_rel_state


def solution(mesh):
    entities = (P("row", "col", None), P("row", "col"), P("col", "row", None), P("col", "row"), P(), P())
    return jax.shard_map(
        functools.partial(body, mesh.shape["row"], mesh.shape["col"]),
        mesh=mesh,
        in_specs=entities + (P("row", "col", None),) * 3 + (P("row", "col", None, None), P("row", "col")),
        out_specs=entities,
        check_vma=False,
    )
```

time: 606 us -> 165 us (0.27)
  waiting for transfers between devices: 272 us -> 54.9 us
  other arithmetic: 155 us -> 18.2 us
  local copies, waits for them, and re-layouts: 117 us -> 7.13 us
  Pallas kernels: 0 us -> 50.5 us
  matrix products: 34.6 us -> 0 us
  starting transfers between devices: 0.16 us -> 31.4 us
  between operations: 14.5 us -> 1.76 us
  blocking collectives: 8.71 us -> 0 us
    psum x2 -> x0, waiting for transfers between devices: 222 us -> none  [the longest x1 119 us: body(): rel_grad = lax.psum(grad_rel, ('row', 'col'))]
    scatter-add x12 -> x0, other arithmetic: 104 us -> none  [the longest x8 61.3 us: group_update(): grad_right.at[right_slots].add(d_target).at[neg_slots].add(d_negative)]
    gather x20 -> x0, local copies, waits for them, and re-layouts: 78.9 us -> none  [the longest x8 29.4 us: group_update(): target = right_part[right_slots]]
    ppermute x0 -> x15, waiting for transfers between devices: none -> 54.9 us  [swap(): return lax.ppermute(array, axis, [(i, i ^ bit) for i in range(size)])]
    pallas_call x0 -> x3, Pallas kernels: none -> 50.5 us  [the longest x1 26.4 us: body(): pl.pallas_call(edge_kernel, grid=(groups * tiles,), in_specs=[smem, pl.Bl...]
    dot_general x20 -> x0, matrix products: 34.6 us -> none  [the longest x4 10.7 us: group_update(): jnp.dot(rel_table.T, d_rel, precision=lax.Precision.HIGHEST, preferred_el...]
    all_gather x1 -> x0, waiting for transfers between devices: 33.8 us -> none  [body(): lax.all_gather(left_emb[0].astype(jnp.bfloat16), 'col', axis=0, tiled=True)]
    ppermute x0 -> x15, starting transfers between devices: none -> 31.4 us  [swap(): return lax.ppermute(array, axis, [(i, i ^ bit) for i in range(size)])]
  transfers between devices with their start and end apart: 4 -> 15, of which waited for: 4 -> 9; matrix products, arithmetic and copies ran while one was open for 1% -> 12% of each run, Pallas kernels for 0% -> 5%
where the time goes in v1:
time: 165 us; the launch traced here: 164 us
  waiting for transfers between devices  54.9 us (33%)
  Pallas kernels  50.5 us (31%)
  starting transfers between devices  31.4 us (19%)
  other arithmetic  18.2 us (11%)
  local copies, waits for them, and re-layouts  7.13 us (4%)
  between operations  1.76 us (1%)
    ppermute x15, waiting for transfers between devices, swap(): return lax.ppermute(array, axis, [(i, i ^ bit) for i in range(size)])  54.9 us
    ppermute x15, starting transfers between devices, swap(): return lax.ppermute(array, axis, [(i, i ^ bit) for i in range(size)])  31.4 us
    pallas_call x1, Pallas kernels, body(): pl.pallas_call(edge_kernel, grid=(groups * tiles,), in_specs=[smem, pl.Bl...  26.4 us
    pallas_call x1, Pallas kernels, body(): pl.pallas_call(left_kernel, grid=(n_left // row_block,), in_specs=[smem,...  16.8 us
    pallas_call x1, Pallas kernels, body(): pl.pallas_call(right_kernel, grid=(groups,), in_specs=[group_block(wide),...  7.4 us
  transfers between devices with their start and end apart: 15, of which 9 were waited for; matrix products, arithmetic and copies ran while one was open for 12% of the time, Pallas kernels for 5%

profile of v1, /device:TPU:0, one launch (start us, length us, event | category | flops | bytes accessed | tf_op | source)
XLA Modules:
  0.0 163.9 jit_solution(947963530915721734)
XLA Ops:
  2.4 4.1 %collective-permute-start = (bf16[96,512]{1,0:T(8,128)(2,1)S(1)}, bf16[96,512]{1,0:T(8,128)(2,1)S(1)}, u32[]{:S(2)}, u32[]{:S(2)}) collective-permute-start(bf16[96,512]{1,0:T(8,128)(2,1)S(1)} %get-tuple-element.50), channel_id=1, source_target_pairs={{0,8},{1,9},{2,10},{3,11},{4,12},{5,13},{6,14},{7,15},{8,0},{9,1},... | collective-permute-start | bytes 294920 | tf_op jit(solution)/shard_map/ppermute | solution.py:40
  6.5 1.2 copy.25
  8.0 1.6 collective-permute-start.4
  11.7 1.6 %collective-permute-start.1 = (bf16[192,512]{1,0:T(8,128)(2,1)S(1)}, bf16[192,512]{1,0:T(8,128)(2,1)S(1)}, u32[]{:S(2)}, u32[]{:S(2)}) collective-permute-start(bf16[192,512]{1,0:T(8,128)(2,1)S(1)} %pad_maximum_fusion.4), channel_id=1, source_target_pairs={{0,4},{1,5},{2,6},{3,7},{4,0},{5,1},{6,2},{7,3},{8,12},{9,13},{10,... | collective-permute-start | bytes 589832 | tf_op jit(solution)/shard_map/ppermute | solution.py:40
  14.2 3.6 %collective-permute-done.1 = bf16[192,512]{1,0:T(8,128)(2,1)S(1)} collective-permute-done((bf16[192,512]{1,0:T(8,128)(2,1)S(1)}, bf16[192,512]{1,0:T(8,128)(2,1)S(1)}, u32[]{:S(2)}, u32[]{:S(2)}) %collective-permute-start.1) | collective-permute-done | bytes 196640 | tf_op jit(solution)/shard_map/ppermute | solution.py:40
  17.9 1.6 collective-permute-start.2
  20.2 1.3 slice_select_fusion.1
  21.5 5.8 %collective-permute-done.2 = bf16[384,512]{1,0:T(8,128)(2,1)S(1)} collective-permute-done((bf16[384,512]{1,0:T(8,128)(2,1)S(1)}, bf16[384,512]{1,0:T(8,128)(2,1)S(1)}, u32[]{:S(2)}, u32[]{:S(2)}) %collective-permute-start.2) | collective-permute-done | bytes 393248 | tf_op jit(solution)/shard_map/ppermute | solution.py:40
  28.3 1.6 convert_reduce_fusion
  30.6 1.4 reduce.10
  36.4 1.2 constant_dynamic-update-slice_fusion.left_ref
  37.6 26.4 %edges.1 = (bf16[4096,512]{1,0:T(8,128)(2,1)}, bf16[4096,512]{1,0:T(8,128)(2,1)}, bf16[4096,512]{1,0:T(8,128)(2,1)}, bf16[4096,512]{1,0:T(8,128)(2,1)}, bf16[409...) custom-call(s32[1]{0:T(128)} %bitcast.44.count_ref, s32[4,8,1024]{2,1,0:T(8,128)S(1)} %pad.25.ids_ref, ...), custom_call_target="tpu_custom_call" | custom-call | tf_op jit(solution)/shard_map/edges/pallas_call | solution.py:218
  63.9 16.8 %left_sum.1 = f32[1536,512]{1,0:T(8,128)S(1)} custom-call(s32[1]{0:T(128)S(6)} %select_n.36.groups_ref, s32[4,8,1024]{2,1,0:T(8,128)S(1)} %pad.25.ids_ref, bf16[4096,512]{1,0:T(8,128)(2,1)} %get-tuple-element.12.d_hi_ref, bf16[4096,512]{1,0:T(8,128)(2,1)} %get-tuple-element.13.d_lo_ref), custom_call_target="tpu_custom_call" | custom-call | tf_op jit(solution)/shard_map/left_sum/pallas_call | solution.py:254
  81.4 7.4 %right_sum.1 = f32[512,512]{1,0:T(8,128)S(1)} custom-call(bf16[4096,512]{1,0:T(8,128)(2,1)S(1)} %copy-done, bf16[4096,512]{1,0:T(8,128)(2,1)} %get-tuple-element.15.c_hi_ref, bf16[4096,512]{1,0:T(8,128)(2,1)} %get-tuple-element.16.c_lo_ref), custom_call_target="tpu_custom_call" | custom-call | flops 4294967296 | bytes 12582912 | tf_op jit(solution)/shard_map/right_sum/pallas_call | solution.py:265
  88.9 13.2 %collective-permute-start.9 = (f32[256,512]{1,0:T(8,128)S(1)}, f32[256,512]{1,0:T(8,128)S(1)}, u32[]{:S(2)}, u32[]{:S(2)}) collective-permute-start(f32[256,512]{1,0:T(8,128)S(1)} %slice.106), channel_id=1, source_target_pairs={{0,16},{16,0},{1,17},{17,1},{2,18},{18,2},{3,19},{19,3},{4,20},{20... | collective-permute-start | bytes 1572872 | tf_op jit(solution)/shard_map/ppermute | solution.py:40
  102.8 4.6 %collective-permute-done.11 = f32[64,512]{1,0:T(8,128)S(1)} collective-permute-done((f32[64,512]{1,0:T(8,128)S(1)}, f32[64,512]{1,0:T(8,128)S(1)}, u32[]{:S(2)}, u32[]{:S(2)}) %collective-permute-start.11) | collective-permute-done | bytes 131104 | tf_op jit(solution)/shard_map/ppermute | solution.py:40
  107.4 4.7 %collective-permute-start.12 = (f32[64,512]{1,0:T(8,128)S(1)}, f32[64,512]{1,0:T(8,128)S(1)}, u32[]{:S(2)}, u32[]{:S(2)}) collective-permute-start(f32[64,512]{1,0:T(8,128)S(1)} %add.168), channel_id=1, source_target_pairs={{0,4},{1,5},{2,6},{3,7},{4,0},{5,1},{6,2},{7,3},{8,12},{9,13},{10,... | collective-permute-start | bytes 393224 | tf_op jit(solution)/shard_map/ppermute | solution.py:40
  112.1 3.0 %collective-permute-done.12 = f32[64,512]{1,0:T(8,128)S(1)} collective-permute-done((f32[64,512]{1,0:T(8,128)S(1)}, f32[64,512]{1,0:T(8,128)S(1)}, u32[]{:S(2)}, u32[]{:S(2)}) %collective-permute-start.12) | collective-permute-done | bytes 131104 | tf_op jit(solution)/shard_map/ppermute | solution.py:40
  115.1 1.3 collective-permute-start.13
  116.4 6.6 %collective-permute-done.13 = f32[64,512]{1,0:T(8,128)S(1)} collective-permute-done((f32[64,512]{1,0:T(8,128)S(1)}, f32[64,512]{1,0:T(8,128)S(1)}, u32[]{:S(2)}, u32[]{:S(2)}) %collective-permute-start.13) | collective-permute-done | bytes 131104 | tf_op jit(solution)/shard_map/ppermute | solution.py:40
  129.2 13.9 %collective-permute-done.6 = f32[384,512]{1,0:T(8,128)} collective-permute-done((f32[384,512]{1,0:T(8,128)S(1)}, f32[384,512]{1,0:T(8,128)}, u32[]{:S(2)}, u32[]{:S(2)}) %collective-permute-start.6) | collective-permute-done | bytes 786464 | tf_op jit(solution)/shard_map/ppermute | solution.py:40
  143.1 1.3 slice_add_fusion.1
  145.0 8.4 %collective-permute-done.7 = f32[192,512]{1,0:T(8,128)S(1)} collective-permute-done((f32[192,512]{1,0:T(8,128)S(1)}, f32[192,512]{1,0:T(8,128)S(1)}, u32[]{:S(2)}, u32[]{:S(2)}) %collective-permute-start.7) | collective-permute-done | bytes 393248 | tf_op jit(solution)/shard_map/ppermute | solution.py:40
  154.3 8.1 %collective-permute-done.8 = f32[96,512]{1,0:T(8,128)S(1)} collective-permute-done((f32[96,512]{1,0:T(8,128)S(1)}, f32[96,512]{1,0:T(8,128)S(1)}, u32[]{:S(2)}, u32[]{:S(2)}) %collective-permute-start.8) | collective-permute-done | bytes 196640 | tf_op jit(solution)/shard_map/ppermute | solution.py:40
  (93 shorter events, 21.6 us)
Async XLA Ops:
  0.6 7.3 %copy-start.6 = (pred[256]{0:T(512)(128)(4,1)S(1)}, pred[256]{0:T(512)(128)(4,1)}, u32[]{:S(2)}) copy-start(pred[256]{0:T(512)(128)(4,1)} %constant.95.clone.1) | copy-start | bytes 772
  2.4 7.7 %copy-start.4 = (s32[1,1,4000]{2,1,0:T(1,128)S(1)}, s32[1,1,4000]{2,1,0:T(1,128)}, u32[]{:S(2)}) copy-start(s32[1,1,4000]{2,1,0:T(1,128)} %param.17) | copy-start | bytes 48004
  2.4 8.5 %copy-start.5 = (s32[1,1,4000]{2,1,0:T(1,128)S(1)}, s32[1,1,4000]{2,1,0:T(1,128)}, u32[]{:S(2)}) copy-start(s32[1,1,4000]{2,1,0:T(1,128)} %param.19) | copy-start | bytes 48004
  2.4 9.2 %collective-permute-start = (bf16[96,512]{1,0:T(8,128)(2,1)S(1)}, bf16[96,512]{1,0:T(8,128)(2,1)S(1)}, u32[]{:S(2)}, u32[]{:S(2)}) collective-permute-start(bf16[96,512]{1,0:T(8,128)(2,1)S(1)} %get-tuple-element.50), channel_id=1, source_target_pairs={{0,8},{1,9},{2,10},{3,11},{4,12},{5,13},{6,14},{7,15},{8,0},{9,1},... | collective-permute-start | bytes 294920 | tf_op jit(solution)/shard_map/ppermute | solution.py:40
  7.7 12.5 %copy-start.2 = (f32[64,400]{1,0:T(8,128)S(1)}, f32[64,400]{1,0:T(8,128)}, u32[]{:S(2)}) copy-start(f32[64,400]{1,0:T(8,128)} %param.15) | copy-start | bytes 307204
  8.0 27.3 %collective-permute-start.4 = (bf16[256,512]{1,0:T(8,128)(2,1)S(1)}, bf16[256,512]{1,0:T(8,128)(2,1)}, u32[]{:S(2)}, u32[]{:S(2)}) collective-permute-start(bf16[256,512]{1,0:T(8,128)(2,1)S(1)} %pad_maximum_fusion.3), channel_id=1, source_target_pairs={{0,16},{16,0},{1,17},{17,1},{2,18},{18,2},{3,19},{19,3},{4,20},{20... | collective-permute-start | bytes 786440 | tf_op jit(solution)/shard_map/ppermute | solution.py:40
  11.7 6.1 %collective-permute-start.1 = (bf16[192,512]{1,0:T(8,128)(2,1)S(1)}, bf16[192,512]{1,0:T(8,128)(2,1)S(1)}, u32[]{:S(2)}, u32[]{:S(2)}) collective-permute-start(bf16[192,512]{1,0:T(8,128)(2,1)S(1)} %pad_maximum_fusion.4), channel_id=1, source_target_pairs={{0,4},{1,5},{2,6},{3,7},{4,0},{5,1},{6,2},{7,3},{8,12},{9,13},{10,... | collective-permute-start | bytes 589832 | tf_op jit(solution)/shard_map/ppermute | solution.py:40
  17.9 9.4 %collective-permute-start.2 = (bf16[384,512]{1,0:T(8,128)(2,1)S(1)}, bf16[384,512]{1,0:T(8,128)(2,1)S(1)}, u32[]{:S(2)}, u32[]{:S(2)}) collective-permute-start(bf16[384,512]{1,0:T(8,128)(2,1)S(1)} %pad_maximum_fusion.2), channel_id=1, source_target_pairs={{0,2},{1,3},{2,0},{3,1},{4,6},{5,7},{6,4},{7,5},{8,10},{9,11},{10,... | collective-permute-start | bytes 1179656 | tf_op jit(solution)/shard_map/ppermute | solution.py:40
  28.3 8.1 %collective-permute-start.3 = (bf16[768,512]{1,0:T(8,128)(2,1)}, bf16[768,512]{1,0:T(8,128)(2,1)}, u32[]{:S(2)}, u32[]{:S(2)}) collective-permute-start(bf16[768,512]{1,0:T(8,128)(2,1)} %pad_maximum_fusion), channel_id=1, source_target_pairs={{0,1},{1,0},{2,3},{3,2},{4,5},{5,4},{6,7},{7,6},{8,9},{9,8},{10,11... | collective-permute-start | bytes 2359304 | tf_op jit(solution)/shard_map/ppermute | solution.py:40
  63.9 17.5 %copy-start = (bf16[4096,512]{1,0:T(8,128)(2,1)S(1)}, bf16[4096,512]{1,0:T(8,128)(2,1)}, u32[]{:S(2)}) copy-start(bf16[4096,512]{1,0:T(8,128)(2,1)} %get-tuple-element.14.query_ref) | copy-start | bytes 12582916
  80.8 43.4 %collective-permute-start.5 = (f32[768,512]{1,0:T(8,128)S(1)}, f32[768,512]{1,0:T(8,128)S(1)}, u32[]{:S(2)}, u32[]{:S(2)}) collective-permute-start(f32[768,512]{1,0:T(8,128)S(1)} %slice.96), channel_id=1, source_target_pairs={{0,1},{1,0},{2,3},{3,2},{4,5},{5,4},{6,7},{7,6},{8,9},{9,8},{10,11... | collective-permute-start | bytes 4718600 | tf_op jit(solution)/shard_map/ppermute | solution.py:40
  80.9 21.1 %collective-permute-start.10 = (f32[64,512]{1,0:T(8,128)S(1)}, f32[64,512]{1,0:T(8,128)S(1)}, u32[]{:S(2)}, u32[]{:S(2)}) collective-permute-start(f32[64,512]{1,0:T(8,128)S(1)} %get-tuple-element.17), channel_id=1, source_target_pairs={{0,1},{1,0},{2,3},{3,2},{4,5},{5,4},{6,7},{7,6},{8,9},{9,8},{10,11... | collective-permute-start | bytes 393224 | tf_op jit(solution)/shard_map/ppermute | solution.py:40
  88.9 35.2 %collective-permute-start.9 = (f32[256,512]{1,0:T(8,128)S(1)}, f32[256,512]{1,0:T(8,128)S(1)}, u32[]{:S(2)}, u32[]{:S(2)}) collective-permute-start(f32[256,512]{1,0:T(8,128)S(1)} %slice.106), channel_id=1, source_target_pairs={{0,16},{16,0},{1,17},{17,1},{2,18},{18,2},{3,19},{19,3},{4,20},{20... | collective-permute-start | bytes 1572872 | tf_op jit(solution)/shard_map/ppermute | solution.py:40
  102.1 5.3 %collective-permute-start.11 = (f32[64,512]{1,0:T(8,128)S(1)}, f32[64,512]{1,0:T(8,128)S(1)}, u32[]{:S(2)}, u32[]{:S(2)}) collective-permute-start(f32[64,512]{1,0:T(8,128)S(1)} %add.167), channel_id=1, source_target_pairs={{0,2},{1,3},{2,0},{3,1},{4,6},{5,7},{6,4},{7,5},{8,10},{9,11},{10,... | collective-permute-start | bytes 393224 | tf_op jit(solution)/shard_map/ppermute | solution.py:40
  107.4 7.7 %collective-permute-start.12 = (f32[64,512]{1,0:T(8,128)S(1)}, f32[64,512]{1,0:T(8,128)S(1)}, u32[]{:S(2)}, u32[]{:S(2)}) collective-permute-start(f32[64,512]{1,0:T(8,128)S(1)} %add.168), channel_id=1, source_target_pairs={{0,4},{1,5},{2,6},{3,7},{4,0},{5,1},{6,2},{7,3},{8,12},{9,13},{10,... | collective-permute-start | bytes 393224 | tf_op jit(solution)/shard_map/ppermute | solution.py:40
  115.1 7.9 %collective-permute-start.13 = (f32[64,512]{1,0:T(8,128)S(1)}, f32[64,512]{1,0:T(8,128)S(1)}, u32[]{:S(2)}, u32[]{:S(2)}) collective-permute-start(f32[64,512]{1,0:T(8,128)S(1)} %add.169), channel_id=1, source_target_pairs={{0,8},{1,9},{2,10},{3,11},{4,12},{5,13},{6,14},{7,15},{8,0},{9,1},... | collective-permute-start | bytes 393224 | tf_op jit(solution)/shard_map/ppermute | solution.py:40
  123.0 5.1 %collective-permute-start.14 = (f32[64,512]{1,0:T(8,128)S(1)}, f32[64,512]{1,0:T(8,128)}, u32[]{:S(2)}, u32[]{:S(2)}) collective-permute-start(f32[64,512]{1,0:T(8,128)S(1)} %add.170), channel_id=1, source_target_pairs={{0,16},{16,0},{1,17},{17,1},{2,18},{18,2},{3,19},{19,3},{4,20},{20... | collective-permute-start | bytes 393224 | tf_op jit(solution)/shard_map/ppermute | solution.py:40
  124.7 18.4 %collective-permute-start.6 = (f32[384,512]{1,0:T(8,128)S(1)}, f32[384,512]{1,0:T(8,128)}, u32[]{:S(2)}, u32[]{:S(2)}) collective-permute-start(f32[384,512]{1,0:T(8,128)S(1)} %slice.98), channel_id=1, source_target_pairs={{0,2},{1,3},{2,0},{3,1},{4,6},{5,7},{6,4},{7,5},{8,10},{9,11},{10,... | collective-permute-start | bytes 2359304 | tf_op jit(solution)/shard_map/ppermute | solution.py:40
  129.2 15.3 %copy-start.8 = (f32[64]{0:T(128)S(1)}, f32[64]{0:T(128)}, u32[]{:S(2)}) copy-start(f32[64]{0:T(128)} %param.16) | copy-start | bytes 772
  144.4 9.2 %copy-start.3 = (f32[64,400]{1,0:T(8,128)S(1)}, f32[64,400]{1,0:T(8,128)}, u32[]{:S(2)}) copy-start(f32[64,400]{1,0:T(8,128)} %param.15) | copy-start | bytes 307204
  144.4 18.1 %copy-start.9 = (f32[1,96]{1,0:T(1,128)S(1)}, f32[1,96]{1,0:T(1,128)}, u32[]{:S(2)}) copy-start(f32[1,96]{1,0:T(1,128)} %param.12) | copy-start | bytes 1156
  144.4 9.0 %collective-permute-start.7 = (f32[192,512]{1,0:T(8,128)S(1)}, f32[192,512]{1,0:T(8,128)S(1)}, u32[]{:S(2)}, u32[]{:S(2)}) collective-permute-start(f32[192,512]{1,0:T(8,128)S(1)} %slice.100), channel_id=1, source_target_pairs={{0,4},{1,5},{2,6},{3,7},{4,0},{5,1},{6,2},{7,3},{8,12},{9,13},{10,... | collective-permute-start | bytes 1179656 | tf_op jit(solution)/shard_map/ppermute | solution.py:40
  145.0 18.1 %copy-start.1 = (f32[1,96,400]{2,1,0:T(8,128)S(1)}, f32[1,96,400]{2,1,0:T(8,128)}, u32[]{:S(2)}) copy-start(f32[1,96,400]{2,1,0:T(8,128)} %param.11) | copy-start | bytes 460804
  153.5 9.0 %collective-permute-start.8 = (f32[96,512]{1,0:T(8,128)S(1)}, f32[96,512]{1,0:T(8,128)S(1)}, u32[]{:S(2)}, u32[]{:S(2)}) collective-permute-start(f32[96,512]{1,0:T(8,128)S(1)} %slice.102), channel_id=1, source_target_pairs={{0,8},{1,9},{2,10},{3,11},{4,12},{5,13},{6,14},{7,15},{8,0},{9,1},... | collective-permute-start | bytes 589832 | tf_op jit(solution)/shard_map/ppermute | solution.py:40
  (1 other events, 0.8 us)

commit v2 on v1

--- a/solution.py
+++ b/solution.py
@@ -9,7 +9,7 @@
 
 CH = 1000
 LANES = 128
-TILE = 256
+TILE = 512
 
 learn_rate = 0.1
 epsilon = 1e-10
@@ -38,6 +38,10 @@
 
 def swap(array, axis, size, bit):
     return lax.ppermute(array, axis, [(i, i ^ bit) for i in range(size)])
+
+
+def tie(*arrays):
+    return lax.optimization_barrier(arrays)
 
 
 def gather_chunks(array, axis, size):
@@ -53,15 +57,36 @@
     return array
 
 
+def routes(size):
+    rest = bits_of(size)[1:]
+    turn = len(rest) // 2
+    return rest, rest[turn:] + rest[:turn]
+
+
 def relative_ids(ids, axis, size, share):
     owner = ids // share
     within = ids - owner * share
     apart = owner ^ lax.axis_index(axis)
     place = jnp.zeros_like(apart)
-    top = size.bit_length() - 2
-    for b in range(top + 1):
-        place = place | (((apart >> b) & 1) << (top - b))
+    for s, bit in enumerate(reversed(bits_of(size))):
+        place = place | jnp.where((apart & bit) != 0, 1 << s, 0)
     return place * share + within
+
+
+def left_places(ids, size, share):
+    owner = ids // share
+    within = ids - owner * share
+    apart = owner ^ lax.axis_index("col")
+    half = share // 2
+    quarter = size // 2 * half
+    places = []
+    for route in routes(size):
+        place = jnp.zeros_like(apart)
+        for s, bit in enumerate(reversed(route)):
+            place = place | jnp.where((apart & bit) != 0, 1 << s, 0)
+        places.append(place * half)
+    first, second = places[0] + within, places[1] + within + (quarter - half)
+    return (apart & 1) * (2 * quarter) + jnp.where(within < half, first, second)
 
 
 def split_two(value):
@@ -150,11 +175,11 @@
         grad_rel_ref[...] += dot(rel_hot_t, r_hi) + dot(rel_hot_t, r_lo)
 
 
-def left_kernel(groups_ref, ids_ref, d_hi_ref, d_lo_ref, out_ref):
+def left_kernel(base, groups_ref, ids_ref, d_hi_ref, d_lo_ref, out_ref):
     rows = out_ref.shape[0]
     edges = ids_ref.shape[2]
     out_ref[...] = jnp.zeros_like(out_ref)
-    row_iota = lax.broadcasted_iota(jnp.int32, (rows, edges), 0) + pl.program_id(0) * rows
+    row_iota = lax.broadcasted_iota(jnp.int32, (rows, edges), 0) + (base + pl.program_id(0) * rows)
 
     def group_step(g, carry):
         hot = jnp.where(row_iota == ids_ref[g, 0:1, :], 1.0, 0.0).astype(bf16)
@@ -198,10 +223,8 @@
     slots = groups * edges
     tiles = edges // TILE
 
-    right_part = gather_chunks(to_halves(right_emb[0].astype(bf16), half_pad), "row", n_row)
-    left_part = gather_chunks(to_halves(left_emb[0].astype(bf16), half_pad), "col", n_col)
     edge_count = counts[0, 0]
-    my_left = relative_ids(left_ids[0, 0], "col", n_col, left_share).reshape(groups, CH)
+    my_left = left_places(left_ids[0, 0], n_col, left_share).reshape(groups, CH)
     my_right = relative_ids(right_ids[0, 0], "row", n_row, right_share).reshape(groups, CH)
     my_neg = relative_ids(neg_ids[0, 0], "row", n_row, right_share)
     my_rel = rel_ids[0, 0].reshape(groups, CH)
@@ -212,6 +235,21 @@
     mult = jnp.sum(hot.astype(f32), axis=2)[:, None, :]
     count_arg = edge_count.reshape(1)
     group_arg = (count_arg + CH - 1) // CH
+
+    rel_wide = to_halves(relation, half_pad)
+    right_mine = to_halves(right_emb[0].astype(bf16), half_pad)
+    mine = to_halves(left_emb[0].astype(bf16), half_pad)
+    part_a, part_b = mine[: left_share // 2], mine[left_share // 2 :]
+    route_a, route_b = routes(n_col)
+    right_part = gather_chunks(right_mine, "row", n_row)
+    for step, (bit_a, bit_b) in enumerate(zip(reversed(route_a), reversed(route_b))):
+        part_a, part_b = tie(part_a, part_b)
+        more_a, more_b = tie(swap(part_a, "col", n_col, bit_a), swap(part_b, "col", n_col, bit_b))
+        part_a = jnp.concatenate([part_a, more_a], axis=0)
+        part_b = jnp.concatenate([part_b, more_b], axis=0)
+    own = jnp.concatenate([part_a, part_b], axis=0)
+    own, ids, mult, right_part, rel_wide, count_arg, group_arg = tie(own, ids, mult, right_part, rel_wide, count_arg, group_arg)
+    left_part = jnp.concatenate([own, swap(own, "col", n_col, 1)], axis=0)
 
     smem = pl.BlockSpec(memory_space=pltpu.SMEM)
     tile_block = lambda lanes: pl.BlockSpec((TILE, lanes), lambda i: (i, 0))
@@ -248,37 +286,67 @@
         ],
         compiler_params=pltpu.CompilerParams(vmem_limit_bytes=48 << 20),
         name="edges",
-    )(count_arg, ids, mult, left_part, right_part, to_halves(relation, half_pad))
-
-    row_block = 256 if n_left % 256 == 0 else left_share
-    grad_left = pl.pallas_call(
-        left_kernel,
-        grid=(n_left // row_block,),
-        in_specs=[smem, whole((groups, 8, edges)), whole((slots, wide)), whole((slots, wide))],
-        out_specs=pl.BlockSpec((row_block, wide), lambda i: (i, 0)),
-        out_shape=jax.ShapeDtypeStruct((n_left, wide), f32),
-        compiler_params=pltpu.CompilerParams(vmem_limit_bytes=48 << 20),
-        name="left_sum",
-    )(group_arg, ids, d_hi, d_lo)
-
-    group_block = lambda lanes: pl.BlockSpec((edges, lanes), lambda i: (i, 0))
-    grad_right = pl.pallas_call(
-        right_kernel,
-        grid=(groups,),
-        in_specs=[group_block(wide), group_block(n_right), group_block(n_right)],
-        out_specs=whole((n_right, wide)),
-        out_shape=jax.ShapeDtypeStruct((n_right, wide), f32),
-        scratch_shapes=[pltpu.VMEM((wide, n_right), f32)],
-        compiler_params=pltpu.CompilerParams(vmem_limit_bytes=48 << 20),
-        cost_estimate=pl.CostEstimate(flops=4 * slots * wide * n_right, bytes_accessed=6 * slots * wide, transcendentals=0),
-        name="right_sum",
-    )(query, c_hi, c_lo)
-
-    for bit in bits_of(n_col):
-        grad_rel = grad_rel + swap(grad_rel, "col", n_col, bit)
-    for bit in bits_of(n_row):
-        grad_rel = grad_rel + swap(grad_rel, "row", n_row, bit)
-    grad_left = reduce_chunks(grad_left, "col", n_col)
+    )(count_arg, ids, mult, left_part, right_part, rel_wide)
+
+    piece = n_left // 4
+    row_block = min(piece, left_share * 4)
+
+    def left_sum(quarter, d_hi, d_lo):
+        return pl.pallas_call(
+            functools.partial(left_kernel, quarter * piece),
+            grid=(piece // row_block,),
+            in_specs=[smem, whole((groups, 8, edges)), whole((slots, wide)), whole((slots, wide))],
+            out_specs=pl.BlockSpec((row_block, wide), lambda i: (i, 0)),
+            out_shape=jax.ShapeDtypeStruct((piece, wide), f32),
+            compiler_params=pltpu.CompilerParams(vmem_limit_bytes=48 << 20),
+            cost_estimate=pl.CostEstimate(flops=4 * slots * wide * piece, bytes_accessed=4 * slots * wide, transcendentals=0),
+            name="left_sum",
+        )(group_arg, ids, d_hi, d_lo)
+
+    def right_sum(query, c_hi, c_lo):
+        group_block = lambda lanes: pl.BlockSpec((edges, lanes), lambda i: (i, 0))
+        return pl.pallas_call(
+            right_kernel,
+            grid=(groups,),
+            in_specs=[group_block(wide), group_block(n_right), group_block(n_right)],
+            out_specs=whole((n_right, wide)),
+            out_shape=jax.ShapeDtypeStruct((n_right, wide), f32),
+            scratch_shapes=[pltpu.VMEM((wide, n_right), f32)],
+            compiler_params=pltpu.CompilerParams(vmem_limit_bytes=48 << 20),
+            cost_estimate=pl.CostEstimate(flops=4 * slots * wide * n_right, bytes_accessed=6 * slots * wide, transcendentals=0),
+            name="right_sum",
+        )(query, c_hi, c_lo)
+
+    rel_steps = [("col", n_col, bit) for bit in bits_of(n_col)] + [("row", n_row, bit) for bit in bits_of(n_row)]
+
+    def add_rel(total, last=False):
+        for _ in range(len(rel_steps) if last else 1):
+            if rel_steps:
+                total = total + swap(total, *rel_steps.pop(0))
+        return total
+
+    far_a, next_rel = left_sum(2, d_hi, d_lo), add_rel(grad_rel)
+    far_a, grad_rel, d_hi, d_lo = tie(far_a, next_rel, d_hi, d_lo)
+    far_b, next_rel = left_sum(3, d_hi, d_lo), add_rel(grad_rel)
+    far_a, far_b, grad_rel, d_hi, d_lo = tie(far_a, far_b, next_rel, d_hi, d_lo)
+    come_a = swap(far_a, "col", n_col, 1)
+    near_a, next_rel = left_sum(0, d_hi, d_lo), add_rel(grad_rel)
+    near_a, come_a, grad_rel, far_b, d_hi, d_lo = tie(near_a, come_a, next_rel, far_b, d_hi, d_lo)
+    come_b = swap(far_b, "col", n_col, 1)
+    near_b, next_rel = left_sum(1, d_hi, d_lo), add_rel(grad_rel)
+    near_b, come_b, grad_rel, query, c_hi, c_lo = tie(near_b, come_b, next_rel, query, c_hi, c_lo)
+    sum_a, sum_b = tie(near_a + come_a, near_b + come_b)
+    grad_right = None
+    for bit_a, bit_b in zip(route_a, route_b):
+        half = sum_a.shape[0] // 2
+        more_a, more_b = swap(sum_a[half:], "col", n_col, bit_a), swap(sum_b[half:], "col", n_col, bit_b)
+        if grad_right is None:
+            grad_right, next_rel = right_sum(query, c_hi, c_lo), add_rel(grad_rel, last=True)
+            more_a, more_b, grad_right, grad_rel = tie(more_a, more_b, grad_right, next_rel)
+        else:
+            more_a, more_b = tie(more_a, more_b)
+        sum_a, sum_b = tie(sum_a[:half] + more_a, sum_b[:half] + more_b)
+    grad_left = jnp.concatenate([sum_a, sum_b], axis=0)
     grad_right = reduce_chunks(grad_right, "row", n_row)
 
     def adagrad(embedding, accumulator, gradient):

time: 165 us -> 130 us (0.79)
  waiting for transfers between devices: 54.9 us -> 29 us
  Pallas kernels: 50.5 us -> 62.1 us
  starting transfers between devices: 31.4 us -> 20.8 us
  other arithmetic: 18.2 us -> 9.76 us
    ppermute x15 -> x22, waiting for transfers between devices: 54.9 us -> 29 us  [swap(): return lax.ppermute(array, axis, [(i, i ^ bit) for i in range(size)])]
    ppermute x15 -> x22, starting transfers between devices: 31.4 us -> 20.8 us  [swap(): return lax.ppermute(array, axis, [(i, i ^ bit) for i in range(size)])]
    pallas_call x2 -> x5, Pallas kernels: 24.2 us -> 32.4 us  [the longest x4 25 us: left_sum(): pl.pallas_call(functools.partial(left_kernel, quarter * piece), grid=(pie...]
    pallas_call x1, Pallas kernels: 26.4 us -> 29.8 us  [body(): pl.pallas_call(edge_kernel, grid=(groups * tiles,), in_specs=[smem, pl.Bl...]
    unnamed x26 -> x28, local copies, waits for them, and re-layouts: 2.74 us -> 4.89 us
    concatenate x4 -> x1, other arithmetic: 1.99 us -> 0.04 us  [gather_chunks(): array = jnp.concatenate([array, swap(array, axis, size, bit)], axis=0)]
  transfers between devices with their start and end apart: 15 -> 22, of which waited for: 9 -> 11; matrix products, arithmetic and copies ran while one was open for 12% -> 7% of each run, Pallas kernels for 5% -> 25%
where the time goes in v2:
time: 130 us
  Pallas kernels  62.1 us (48%)
  waiting for transfers between devices  29 us (22%)
  starting transfers between devices  20.8 us (16%)
  other arithmetic  9.76 us (8%)
  local copies, waits for them, and re-layouts  5.8 us (4%)
  between operations  2.03 us (2%)
    pallas_call x1, Pallas kernels, body(): pl.pallas_call(edge_kernel, grid=(groups * tiles,), in_specs=[smem, pl.Bl...  29.8 us
    ppermute x22, waiting for transfers between devices, swap(): return lax.ppermute(array, axis, [(i, i ^ bit) for i in range(size)])  29 us
    pallas_call x4, Pallas kernels, left_sum(): pl.pallas_call(functools.partial(left_kernel, quarter * piece), grid=(pie...  25 us
    ppermute x22, starting transfers between devices, swap(): return lax.ppermute(array, axis, [(i, i ^ bit) for i in range(size)])  20.8 us
    pallas_call x1, Pallas kernels, right_sum(): pl.pallas_call(right_kernel, grid=(groups,), in_specs=[group_block(wide),...  7.4 us
    unnamed x28, local copies, waits for them, and re-layouts  4.89 us
  transfers between devices with their start and end apart: 22, of which 11 were waited for; matrix products, arithmetic and copies ran while one was open for 7% of the time, Pallas kernels for 25%

profile of v2, /device:TPU:0, one launch (start us, length us, event | category | flops | bytes accessed | tf_op | source)
XLA Modules:
  0.0 129.6 jit_solution(15677629405939834280)
XLA Ops:
  2.5 4.1 %collective-permute-start = (bf16[48,512]{1,0:T(8,128)(2,1)S(1)}, bf16[48,512]{1,0:T(8,128)(2,1)S(1)}, u32[]{:S(2)}, u32[]{:S(2)}) collective-permute-start(bf16[48,512]{1,0:T(8,128)(2,1)S(1)} %get-tuple-element.68), channel_id=1, source_target_pairs={{0,8},{1,9},{2,10},{3,11},{4,12},{5,13},{6,14},{7,15},{8,0},{9,1},... | collective-permute-start | bytes 147464 | tf_op jit(solution)/shard_map/ppermute | solution.py:40
  6.6 1.5 %collective-permute-start.1 = (bf16[48,512]{1,0:T(8,128)(2,1)S(1)}, bf16[48,512]{1,0:T(8,128)(2,1)S(1)}, u32[]{:S(2)}, u32[]{:S(2)}) collective-permute-start(bf16[48,512]{1,0:T(8,128)(2,1)S(1)} %get-tuple-element.69), channel_id=1, source_target_pairs={{0,2},{1,3},{2,0},{3,1},{4,6},{5,7},{6,4},{7,5},{8,10},{9,11},{10,... | collective-permute-start | bytes 147464 | tf_op jit(solution)/shard_map/ppermute | solution.py:40
  8.1 1.2 copy.20
  9.5 1.6 %collective-permute-start.6 = (bf16[256,512]{1,0:T(8,128)(2,1)S(1)}, bf16[256,512]{1,0:T(8,128)(2,1)S(1)}, u32[]{:S(2)}, u32[]{:S(2)}) collective-permute-start(bf16[256,512]{1,0:T(8,128)(2,1)S(1)} %pad_maximum_fusion.3), channel_id=1, source_target_pairs={{0,16},{16,0},{1,17},{17,1},{2,18},{18,2},{3,19},{19,3},{4,20},{20... | collective-permute-start | bytes 786440 | tf_op jit(solution)/shard_map/ppermute | solution.py:40
  16.2 1.6 %collective-permute-start.2 = (bf16[96,512]{1,0:T(8,128)(2,1)S(1)}, bf16[96,512]{1,0:T(8,128)(2,1)S(1)}, u32[]{:S(2)}, u32[]{:S(2)}) collective-permute-start(bf16[96,512]{1,0:T(8,128)(2,1)S(1)} %get-tuple-element.72), channel_id=1, source_target_pairs={{0,4},{1,5},{2,6},{3,7},{4,0},{5,1},{6,2},{7,3},{8,12},{9,13},{10,... | collective-permute-start | bytes 294920 | tf_op jit(solution)/shard_map/ppermute | solution.py:40
  18.4 3.2 %collective-permute-done.2 = bf16[96,512]{1,0:T(8,128)(2,1)S(1)} collective-permute-done((bf16[96,512]{1,0:T(8,128)(2,1)S(1)}, bf16[96,512]{1,0:T(8,128)(2,1)S(1)}, u32[]{:S(2)}, u32[]{:S(2)}) %collective-permute-start.2) | collective-permute-done | bytes 98336 | tf_op jit(solution)/shard_map/ppermute | solution.py:40
  21.6 2.7 %collective-permute-done.3 = bf16[96,512]{1,0:T(8,128)(2,1)S(1)} collective-permute-done((bf16[96,512]{1,0:T(8,128)(2,1)S(1)}, bf16[96,512]{1,0:T(8,128)(2,1)S(1)}, u32[]{:S(2)}, u32[]{:S(2)}) %collective-permute-start.3) | collective-permute-done | bytes 98336 | tf_op jit(solution)/shard_map/ppermute | solution.py:40
  25.0 5.1 %collective-permute-done.4 = bf16[192,512]{1,0:T(8,128)(2,1)S(1)} collective-permute-done((bf16[192,512]{1,0:T(8,128)(2,1)S(1)}, bf16[192,512]{1,0:T(8,128)(2,1)S(1)}, u32[]{:S(2)}, u32[]{:S(2)}) %collective-permute-start.4) | collective-permute-done | bytes 196640 | tf_op jit(solution)/shard_map/ppermute | solution.py:40
  30.7 2.3 %collective-permute-done.7 = bf16[768,512]{1,0:T(8,128)(2,1)S(1)} collective-permute-done((bf16[768,512]{1,0:T(8,128)(2,1)S(1)}, bf16[768,512]{1,0:T(8,128)(2,1)S(1)}, u32[]{:S(2)}, u32[]{:S(2)}) %collective-permute-start.7) | collective-permute-done | bytes 786464 | tf_op jit(solution)/shard_map/ppermute | solution.py:40
  33.1 29.8 %edges.1 = (bf16[4096,512]{1,0:T(8,128)(2,1)}, bf16[4096,512]{1,0:T(8,128)(2,1)}, bf16[4096,512]{1,0:T(8,128)(2,1)}, bf16[4096,512]{1,0:T(8,128)(2,1)}, bf16[409...) custom-call(s32[1]{0:T(128)} %bitcast.43.count_ref, s32[4,8,1024]{2,1,0:T(8,128)S(1)} %pad.27.ids_ref, ...), custom_call_target="tpu_custom_call" | custom-call | tf_op jit(solution)/shard_map/edges/pallas_call | solution.py:256
  62.9 2.2 %copy-done.1 = bf16[4096,512]{1,0:T(8,128)(2,1)S(1)} copy-done((bf16[4096,512]{1,0:T(8,128)(2,1)S(1)}, bf16[4096,512]{1,0:T(8,128)(2,1)}, u32[]{:S(2)}) %copy-start.1) | copy-done | bytes 4194328
  65.1 6.2 %left_sum.4 = f32[384,512]{1,0:T(8,128)S(1)} custom-call(s32[1]{0:T(128)S(6)} %select_n.137.groups_ref, s32[4,8,1024]{2,1,0:T(8,128)S(1)} %pad.27.ids_ref, bf16[4096,512]{1,0:T(8,128)(2,1)S(1)} %copy-done.1, bf16[4096,512]{1,0:T(8,128)(2,1)} %get-tuple-element.102.d_lo_ref), custom_call_target="tpu_custom_call" | custom-call | flops 3221225472 | bytes 8388608 | tf_op jit(solution)/shard_map/left_sum/pallas_call | solution.py:295
  71.4 6.2 %left_sum.5 = f32[384,512]{1,0:T(8,128)S(1)} custom-call(s32[1]{0:T(128)S(6)} %select_n.137.groups_ref, s32[4,8,1024]{2,1,0:T(8,128)S(1)} %pad.27.ids_ref, bf16[4096,512]{1,0:T(8,128)(2,1)S(1)} %copy-done.1, bf16[4096,512]{1,0:T(8,128)(2,1)} %get-tuple-element.102.d_lo_ref), custom_call_target="tpu_custom_call" | custom-call | flops 3221225472 | bytes 8388608 | tf_op jit(solution)/shard_map/left_sum/pallas_call | solution.py:295
  77.8 6.1 %left_sum.6 = f32[384,512]{1,0:T(8,128)S(1)} custom-call(s32[1]{0:T(128)S(6)} %select_n.137.groups_ref, s32[4,8,1024]{2,1,0:T(8,128)S(1)} %pad.27.ids_ref, bf16[4096,512]{1,0:T(8,128)(2,1)S(1)} %copy-done.1, bf16[4096,512]{1,0:T(8,128)(2,1)} %get-tuple-element.102.d_lo_ref), custom_call_target="tpu_custom_call" | custom-call | flops 3221225472 | bytes 8388608 | tf_op jit(solution)/shard_map/left_sum/pallas_call | solution.py:295
  84.1 2.1 %collective-permute-start.13 = (f32[64,512]{1,0:T(8,128)S(1)}, f32[64,512]{1,0:T(8,128)S(1)}, u32[]{:S(2)}, u32[]{:S(2)}) collective-permute-start(f32[64,512]{1,0:T(8,128)S(1)} %add.205), channel_id=1, source_target_pairs={{0,8},{1,9},{2,10},{3,11},{4,12},{5,13},{6,14},{7,15},{8,0},{9,1},... | collective-permute-start | bytes 393224 | tf_op jit(solution)/shard_map/ppermute | solution.py:40
  86.2 6.4 %left_sum.7 = f32[384,512]{1,0:T(8,128)S(1)} custom-call(s32[1]{0:T(128)S(6)} %select_n.137.groups_ref, s32[4,8,1024]{2,1,0:T(8,128)S(1)} %pad.27.ids_ref, bf16[4096,512]{1,0:T(8,128)(2,1)S(1)} %copy-done.1, bf16[4096,512]{1,0:T(8,128)(2,1)} %get-tuple-element.102.d_lo_ref), custom_call_target="tpu_custom_call" | custom-call | flops 3221225472 | bytes 8388608 | tf_op jit(solution)/shard_map/left_sum/pallas_call | solution.py:295
  96.2 7.4 %right_sum.1 = f32[512,512]{1,0:T(8,128)S(1)} custom-call(bf16[4096,512]{1,0:T(8,128)(2,1)S(1)} %copy-done, bf16[4096,512]{1,0:T(8,128)(2,1)} %get-tuple-element.113.c_hi_ref, bf16[4096,512]{1,0:T(8,128)(2,1)} %get-tuple-element.114.c_lo_ref), custom_call_target="tpu_custom_call" | custom-call | flops 4294967296 | bytes 12582912 | tf_op jit(solution)/shard_map/right_sum/pallas_call | solution.py:308
  103.6 2.0 %collective-permute-done.14 = f32[192,512]{1,0:T(8,128)S(1)} collective-permute-done((f32[192,512]{1,0:T(8,128)S(1)}, f32[192,512]{1,0:T(8,128)S(1)}, u32[]{:S(2)}, u32[]{:S(2)}) %collective-permute-start.14) | collective-permute-done | bytes 393248 | tf_op jit(solution)/shard_map/ppermute | solution.py:40
  105.9 1.7 %collective-permute-start.21 = (f32[256,512]{1,0:T(8,128)S(1)}, f32[256,512]{1,0:T(8,128)S(1)}, u32[]{:S(2)}, u32[]{:S(2)}) collective-permute-start(f32[256,512]{1,0:T(8,128)S(1)} %slice.110), channel_id=1, source_target_pairs={{0,16},{16,0},{1,17},{17,1},{2,18},{18,2},{3,19},{19,3},{4,20},{20... | collective-permute-start | bytes 1572872 | tf_op jit(solution)/shard_map/ppermute | solution.py:40
  108.8 2.4 %collective-permute-start.18 = (f32[96,512]{1,0:T(8,128)S(1)}, f32[96,512]{1,0:T(8,128)S(1)}, u32[]{:S(2)}, u32[]{:S(2)}) collective-permute-start(f32[96,512]{1,0:T(8,128)S(1)} %slice.101), channel_id=1, source_target_pairs={{0,8},{1,9},{2,10},{3,11},{4,12},{5,13},{6,14},{7,15},{8,0},{9,1},... | collective-permute-start | bytes 589832 | tf_op jit(solution)/shard_map/ppermute | solution.py:40
  111.7 4.3 %collective-permute-done.17 = f32[96,512]{1,0:T(8,128)S(1)} collective-permute-done((f32[96,512]{1,0:T(8,128)S(1)}, f32[96,512]{1,0:T(8,128)S(1)}, u32[]{:S(2)}, u32[]{:S(2)}) %collective-permute-start.17) | collective-permute-done | bytes 196640 | tf_op jit(solution)/shard_map/ppermute | solution.py:40
  116.0 3.4 %collective-permute-done.18 = f32[96,512]{1,0:T(8,128)S(1)} collective-permute-done((f32[96,512]{1,0:T(8,128)S(1)}, f32[96,512]{1,0:T(8,128)S(1)}, u32[]{:S(2)}, u32[]{:S(2)}) %collective-permute-start.18) | collective-permute-done | bytes 196640 | tf_op jit(solution)/shard_map/ppermute | solution.py:40
  119.5 1.3 %collective-permute-start.20 = (f32[48,512]{1,0:T(8,128)S(1)}, f32[48,512]{1,0:T(8,128)S(1)}, u32[]{:S(2)}, u32[]{:S(2)}) collective-permute-start(f32[48,512]{1,0:T(8,128)S(1)} %slice.105), channel_id=1, source_target_pairs={{0,2},{1,3},{2,0},{3,1},{4,6},{5,7},{6,4},{7,5},{8,10},{9,11},{10,... | collective-permute-start | bytes 294920 | tf_op jit(solution)/shard_map/ppermute | solution.py:40
  121.6 4.4 %collective-permute-done.19 = f32[48,512]{1,0:T(8,128)S(1)} collective-permute-done((f32[48,512]{1,0:T(8,128)S(1)}, f32[48,512]{1,0:T(8,128)S(1)}, u32[]{:S(2)}, u32[]{:S(2)}) %collective-permute-start.19) | collective-permute-done | bytes 98336 | tf_op jit(solution)/shard_map/ppermute | solution.py:40
  (122 shorter events, 18.3 us)
Async XLA Ops:
  2.5 13.7 %collective-permute-start = (bf16[48,512]{1,0:T(8,128)(2,1)S(1)}, bf16[48,512]{1,0:T(8,128)(2,1)S(1)}, u32[]{:S(2)}, u32[]{:S(2)}) collective-permute-start(bf16[48,512]{1,0:T(8,128)(2,1)S(1)} %get-tuple-element.68), channel_id=1, source_target_pairs={{0,8},{1,9},{2,10},{3,11},{4,12},{5,13},{6,14},{7,15},{8,0},{9,1},... | collective-permute-start | bytes 147464 | tf_op jit(solution)/shard_map/ppermute | solution.py:40
  6.6 9.6 %collective-permute-start.1 = (bf16[48,512]{1,0:T(8,128)(2,1)S(1)}, bf16[48,512]{1,0:T(8,128)(2,1)S(1)}, u32[]{:S(2)}, u32[]{:S(2)}) collective-permute-start(bf16[48,512]{1,0:T(8,128)(2,1)S(1)} %get-tuple-element.69), channel_id=1, source_target_pairs={{0,2},{1,3},{2,0},{3,1},{4,6},{5,7},{6,4},{7,5},{8,10},{9,11},{10,... | collective-permute-start | bytes 147464 | tf_op jit(solution)/shard_map/ppermute | solution.py:40
  9.5 15.4 %collective-permute-start.6 = (bf16[256,512]{1,0:T(8,128)(2,1)S(1)}, bf16[256,512]{1,0:T(8,128)(2,1)S(1)}, u32[]{:S(2)}, u32[]{:S(2)}) collective-permute-start(bf16[256,512]{1,0:T(8,128)(2,1)S(1)} %pad_maximum_fusion.3), channel_id=1, source_target_pairs={{0,16},{16,0},{1,17},{17,1},{2,18},{18,2},{3,19},{19,3},{4,20},{20... | collective-permute-start | bytes 786440 | tf_op jit(solution)/shard_map/ppermute | solution.py:40
  16.2 5.4 %collective-permute-start.2 = (bf16[96,512]{1,0:T(8,128)(2,1)S(1)}, bf16[96,512]{1,0:T(8,128)(2,1)S(1)}, u32[]{:S(2)}, u32[]{:S(2)}) collective-permute-start(bf16[96,512]{1,0:T(8,128)(2,1)S(1)} %get-tuple-element.72), channel_id=1, source_target_pairs={{0,4},{1,5},{2,6},{3,7},{4,0},{5,1},{6,2},{7,3},{8,12},{9,13},{10,... | collective-permute-start | bytes 294920 | tf_op jit(solution)/shard_map/ppermute | solution.py:40
  17.8 6.5 %collective-permute-start.3 = (bf16[96,512]{1,0:T(8,128)(2,1)S(1)}, bf16[96,512]{1,0:T(8,128)(2,1)S(1)}, u32[]{:S(2)}, u32[]{:S(2)}) collective-permute-start(bf16[96,512]{1,0:T(8,128)(2,1)S(1)} %get-tuple-element.73), channel_id=1, source_target_pairs={{0,8},{1,9},{2,10},{3,11},{4,12},{5,13},{6,14},{7,15},{8,0},{9,1},... | collective-permute-start | bytes 294920 | tf_op jit(solution)/shard_map/ppermute | solution.py:40
  24.3 5.7 %collective-permute-start.4 = (bf16[192,512]{1,0:T(8,128)(2,1)S(1)}, bf16[192,512]{1,0:T(8,128)(2,1)S(1)}, u32[]{:S(2)}, u32[]{:S(2)}) collective-permute-start(bf16[192,512]{1,0:T(8,128)(2,1)S(1)} %pad_maximum_fusion.4), channel_id=1, source_target_pairs={{0,2},{1,3},{2,0},{3,1},{4,6},{5,7},{6,4},{7,5},{8,10},{9,11},{10,... | collective-permute-start | bytes 589832 | tf_op jit(solution)/shard_map/ppermute | solution.py:40
  24.9 5.7 %collective-permute-start.5 = (bf16[192,512]{1,0:T(8,128)(2,1)S(1)}, bf16[192,512]{1,0:T(8,128)(2,1)S(1)}, u32[]{:S(2)}, u32[]{:S(2)}) collective-permute-start(bf16[192,512]{1,0:T(8,128)(2,1)S(1)} %pad_maximum_fusion.5), channel_id=1, source_target_pairs={{0,4},{1,5},{2,6},{3,7},{4,0},{5,1},{6,2},{7,3},{8,12},{9,13},{10,... | collective-permute-start | bytes 589832 | tf_op jit(solution)/shard_map/ppermute | solution.py:40
  30.6 2.4 %collective-permute-start.7 = (bf16[768,512]{1,0:T(8,128)(2,1)S(1)}, bf16[768,512]{1,0:T(8,128)(2,1)S(1)}, u32[]{:S(2)}, u32[]{:S(2)}) collective-permute-start(bf16[768,512]{1,0:T(8,128)(2,1)S(1)} %pad_maximum_fusion.1), channel_id=1, source_target_pairs={{0,1},{1,0},{2,3},{3,2},{4,5},{5,4},{6,7},{7,6},{8,9},{9,8},{10,11... | collective-permute-start | bytes 2359304 | tf_op jit(solution)/shard_map/ppermute | solution.py:40
  62.9 8.4 %collective-permute-start.8 = (f32[64,512]{1,0:T(8,128)S(1)}, f32[64,512]{1,0:T(8,128)S(1)}, u32[]{:S(2)}, u32[]{:S(2)}) collective-permute-start(f32[64,512]{1,0:T(8,128)S(1)} %get-tuple-element.89), channel_id=1, source_target_pairs={{0,1},{1,0},{2,3},{3,2},{4,5},{5,4},{6,7},{7,6},{8,9},{9,8},{10,11... | collective-permute-start | bytes 393224 | tf_op jit(solution)/shard_map/ppermute | solution.py:40
  71.3 6.3 %collective-permute-start.9 = (f32[64,512]{1,0:T(8,128)S(1)}, f32[64,512]{1,0:T(8,128)S(1)}, u32[]{:S(2)}, u32[]{:S(2)}) collective-permute-start(f32[64,512]{1,0:T(8,128)S(1)} %add.203), channel_id=1, source_target_pairs={{0,2},{1,3},{2,0},{3,1},{4,6},{5,7},{6,4},{7,5},{8,10},{9,11},{10,... | collective-permute-start | bytes 393224 | tf_op jit(solution)/shard_map/ppermute | solution.py:40
  77.7 6.4 %collective-permute-start.10 = (f32[384,512]{1,0:T(8,128)S(1)}, f32[384,512]{1,0:T(8,128)S(1)}, u32[]{:S(2)}, u32[]{:S(2)}) collective-permute-start(f32[384,512]{1,0:T(8,128)S(1)} %left_sum.4), channel_id=1, source_target_pairs={{0,1},{1,0},{2,3},{3,2},{4,5},{5,4},{6,7},{7,6},{8,9},{9,8},{10,11... | collective-permute-start | bytes 2359304 | tf_op jit(solution)/shard_map/ppermute | solution.py:40
  77.8 6.2 %collective-permute-start.11 = (f32[64,512]{1,0:T(8,128)S(1)}, f32[64,512]{1,0:T(8,128)S(1)}, u32[]{:S(2)}, u32[]{:S(2)}) collective-permute-start(f32[64,512]{1,0:T(8,128)S(1)} %add.204), channel_id=1, source_target_pairs={{0,4},{1,5},{2,6},{3,7},{4,0},{5,1},{6,2},{7,3},{8,12},{9,13},{10,... | collective-permute-start | bytes 393224 | tf_op jit(solution)/shard_map/ppermute | solution.py:40
  84.0 9.7 %collective-permute-start.12 = (f32[384,512]{1,0:T(8,128)S(1)}, f32[384,512]{1,0:T(8,128)S(1)}, u32[]{:S(2)}, u32[]{:S(2)}) collective-permute-start(f32[384,512]{1,0:T(8,128)S(1)} %left_sum.5), channel_id=1, source_target_pairs={{0,1},{1,0},{2,3},{3,2},{4,5},{5,4},{6,7},{7,6},{8,9},{9,8},{10,11... | collective-permute-start | bytes 2359304 | tf_op jit(solution)/shard_map/ppermute | solution.py:40
  84.1 9.6 %collective-permute-start.13 = (f32[64,512]{1,0:T(8,128)S(1)}, f32[64,512]{1,0:T(8,128)S(1)}, u32[]{:S(2)}, u32[]{:S(2)}) collective-permute-start(f32[64,512]{1,0:T(8,128)S(1)} %add.205), channel_id=1, source_target_pairs={{0,8},{1,9},{2,10},{3,11},{4,12},{5,13},{6,14},{7,15},{8,0},{9,1},... | collective-permute-start | bytes 393224 | tf_op jit(solution)/shard_map/ppermute | solution.py:40
  93.8 9.8 %collective-permute-start.16 = (f32[64,512]{1,0:T(8,128)S(1)}, f32[64,512]{1,0:T(8,128)S(1)}, u32[]{:S(2)}, u32[]{:S(2)}) collective-permute-start(f32[64,512]{1,0:T(8,128)S(1)} %add.207), channel_id=1, source_target_pairs={{0,16},{16,0},{1,17},{17,1},{2,18},{18,2},{3,19},{19,3},{4,20},{20... | collective-permute-start | bytes 393224 | tf_op jit(solution)/shard_map/ppermute | solution.py:40
  94.8 10.9 %collective-permute-start.14 = (f32[192,512]{1,0:T(8,128)S(1)}, f32[192,512]{1,0:T(8,128)S(1)}, u32[]{:S(2)}, u32[]{:S(2)}) collective-permute-start(f32[192,512]{1,0:T(8,128)S(1)} %slice.96), channel_id=1, source_target_pairs={{0,2},{1,3},{2,0},{3,1},{4,6},{5,7},{6,4},{7,5},{8,10},{9,11},{10,... | collective-permute-start | bytes 1179656 | tf_op jit(solution)/shard_map/ppermute | solution.py:40
  95.2 10.5 %collective-permute-start.15 = (f32[192,512]{1,0:T(8,128)S(1)}, f32[192,512]{1,0:T(8,128)S(1)}, u32[]{:S(2)}, u32[]{:S(2)}) collective-permute-start(f32[192,512]{1,0:T(8,128)S(1)} %slice.97), channel_id=1, source_target_pairs={{0,4},{1,5},{2,6},{3,7},{4,0},{5,1},{6,2},{7,3},{8,12},{9,13},{10,... | collective-permute-start | bytes 1179656 | tf_op jit(solution)/shard_map/ppermute | solution.py:40
  105.9 21.7 %collective-permute-start.21 = (f32[256,512]{1,0:T(8,128)S(1)}, f32[256,512]{1,0:T(8,128)S(1)}, u32[]{:S(2)}, u32[]{:S(2)}) collective-permute-start(f32[256,512]{1,0:T(8,128)S(1)} %slice.110), channel_id=1, source_target_pairs={{0,16},{16,0},{1,17},{17,1},{2,18},{18,2},{3,19},{19,3},{4,20},{20... | collective-permute-start | bytes 1572872 | tf_op jit(solution)/shard_map/ppermute | solution.py:40
  107.7 18.6 %copy-start.11 = (f32[1,96]{1,0:T(1,128)S(1)}, f32[1,96]{1,0:T(1,128)}, u32[]{:S(2)}) copy-start(f32[1,96]{1,0:T(1,128)} %param.12) | copy-start | bytes 1156
  107.8 19.1 %copy-start.2 = (f32[1,96,400]{2,1,0:T(8,128)S(1)}, f32[1,96,400]{2,1,0:T(8,128)}, u32[]{:S(2)}) copy-start(f32[1,96,400]{2,1,0:T(8,128)} %param.11) | copy-start | bytes 460804
  107.8 8.2 %collective-permute-start.17 = (f32[96,512]{1,0:T(8,128)S(1)}, f32[96,512]{1,0:T(8,128)S(1)}, u32[]{:S(2)}, u32[]{:S(2)}) collective-permute-start(f32[96,512]{1,0:T(8,128)S(1)} %slice.100), channel_id=1, source_target_pairs={{0,4},{1,5},{2,6},{3,7},{4,0},{5,1},{6,2},{7,3},{8,12},{9,13},{10,... | collective-permute-start | bytes 589832 | tf_op jit(solution)/shard_map/ppermute | solution.py:40
  108.8 10.6 %collective-permute-start.18 = (f32[96,512]{1,0:T(8,128)S(1)}, f32[96,512]{1,0:T(8,128)S(1)}, u32[]{:S(2)}, u32[]{:S(2)}) collective-permute-start(f32[96,512]{1,0:T(8,128)S(1)} %slice.101), channel_id=1, source_target_pairs={{0,8},{1,9},{2,10},{3,11},{4,12},{5,13},{6,14},{7,15},{8,0},{9,1},... | collective-permute-start | bytes 589832 | tf_op jit(solution)/shard_map/ppermute | solution.py:40
  119.4 6.6 %collective-permute-start.19 = (f32[48,512]{1,0:T(8,128)S(1)}, f32[48,512]{1,0:T(8,128)S(1)}, u32[]{:S(2)}, u32[]{:S(2)}) collective-permute-start(f32[48,512]{1,0:T(8,128)S(1)} %slice.104), channel_id=1, source_target_pairs={{0,8},{1,9},{2,10},{3,11},{4,12},{5,13},{6,14},{7,15},{8,0},{9,1},... | collective-permute-start | bytes 294920 | tf_op jit(solution)/shard_map/ppermute | solution.py:40
  119.5 6.5 %collective-permute-start.20 = (f32[48,512]{1,0:T(8,128)S(1)}, f32[48,512]{1,0:T(8,128)S(1)}, u32[]{:S(2)}, u32[]{:S(2)}) collective-permute-start(f32[48,512]{1,0:T(8,128)S(1)} %slice.105), channel_id=1, source_target_pairs={{0,2},{1,3},{2,0},{3,1},{4,6},{5,7},{6,4},{7,5},{8,10},{9,11},{10,... | collective-permute-start | bytes 294920 | tf_op jit(solution)/shard_map/ppermute | solution.py:40
  (10 other events, 81.8 us)

commit v3 on v2

v3 whole, which is shorter than its diff:
```python
import functools

import jax
import jax.numpy as jnp
from jax import lax
from jax.experimental import pallas as pl
from jax.experimental.pallas import tpu as pltpu
from jax.sharding import PartitionSpec as P

CH = 1000
LANES = 128
TILE = 1024
SUB = 512
WINDOW = 128
SPAN = 512

learn_rate = 0.1
epsilon = 1e-10
bf16 = jnp.bfloat16
f32 = jnp.float32


def round_up(value, step):
    return (value + step - 1) // step * step


def to_halves(array, half_pad):
    half = array.shape[-1] // 2
    pad = [(0, 0)] * (array.ndim - 1) + [(0, half_pad - half)]
    return jnp.concatenate([jnp.pad(array[..., :half], pad), jnp.pad(array[..., half:], pad)], axis=-1)


def from_halves(array, width):
    half_pad = array.shape[-1] // 2
    return jnp.concatenate([array[..., : width // 2], array[..., half_pad : half_pad + width // 2]], axis=-1)


def bits_of(size):
    return [1 << b for b in range(size.bit_length() - 1)]


def swap(array, axis, size, bit):
    return lax.ppermute(array, axis, [(i, i ^ bit) for i in range(size)])


def tie(*arrays):
    return lax.optimization_barrier(arrays)


def gather_chunks(array, axis, size):
    for bit in reversed(bits_of(size)):
        array = jnp.concatenate([array, swap(array, axis, size, bit)], axis=0)
    return array


def reduce_chunks(array, axis, size):
    for bit in bits_of(size):
        half = array.shape[0] // 2
        array = array[:half] + swap(array[half:], axis, size, bit)
    return array


def routes(size):
    rest = bits_of(size)[1:]
    turn = len(rest) // 2
    return rest, rest[turn:] + rest[:turn]


def spread(apart, route):
    place = jnp.zeros_like(apart)
    for s, bit in enumerate(reversed(route)):
        place = place | jnp.where((apart & bit) != 0, 1 << s, 0)
    return place


def owner_of(ids, share):
    owner = ((ids.astype(f32) + 0.5) * (1.0 / share)).astype(jnp.int32)
    return owner, ids - owner * share


def right_places(ids, me, size, share):
    owner, within = owner_of(ids, share)
    return spread(owner ^ me, bits_of(size)) * share + within


def left_places(ids, me, size, share):
    owner, within = owner_of(ids, share)
    apart = owner ^ me
    half = share // 2
    quarter = size // 2 * half
    first, second = (spread(apart, route) * half for route in routes(size))
    return (apart & 1) * (2 * quarter) + jnp.where(within < half, first + within, second + within + (quarter - half))


def prep_kernel(n_row, n_col, left_share, rows, where_ref, raw_ref, ids_ref, mult_ref, bound_ref):
    groups, _, edges = raw_ref.shape
    n_right = mult_ref.shape[2]
    n_left = left_share * n_col
    count, me_col, me_row = where_ref[0], where_ref[1], where_ref[2]

    def group_step(g, carry):
        raw = raw_ref[g]
        slot = lax.broadcasted_iota(jnp.int32, (1, edges), 1)
        real = slot < CH
        valid = real & (slot + g * CH < count)
        left = jnp.where(valid, left_places(raw[0:1], me_col, n_col, left_share), n_left)
        right = right_places(raw[2:3], me_row, n_row, n_right // n_row)
        neg = jnp.where(real, right_places(raw[3:4], me_row, n_row, n_right // n_row), -1)
        key = left * edges + slot
        rows_in = [key, neg, left >> 6, left & 63, raw[1:2], right >> 6, right & 63, valid.astype(jnp.int32)]
        cols = jnp.concatenate(rows_in, axis=0).T
        payload = cols.astype(f32).astype(bf16)
        rank = jnp.zeros((8, edges), jnp.int32)
        mult = jnp.zeros((8, n_right), f32)
        bound = jnp.zeros((8, LANES), jnp.int32)
        lane_start = lax.broadcasted_iota(jnp.int32, (LANES, LANES), 1) * rows
        lane_right = lax.broadcasted_iota(jnp.int32, (LANES, n_right), 1)
        for k in range(edges // LANES):
            part = cols[k * LANES : (k + 1) * LANES]
            less = jnp.where(part[:, 0:1] < key, 1, 0)
            rank = rank + jnp.sum(less.reshape(LANES // 8, 8, edges), axis=0)
            same = jnp.where(part[:, 1:2] == lane_right, 1.0, 0.0)
            mult = mult + jnp.sum(same.reshape(LANES // 8, 8, n_right), axis=0)
            below = jnp.where(part[:, 2:3] * 64 + part[:, 3:4] < lane_start, 1, 0)
            bound = bound + jnp.sum(below.reshape(LANES // 8, 8, LANES), axis=0)
        rank = jnp.sum(rank, axis=0, keepdims=True)
        mult_ref[g] = jnp.sum(mult, axis=0, keepdims=True)
        bound_ref[g] = jnp.sum(bound, axis=0, keepdims=True)
        moved = []
        for k in range(edges // LANES):
            place = lax.broadcasted_iota(jnp.int32, (LANES, edges), 0) + k * LANES
            moved.append(dot(jnp.where(place == rank, 1.0, 0.0).astype(bf16), payload))
        moved = jnp.concatenate(moved, axis=0).T.astype(jnp.int32)
        out = [moved[2:3] * 64 + moved[3:4], moved[4:5], moved[5:6] * 64 + moved[6:7], moved[7:8]]
        ids_ref[g] = jnp.concatenate(out + out, axis=0)
        return carry

    lax.fori_loop(0, groups, group_step, 0)


def split_two(value):
    high = value.astype(bf16)
    return high, (value - high.astype(f32)).astype(bf16)


def packed_rows(rows):
    return 3 * rows + 8


def pack(value, tail):
    rows = value.shape[0]
    lane = lax.broadcasted_iota(jnp.int32, (rows, LANES), 1)
    first, second, third, fourth = (value[:, k * LANES : (k + 1) * LANES] for k in range(4))
    mixed = jnp.where(lane < tail, second, pltpu.roll(fourth, tail, 1))
    spill = 2 * tail - LANES
    last = jnp.zeros((8, LANES), f32)
    for k in range(rows // 8):
        moved = pltpu.roll(fourth[8 * k : 8 * k + 8], (spill * k + tail) % LANES, 1)
        place = lane[:8] - spill * k
        last = jnp.where((place >= 0) & (place < spill), moved, last)
    return jnp.concatenate([first, third, mixed, last], axis=0)


def unpack(value, rows, tail):
    lane = lax.broadcasted_iota(jnp.int32, (rows, LANES), 1)
    first, third, mixed = (value[k * rows : (k + 1) * rows] for k in range(3))
    last = value[3 * rows :]
    spill = 2 * tail - LANES
    turned = pltpu.roll(third, tail, 1)
    fourth = [pltpu.roll(last, (LANES - spill * k) % LANES, 1) for k in range(rows // 8)]
    fourth = jnp.where(lane < spill, jnp.concatenate(fourth, axis=0), 0.0)
    return first, jnp.where(lane < tail, mixed, turned), jnp.where(lane < tail, turned, mixed), fourth


def finish_kernel(parts, chunk, tail, *refs):
    n_grads = sum(len(p) for p in parts)
    grads, (emb_ref, state_ref, new_ref, new_state_ref) = refs[:n_grads], refs[n_grads:]
    width = emb_ref.shape[1]
    means, tiles_of = [], []
    for part in parts:
        total = grads[part[0]][...]
        for k in part[1:]:
            total = total + grads[k][...]
        size = packed_rows(chunk)
        for k in range(total.shape[0] // size):
            tiles = unpack(total[k * size : (k + 1) * size], chunk, tail)
            squares = sum(t * t for t in tiles)
            means.append(jnp.sum(squares, axis=1, keepdims=True) / width)
            tiles_of.append(tiles)
    rows = chunk * len(means)
    mean = jnp.broadcast_to(jnp.concatenate(means, axis=0), (rows, LANES))
    state = jnp.broadcast_to(state_ref[...], (LANES, rows)).T
    accum = state + mean
    new_state_ref[...] = accum.T[0:1, :]
    rate = learn_rate / (jnp.sqrt(accum) + epsilon)
    for k, tiles in enumerate(tiles_of):
        here = slice(k * chunk, (k + 1) * chunk)
        for j, tile in enumerate(tiles):
            low, high = j * LANES, min((j + 1) * LANES, width)
            new_ref[here, low:high] = emb_ref[here, low:high] - (rate[here] * tile)[:, : high - low]


def finish(parts, chunk, tail, grads, embedding, state, name):
    return pl.pallas_call(
        functools.partial(finish_kernel, parts, chunk, tail),
        out_shape=[jax.ShapeDtypeStruct(embedding.shape, f32), jax.ShapeDtypeStruct((1, embedding.shape[0]), f32)],
        name=name,
    )(*grads, embedding, state.reshape(1, -1))


def dot(a, b):
    return jnp.dot(a, b, preferred_element_type=f32)


def edge_kernel(
    rows, chunk, tail, count_ref, bound_ref, ids_ref, mult_ref, left_ref, right_ref, rel_ref,
    query_ref, c_hi_ref, c_lo_ref, rel_out_ref, near_ref, far_ref,
    rel_parts, right_t, d_hi_ref, d_lo_ref, grad_rel_ref, piece_ref,
):
    step = pl.program_id(0)
    tile = query_ref.shape[0]
    groups, _, edges = ids_ref.shape
    tiles_in_group = pl.num_programs(0) // mult_ref.shape[0]
    n_rel, wide = rel_ref.shape
    half = wide // 2
    n_left, n_right = left_ref.shape[0], right_ref.shape[0]
    rel_rows = rel_parts.shape[0]

    @pl.when(step == 0)
    def _():
        grad_rel_ref[...] = jnp.zeros_like(grad_rel_ref)
        rel_parts[...] = jnp.zeros_like(rel_parts)
        rest = rel_ref[...]
        for part in range(3):
            piece = rest.astype(bf16)
            rel_parts[part * n_rel : (part + 1) * n_rel, :] = piece
            rest = rest - piece.astype(f32)
        right_t[...] = right_ref[...].T

    group = step // tiles_in_group
    start = group * CH + (step - group * tiles_in_group) * tile

    @pl.when(start >= count_ref[0])
    def _():
        for ref in (query_ref, c_hi_ref, c_lo_ref):
            ref[...] = jnp.zeros_like(ref)
        here = pl.ds(pl.multiple_of(step * tile, tile), tile)
        d_hi_ref[here, :] = jnp.zeros((tile, wide), bf16)
        d_lo_ref[here, :] = jnp.zeros((tile, wide), bf16)

    @pl.when(start < count_ref[0])
    def _():
        place = pl.multiple_of((step - group * tiles_in_group) * tile, tile)
        ids = ids_ref[group, :, pl.ds(place, tile)]
        all_cols = ids.T
        mult = mult_ref[group]
        absent = jnp.where(mult > 0.0, 0.0, -jnp.inf)

        def fetch(sub):
            cols = all_cols[sub * SUB : (sub + 1) * SUB]
            left_col, rel_col = cols[:, 0:1], cols[:, 1:2]
            rel_iota = lax.broadcasted_iota(jnp.int32, (SUB, rel_rows), 1) % n_rel
            rel_hot = jnp.where(rel_iota == rel_col, 1.0, 0.0).astype(bf16)
            rel_vec = dot(rel_hot, rel_parts[...])
            left_iota = lax.broadcasted_iota(jnp.int32, (SUB, n_left), 1)
            left_hot = jnp.where(left_iota == left_col, 1.0, 0.0).astype(bf16)
            left_vec = dot(left_hot, left_ref[...])
            a_re, a_im = left_vec[:, :half], left_vec[:, half:]
            b_re, b_im = rel_vec[:, :half], rel_vec[:, half:]
            query = jnp.concatenate([a_re * b_re - a_im * b_im, a_re * b_im + a_im * b_re], axis=1).astype(bf16)
            query_ref[sub * SUB : (sub + 1) * SUB, :] = query
            return (a_re, a_im, b_re, b_im), dot(query, right_t[...])

        def weigh(sub, scores):
            cols = all_cols[sub * SUB : (sub + 1) * SUB]
            right_col, valid = cols[:, 2:3], cols[:, 3:4].astype(f32)
            right_iota = lax.broadcasted_iota(jnp.int32, (SUB, n_right), 1)
            is_target = right_iota == right_col
            positive = jnp.sum(jnp.where(is_target, scores, 0.0), axis=1, keepdims=True)
            masked = scores + absent
            highest = jnp.maximum(jnp.max(masked, axis=1, keepdims=True), positive)
            expo = jnp.exp(masked - highest)
            expo_pos = jnp.exp(positive - highest)
            totals = expo_pos + jnp.sum(expo * mult, axis=1, keepdims=True)
            probability = (expo * (valid / totals)).astype(bf16)
            pos_coeff = (expo_pos / totals - 1.0) * valid
            coeff = mult * probability.astype(f32) + jnp.where(is_target, pos_coeff, 0.0)
            c_hi, c_lo = split_two(coeff)
            c_hi_ref[sub * SUB : (sub + 1) * SUB, :] = c_hi
            c_lo_ref[sub * SUB : (sub + 1) * SUB, :] = c_lo
            return c_hi, c_lo

        def back(sub, parts, coeffs):
            a_re, a_im, b_re, b_im = parts
            d_query = dot(coeffs[0], right_ref[...]) + dot(coeffs[1], right_ref[...])
            g_re, g_im = d_query[:, :half], d_query[:, half:]
            d_left = jnp.concatenate([g_re * b_re + g_im * b_im, g_im * b_re - g_re * b_im], axis=1)
            d_hi, d_lo = split_two(d_left)
            here = pl.ds(pl.multiple_of(step * tile + sub * SUB, SUB), SUB)
            d_hi_ref[here, :] = d_hi
            d_lo_ref[here, :] = d_lo
            d_rel = jnp.concatenate([g_re * a_re + g_im * a_im, g_im * a_re - g_re * a_im], axis=1)
            r_hi, r_lo = split_two(d_rel)
            row_iota = lax.broadcasted_iota(jnp.int32, (n_rel, SUB), 0)
            rel_hot_t = jnp.where(row_iota == ids[1:2, sub * SUB : (sub + 1) * SUB], 1.0, 0.0).astype(bf16)
            return dot(rel_hot_t, r_hi) + dot(rel_hot_t, r_lo)

        subs = tile // SUB
        fetched, weighed, rel_total = {}, {}, 0.0
        for turn in range(subs + 2):
            if turn < subs:
                fetched[turn] = fetch(turn)
            if 0 <= turn - 1 < subs:
                weighed[turn - 1] = weigh(turn - 1, fetched[turn - 1][1])
            if 0 <= turn - 2 < subs:
                rel_total += back(turn - 2, fetched[turn - 2][0], weighed[turn - 2])
        grad_rel_ref[...] += rel_total

    @pl.when(step == pl.num_programs(0) - 1)
    def _():
        n_pieces = n_left // rows

        def hot_rows(g, base, at, size):
            row_iota = lax.broadcasted_iota(jnp.int32, (rows, size), 0) + base
            return jnp.where(row_iota == ids_ref[g, 0:1, pl.ds(at, size)], 1.0, 0.0).astype(bf16)

        def span(g, piece):
            return jnp.minimum(bound_ref[g, piece] // WINDOW * WINDOW, edges - SPAN)

        few = n_rel // 2
        for k in range(2):
            size = packed_rows(few)
            rel_out_ref[k * size : (k + 1) * size, :] = pack(grad_rel_ref[k * few : (k + 1) * few, :], tail)

        def piece_step(piece, out_ref, shift):
            base = pl.multiple_of(piece * rows, rows)
            total = jnp.zeros((rows, wide), f32)
            for g in range(groups):
                at = pl.multiple_of(span(g, piece), WINDOW)
                hot = hot_rows(g, base, at, SPAN)
                here = pl.ds(pl.multiple_of(g * edges + at, WINDOW), SPAN)
                total = total + dot(hot, d_hi_ref[here, :]) + dot(hot, d_lo_ref[here, :])
            piece_ref[...] = total

            def rest_step(g, carry):
                def window_step(w, inner):
                    at = pl.multiple_of(w * WINDOW, WINDOW)
                    hot = hot_rows(g, base, at, WINDOW)
                    here = pl.ds(pl.multiple_of(g * edges + at, WINDOW), WINDOW)
                    piece_ref[...] += dot(hot, d_hi_ref[here, :]) + dot(hot, d_lo_ref[here, :])
                    return inner

                first = (span(g, piece) + SPAN) // WINDOW
                return lax.fori_loop(first, (bound_ref[g, piece + 1] + WINDOW - 1) // WINDOW, window_step, carry)

            lax.fori_loop(0, groups, rest_step, 0)
            size = packed_rows(chunk)
            for k in range(rows // chunk):
                there = pl.ds(pl.multiple_of((piece - shift) * (rows // chunk) * size + k * size, 8), size)
                out_ref[there, :] = pack(piece_ref[k * chunk : (k + 1) * chunk, :], tail)

        for shift, out_ref in ((0, near_ref), (n_pieces // 2, far_ref)):

            def each(k, carry, shift=shift, out_ref=out_ref):
                piece_step(k + shift, out_ref, shift)
                return carry

            lax.fori_loop(0, n_pieces // 2, each, 0)


def right_kernel(query_ref, c_hi_ref, c_lo_ref, out_ref, total):
    step = pl.program_id(0)

    @pl.when(step == 0)
    def _():
        total[...] = jnp.zeros_like(total)

    dims = (((0,), (0,)), ((), ()))
    query = query_ref[...]
    total[...] += lax.dot_general(query, c_hi_ref[...], dims, preferred_element_type=f32) + lax.dot_general(
        query, c_lo_ref[...], dims, preferred_element_type=f32
    )

    @pl.when(step == pl.num_programs(0) - 1)
    def _():
        out_ref[...] = total[...].T


def whole(shape):
    return pl.BlockSpec(shape, lambda *_: (0,) * len(shape))


def body(n_row, n_col, left_emb, left_state, right_emb, right_state, relation, rel_state, left_ids, rel_ids, right_ids, neg_ids, counts):
    width = relation.shape[1]
    half_pad = round_up(width // 2, LANES)
    wide = 2 * half_pad
    left_share, right_share = left_emb.shape[1], right_emb.shape[1]
    n_left, n_right, n_rel = left_share * n_col, right_share * n_row, relation.shape[0]
    groups = neg_ids.shape[2]
    edges = round_up(CH, TILE)
    slots = groups * edges
    tile = TILE if n_right <= SUB else SUB
    tiles = edges // tile

    smem = pl.BlockSpec(memory_space=pltpu.SMEM)
    rows = left_share * 4
    count_arg = counts.reshape(1)
    where = jnp.stack([counts[0, 0], lax.axis_index("col"), lax.axis_index("row")])
    raw = jnp.stack([a.reshape(groups, CH) for a in (left_ids, rel_ids, right_ids, neg_ids)], axis=1)
    raw = jnp.pad(raw, ((0, 0), (0, 0), (0, edges - CH)))
    ids, mult, bound = pl.pallas_call(
        functools.partial(prep_kernel, n_row, n_col, left_share, rows),
        in_specs=[smem, whole((groups, 4, edges))],
        out_specs=[whole((groups, 8, edges)), whole((groups, 1, n_right)), whole((groups, 1, LANES))],
        out_shape=[
            jax.ShapeDtypeStruct((groups, 8, edges), jnp.int32),
            jax.ShapeDtypeStruct((groups, 1, n_right), f32),
            jax.ShapeDtypeStruct((groups, 1, LANES), jnp.int32),
        ],
        cost_estimate=pl.CostEstimate(flops=16 * slots * edges, bytes_accessed=32 * slots, transcendentals=0),
        compiler_params=pltpu.CompilerParams(vmem_limit_bytes=32 << 20),
        name="prep",
    )(where, raw)
    bound = bound.reshape(groups, LANES)

    rel_wide = to_halves(relation, half_pad)
    right_mine = to_halves(right_emb[0].astype(bf16), half_pad)
    mine = to_halves(left_emb[0].astype(bf16), half_pad)
    part_a, part_b = mine[: left_share // 2], mine[left_share // 2 :]
    route_a, route_b = routes(n_col)
    right_part = gather_chunks(right_mine, "row", n_row)
    for step, (bit_a, bit_b) in enumerate(zip(reversed(route_a), reversed(route_b))):
        part_a, part_b = tie(part_a, part_b)
        more_a, more_b = tie(swap(part_a, "col", n_col, bit_a), swap(part_b, "col", n_col, bit_b))
        part_a = jnp.concatenate([part_a, more_a], axis=0)
        part_b = jnp.concatenate([part_b, more_b], axis=0)
    own = jnp.concatenate([part_a, part_b], axis=0)
    own, ids, mult, bound, right_part, rel_wide = tie(own, ids, mult, bound, right_part, rel_wide)
    left_part = jnp.concatenate([own, swap(own, "col", n_col, 1)], axis=0)

    tile_block = lambda lanes: pl.BlockSpec((tile, lanes), lambda i: (i, 0))
    chunk, tail = left_share // 2, width // 2 - LANES
    packed_half = n_left // 2 // chunk * packed_rows(chunk)
    packed_rel = 2 * packed_rows(n_rel // 2)
    query, c_hi, c_lo, grad_rel, near, far = pl.pallas_call(
        functools.partial(edge_kernel, rows, chunk, tail),
        grid=(groups * tiles,),
        in_specs=[
            smem,
            smem,
            whole((groups, 8, edges)),
            whole((groups, 1, n_right)),
            whole((n_left, wide)),
            whole((n_right, wide)),
            whole((n_rel, wide)),
        ],
        out_specs=[
            tile_block(wide),
            tile_block(n_right),
            tile_block(n_right),
            whole((packed_rel, LANES)),
            whole((packed_half, LANES)),
            whole((packed_half, LANES)),
        ],
        out_shape=[
            jax.ShapeDtypeStruct((slots, wide), bf16),
            jax.ShapeDtypeStruct((slots, n_right), bf16),
            jax.ShapeDtypeStruct((slots, n_right), bf16),
            jax.ShapeDtypeStruct((packed_rel, LANES), f32),
            jax.ShapeDtypeStruct((packed_half, LANES), f32),
            jax.ShapeDtypeStruct((packed_half, LANES), f32),
        ],
        scratch_shapes=[
            pltpu.VMEM((round_up(3 * n_rel, LANES), wide), bf16),
            pltpu.VMEM((wide, n_right), bf16),
            pltpu.VMEM((slots, wide), bf16),
            pltpu.VMEM((slots, wide), bf16),
            pltpu.VMEM((n_rel, wide), f32),
            pltpu.VMEM((rows, wide), f32),
        ],
        compiler_params=pltpu.CompilerParams(vmem_limit_bytes=56 << 20),
        name="edges",
    )(count_arg, bound, ids, mult, left_part, right_part, rel_wide)

    def right_sum(query, c_hi, c_lo):
        group_block = lambda lanes: pl.BlockSpec((edges, lanes), lambda i: (i, 0))
        return pl.pallas_call(
            right_kernel,
            grid=(groups,),
            in_specs=[group_block(wide), group_block(n_right), group_block(n_right)],
            out_specs=whole((n_right, wide)),
            out_shape=jax.ShapeDtypeStruct((n_right, wide), f32),
            scratch_shapes=[pltpu.VMEM((wide, n_right), f32)],
            compiler_params=pltpu.CompilerParams(vmem_limit_bytes=48 << 20),
            cost_estimate=pl.CostEstimate(flops=4 * slots * wide * n_right, bytes_accessed=6 * slots * wide, transcendentals=0),
            name="right_sum",
        )(query, c_hi, c_lo)

    odd = lax.rem(lax.axis_index("col"), 2) == 1
    few = packed_rel // 2
    grad_rel = jnp.where(odd, grad_rel[few:], grad_rel[:few]) + swap(
        jnp.where(odd, grad_rel[:few], grad_rel[few:]), "col", n_col, 1
    )
    for bit in bits_of(n_row):
        grad_rel = grad_rel + swap(grad_rel, "row", n_row, bit)
    come, grad_rel = tie(swap(far, "col", n_col, 1), grad_rel)
    half = packed_half // 2
    sum_a = jnp.concatenate([near[:half] + come[:half], grad_rel], axis=0)
    sum_b = near[half:] + come[half:]
    sum_a, sum_b, query, c_hi, c_lo = tie(sum_a, sum_b, query, c_hi, c_lo)
    grad_right = None
    for bit_a, bit_b in zip(route_a, route_b):
        half = sum_b.shape[0] // 2
        more_a, more_b = swap(sum_a[half:], "col", n_col, bit_a), swap(sum_b[half:], "col", n_col, bit_b)
        if grad_right is None:
            grad_right = right_sum(query, c_hi, c_lo)
            more_a, more_b, grad_right = tie(more_a, more_b, grad_right)
        else:
            more_a, more_b = tie(more_a, more_b)
        keep_a, keep_b, keep_rel = sum_a[:half], sum_b[:half], sum_a[2 * half :]
        if half > packed_rows(chunk):
            sum_a = jnp.concatenate([keep_a + more_a[:half], keep_rel + more_a[half:]], axis=0)
            sum_a, sum_b = tie(sum_a, keep_b + more_b)
    grad_rel = keep_rel + more_a[half:]
    other = swap(grad_rel, "col", n_col, 1)
    new_left, new_left_state = finish(
        ((0, 1), (2, 3)), chunk, tail, (keep_a, more_a[:half], keep_b, more_b), left_emb[0], left_state, "new_left"
    )
    grad_rel = jnp.concatenate([jnp.where(odd, other, grad_rel), jnp.where(odd, grad_rel, other)], axis=0)
    new_rel, new_rel_state = finish(((0,),), n_rel // 2, tail, (grad_rel,), relation, rel_state, "new_rel")
    grad_right = reduce_chunks(grad_right, "row", n_row)

    def adagrad(embedding, accumulator, gradient):
        new_accum = accumulator + jnp.sum(gradient * gradient, axis=-1) / width
        gradient = from_halves(gradient, width)
        return embedding - learn_rate * gradient / (jnp.sqrt(new_accum)[..., None] + epsilon), new_accum

    new_right, new_right_state = adagrad(right_emb[0], right_state[0], grad_right)
    return new_left[None], new_left_state, new_right[None], new_right_state[None], new_rel, new_rel_state[0]


def solution(mesh):
    entities = (P("row", "col", None), P("row", "col"), P("col", "row", None), P("col", "row"), P(), P())
    return jax.shard_map(
        functools.partial(body, mesh.shape["row"], mesh.shape["col"]),
        mesh=mesh,
        in_specs=entities + (P("row", "col", None),) * 3 + (P("row", "col", None, None), P("row", "col")),
        out_specs=entities,
        check_vma=False,
    )
```

time: 130 us -> 117 us (0.900)
  Pallas kernels: 62.1 us -> 45.7 us
  starting transfers between devices: 20.8 us -> 31.7 us
  waiting for transfers between devices: 29 us -> 20.2 us
  other arithmetic: 9.76 us -> 11.8 us
    pallas_call x5 -> x4, Pallas kernels: 54.7 us -> 38.3 us  [the longest x1 26.4 us: body(): pl.pallas_call(functools.partial(edge_kernel, rows, chunk, tail), grid=(g...]
    ppermute x22 -> x19, starting transfers between devices: 20.8 us -> 31.7 us  [swap(): return lax.ppermute(array, axis, [(i, i ^ bit) for i in range(size)])]
    ppermute x22 -> x19, waiting for transfers between devices: 29 us -> 20.2 us  [swap(): return lax.ppermute(array, axis, [(i, i ^ bit) for i in range(size)])]
    unnamed x28 -> x27, local copies, waits for them, and re-layouts: 4.89 us -> 2.7 us
    slice x1 -> x3, local copies, waits for them, and re-layouts: 0.01 us -> 1.93 us  [the longest x2 1.29 us: body(): keep_a, keep_b, keep_rel = (sum_a[:half], sum_b[:half], sum_a[2 * half:])]
    sub x3 -> x1, other arithmetic: 1.76 us -> 0.21 us  [adagrad(): embedding - learn_rate * gradient / (jnp.sqrt(new_accum)[..., None] + eps...]
  transfers between devices with their start and end apart: 22 -> 19, of which waited for: 11 -> 9; matrix products, arithmetic and copies ran while one was open for 7% -> 9% of each run, Pallas kernels for 25% -> 17%
where the time goes in v3:
time: 117 us
  Pallas kernels  45.7 us (39%)
  starting transfers between devices  31.7 us (27%)
  waiting for transfers between devices  20.2 us (17%)
  other arithmetic  11.8 us (10%)
  local copies, waits for them, and re-layouts  5.36 us (5%)
  between operations  1.82 us (2%)
    ppermute x19, starting transfers between devices, swap(): return lax.ppermute(array, axis, [(i, i ^ bit) for i in range(size)])  31.7 us
    pallas_call x1, Pallas kernels, body(): pl.pallas_call(functools.partial(edge_kernel, rows, chunk, tail), grid=(g...  26.4 us
    ppermute x19, waiting for transfers between devices, swap(): return lax.ppermute(array, axis, [(i, i ^ bit) for i in range(size)])  20.2 us
    pallas_call x1, Pallas kernels, body(): pl.pallas_call(functools.partial(prep_kernel, n_row, n_col, left_share, r...  7.86 us
    pallas_call x1, Pallas kernels, right_sum(): pl.pallas_call(right_kernel, grid=(groups,), in_specs=[group_block(wide),...  7.4 us
    pallas_call x2, Pallas kernels, finish(): pl.pallas_call(functools.partial(finish_kernel, parts, chunk, tail), out_...  4.01 us
    unnamed x27, local copies, waits for them, and re-layouts  2.7 us
  transfers between devices with their start and end apart: 19, of which 9 were waited for; matrix products, arithmetic and copies ran while one was open for 9% of the time, Pallas kernels for 17%

profile of v3, /device:TPU:0, one launch (start us, length us, event | category | flops | bytes accessed | tf_op | source)
XLA Modules:
  0.0 116.6 jit_solution(13414240403299601996)
XLA Ops:
  2.4 4.1 %collective-permute-start = (bf16[48,512]{1,0:T(8,128)(2,1)S(1)}, bf16[48,512]{1,0:T(8,128)(2,1)S(1)}, u32[]{:S(2)}, u32[]{:S(2)}) collective-permute-start(bf16[48,512]{1,0:T(8,128)(2,1)S(1)} %get-tuple-element.55), channel_id=1, source_target_pairs={{0,8},{1,9},{2,10},{3,11},{4,12},{5,13},{6,14},{7,15},{8,0},{9,1},... | collective-permute-start | bytes 147464 | tf_op jit(solution)/shard_map/ppermute | solution.py:43
  6.5 1.5 %collective-permute-start.1 = (bf16[48,512]{1,0:T(8,128)(2,1)S(1)}, bf16[48,512]{1,0:T(8,128)(2,1)S(1)}, u32[]{:S(2)}, u32[]{:S(2)}) collective-permute-start(bf16[48,512]{1,0:T(8,128)(2,1)S(1)} %get-tuple-element.56), channel_id=1, source_target_pairs={{0,2},{1,3},{2,0},{3,1},{4,6},{5,7},{6,4},{7,5},{8,10},{9,11},{10,... | collective-permute-start | bytes 147464 | tf_op jit(solution)/shard_map/ppermute | solution.py:43
  8.0 1.2 %copy.17 = f32[1,256,400]{2,1,0:T(8,128)S(1)} copy(f32[1,256,400]{1,2,0:T(8,128)} %param.13) | data formatting | bytes 819200 | tf_op args[2]
  9.5 1.6 %collective-permute-start.6 = (bf16[256,512]{1,0:T(8,128)(2,1)S(1)}, bf16[256,512]{1,0:T(8,128)(2,1)S(1)}, u32[]{:S(2)}, u32[]{:S(2)}) collective-permute-start(bf16[256,512]{1,0:T(8,128)(2,1)S(1)} %pad_maximum_fusion.5), channel_id=1, source_target_pairs={{0,16},{16,0},{1,17},{17,1},{2,18},{18,2},{3,19},{19,3},{4,20},{20... | collective-permute-start | bytes 786440 | tf_op jit(solution)/shard_map/ppermute | solution.py:43
  14.9 1.6 %collective-permute-start.2 = (bf16[96,512]{1,0:T(8,128)(2,1)S(1)}, bf16[96,512]{1,0:T(8,128)(2,1)S(1)}, u32[]{:S(2)}, u32[]{:S(2)}) collective-permute-start(bf16[96,512]{1,0:T(8,128)(2,1)S(1)} %get-tuple-element.59), channel_id=1, source_target_pairs={{0,4},{1,5},{2,6},{3,7},{4,0},{5,1},{6,2},{7,3},{8,12},{9,13},{10,... | collective-permute-start | bytes 294920 | tf_op jit(solution)/shard_map/ppermute | solution.py:43
  17.0 7.9 %prep.1 = (s32[4,8,1024]{2,1,0:T(8,128)S(1)}, f32[4,1,512]{2,1,0:T(1,128)S(1)}, s32[4,1,128]{2,1,0:T(1,128)S(1)}) custom-call(s32[3]{0:T(128)S(1)} %pad_add_fusion.1.where_ref, s32[4,4,1024]{2,1,0:T(4,128)S(1)} %pad.27.raw_ref), custom_call_target="tpu_custom_call" | custom-call | flops 67108864 | bytes 131072 | tf_op jit(solution)/shard_map/prep/pallas_call | solution.py:411
  27.5 3.2 %collective-permute-done.4 = bf16[192,512]{1,0:T(8,128)(2,1)S(1)} collective-permute-done((bf16[192,512]{1,0:T(8,128)(2,1)S(1)}, bf16[192,512]{1,0:T(8,128)(2,1)S(1)}, u32[]{:S(2)}, u32[]{:S(2)}) %collective-permute-start.4) | collective-permute-done | bytes 196640 | tf_op jit(solution)/shard_map/ppermute | solution.py:43
  31.4 2.3 %collective-permute-done.7 = bf16[768,512]{1,0:T(8,128)(2,1)S(1)} collective-permute-done((bf16[768,512]{1,0:T(8,128)(2,1)S(1)}, bf16[768,512]{1,0:T(8,128)(2,1)S(1)}, u32[]{:S(2)}, u32[]{:S(2)}) %collective-permute-start.7) | collective-permute-done | bytes 786464 | tf_op jit(solution)/shard_map/ppermute | solution.py:43
  33.6 1.3 %pad_maximum_fusion.left_ref = bf16[1536,512]{1,0:T(8,128)(2,1)} fusion(bf16[768,512]{1,0:T(8,128)(2,1)S(1)} %collective-permute-done.7, bf16[768,512]{1,0:T(8,128)(2,1)S(1)} %pad_maximum_fusion.1), kind=kLoop, calls=%fused_computation | loop fusion | flops 3145728 | bytes 3145728 | tf_op jit(solution)/shard_map/concatenate | solution.py:439
  34.9 26.4 %edges.1 = (bf16[4096,512]{1,0:T(8,128)(2,1)}, bf16[4096,512]{1,0:T(8,128)(2,1)}, bf16[4096,512]{1,0:T(8,128)(2,1)}, f32[208,128]{1,0:T(8,128)}, f32[2432,128]{1,0:T(8,128)}, /*index=5*/f32[2432,128]{1,0:T(8,128)}) custom-call(s32[1]{0:T(128)} %bitcast.18.count_ref, s32[4,128]{1,0:T(4,128)} %bitcast.19, s32[4,8,1024]{2,1,0:T(8,128)} %copy-done, ...), custom_call_target="tpu_custom_call" | custom-call | tf_op jit(solution)/shard_map/edges/pallas_call | solution.py:445
  61.3 10.0 %collective-permute-start.8 = (f32[2432,128]{1,0:T(8,128)}, f32[2432,128]{1,0:T(8,128)S(1)}, u32[]{:S(2)}, u32[]{:S(2)}) collective-permute-start(f32[2432,128]{1,0:T(8,128)} %get-tuple-element.77), channel_id=1, source_target_pairs={{0,1},{1,0},{2,3},{3,2},{4,5},{5,4},{6,7},{7,6},{8,9},{9,8},{10,11... | collective-permute-start | bytes 3735560 | tf_op jit(solution)/shard_map/ppermute | solution.py:43
  72.2 1.8 %collective-permute-done.9 = f32[104,128]{1,0:T(8,128)S(1)} collective-permute-done((f32[104,128]{1,0:T(8,128)S(1)}, f32[104,128]{1,0:T(8,128)S(1)}, u32[]{:S(2)}, u32[]{:S(2)}) %collective-permute-start.9) | collective-permute-done | bytes 53280 | tf_op jit(solution)/shard_map/ppermute | solution.py:43
  75.7 3.4 %collective-permute-done.10 = f32[104,128]{1,0:T(8,128)S(1)} collective-permute-done((f32[104,128]{1,0:T(8,128)S(1)}, f32[104,128]{1,0:T(8,128)S(1)}, u32[]{:S(2)}, u32[]{:S(2)}) %collective-permute-start.10) | collective-permute-done | bytes 53280 | tf_op jit(solution)/shard_map/ppermute | solution.py:43
  79.1 1.5 %slice_add_fusion = (f32[1216,128]{1,0:T(8,128)S(1)}, f32[1216,128]{1,0:T(8,128)S(1)}) fusion(f32[2432,128]{1,0:T(8,128)S(1)} %collective-permute-done.8, f32[2432,128]{1,0:T(8,128)} %get-tuple-element.76), kind=kLoop, calls=%fused_computation.3 | loop fusion | flops 311296 | bytes 3735552 | tf_op jit(solution)/shard_map/add | solution.py:509
  82.6 7.4 %right_sum.1 = f32[512,512]{1,0:T(8,128)S(1)} custom-call(bf16[4096,512]{1,0:T(8,128)(2,1)S(1)} %copy-done.3, bf16[4096,512]{1,0:T(8,128)(2,1)} %get-tuple-element.87.c_hi_ref, bf16[4096,512]{1,0:T(8,128)(2,1)} %get-tuple-element.88.c_lo_ref), custom_call_target="tpu_custom_call" | custom-call | flops 4294967296 | bytes 12582912 | tf_op jit(solution)/shard_map/right_sum/pallas_call | solution.py:487
  90.8 1.6 %collective-permute-start.13 = (f32[408,128]{1,0:T(8,128)S(1)}, f32[408,128]{1,0:T(8,128)S(1)}, u32[]{:S(2)}, u32[]{:S(2)}) collective-permute-start(f32[408,128]{1,0:T(8,128)S(1)} %slice.144), channel_id=1, source_target_pairs={{0,4},{1,5},{2,6},{3,7},{4,0},{5,1},{6,2},{7,3},{8,12},{9,13},{10,... | collective-permute-start | bytes 626696 | tf_op jit(solution)/shard_map/ppermute | solution.py:43
  92.5 2.7 %collective-permute-start.14 = (f32[304,128]{1,0:T(8,128)S(1)}, f32[304,128]{1,0:T(8,128)S(1)}, u32[]{:S(2)}, u32[]{:S(2)}) collective-permute-start(f32[304,128]{1,0:T(8,128)S(1)} %slice.145), channel_id=1, source_target_pairs={{0,8},{1,9},{2,10},{3,11},{4,12},{5,13},{6,14},{7,15},{8,0},{9,1},... | collective-permute-start | bytes 466952 | tf_op jit(solution)/shard_map/ppermute | solution.py:43
  95.2 4.5 %collective-permute-done.14 = f32[304,128]{1,0:T(8,128)S(1)} collective-permute-done((f32[304,128]{1,0:T(8,128)S(1)}, f32[304,128]{1,0:T(8,128)S(1)}, u32[]{:S(2)}, u32[]{:S(2)}) %collective-permute-start.14) | collective-permute-done | bytes 155680 | tf_op jit(solution)/shard_map/ppermute | solution.py:43
  99.8 2.7 %collective-permute-start.15 = (f32[256,128]{1,0:T(8,128)S(1)}, f32[256,128]{1,0:T(8,128)S(1)}, u32[]{:S(2)}, u32[]{:S(2)}) collective-permute-start(f32[256,128]{1,0:T(8,128)S(1)} %slice.151), channel_id=1, source_target_pairs={{0,8},{1,9},{2,10},{3,11},{4,12},{5,13},{6,14},{7,15},{8,0},{9,1},... | collective-permute-start | bytes 393224 | tf_op jit(solution)/shard_map/ppermute | solution.py:43
  103.1 1.3 %collective-permute-start.16 = (f32[152,128]{1,0:T(8,128)S(1)}, f32[152,128]{1,0:T(8,128)S(1)}, u32[]{:S(2)}, u32[]{:S(2)}) collective-permute-start(f32[152,128]{1,0:T(8,128)S(1)} %get-tuple-element.117), channel_id=1, source_target_pairs={{0,2},{1,3},{2,0},{3,1},{4,6},{5,7},{6,4},{7,5},{8,10},{9,11},{10,... | collective-permute-start | bytes 233480 | tf_op jit(solution)/shard_map/ppermute | solution.py:43
  104.8 2.8 %collective-permute-done.16.refs_3_ = f32[152,128]{1,0:T(8,128)S(1)} collective-permute-done((f32[152,128]{1,0:T(8,128)S(1)}, f32[152,128]{1,0:T(8,128)S(1)}, u32[]{:S(2)}, u32[]{:S(2)}) %collective-permute-start.16) | collective-permute-done | bytes 77856 | tf_op jit(solution)/shard_map/ppermute | solution.py:43
  108.9 2.1 %new_left.1 = (f32[96,400]{1,0:T(8,128)}, f32[1,96]{1,0:T(1,128)}) custom-call(f32[152,128]{1,0:T(8,128)} %slice.150.refs_0_, f32[152,128]{1,0:T(8,128)} %slice.153.refs_1_, f32[152,128]{1,0:T(8,128)} %get-tuple-element.116.refs_2_, f32[152,128]{1,0:T(8,128)} %copy-done.5, f32[96,400]{1,0:T(8,128)} %bitcast.20, f32[1,96]{1,0:T(1,128)} %refs_5_.1), custom_call_target="tpu_custom_call" | custom-call | tf_op jit(solution)/shard_map/new_left/pallas_call | solution.py:204
  111.7 1.9 %new_rel.1 = (f32[64,400]{1,0:T(8,128)}, f32[1,64]{1,0:T(1,128)}) custom-call(f32[208,128]{1,0:T(8,128)} %pad_maximum_fusion.9.refs_0_, f32[64,400]{1,0:T(8,128)} %refs_1_.1, f32[1,64]{1,0:T(1,128)} %bitcast.23), custom_call_target="tpu_custom_call" | custom-call | tf_op jit(solution)/shard_map/new_rel/pallas_call | solution.py:204
  113.6 1.1 collective-permute-done.17
  (105 shorter events, 19.0 us)
Async XLA Ops:
  2.4 9.2 %copy-start.6 = (s32[1,1,4000]{2,1,0:T(1,128)S(1)}, s32[1,1,4000]{2,1,0:T(1,128)}, u32[]{:S(2)}) copy-start(s32[1,1,4000]{2,1,0:T(1,128)} %param.17) | copy-start | bytes 48004
  2.4 10.0 %copy-start.7 = (s32[1,1,4000]{2,1,0:T(1,128)S(1)}, s32[1,1,4000]{2,1,0:T(1,128)}, u32[]{:S(2)}) copy-start(s32[1,1,4000]{2,1,0:T(1,128)} %param.18) | copy-start | bytes 48004
  2.4 10.8 %copy-start.8 = (s32[1,1,4000]{2,1,0:T(1,128)S(1)}, s32[1,1,4000]{2,1,0:T(1,128)}, u32[]{:S(2)}) copy-start(s32[1,1,4000]{2,1,0:T(1,128)} %param.19) | copy-start | bytes 48004
  2.4 11.5 %copy-start.9 = (s32[1,1,4,1000]{3,2,1,0:T(4,128)S(1)}, s32[1,1,4,1000]{3,2,1,0:T(4,128)}, u32[]{:S(2)}) copy-start(s32[1,1,4,1000]{3,2,1,0:T(4,128)} %param.20) | copy-start | bytes 48004
  2.4 11.6 %copy-start.4 = (f32[64,400]{1,0:T(8,128)S(1)}, f32[64,400]{1,0:T(8,128)}, u32[]{:S(2)}) copy-start(f32[64,400]{1,0:T(8,128)} %refs_1_.1) | copy-start | bytes 307204
  2.4 12.4 %collective-permute-start = (bf16[48,512]{1,0:T(8,128)(2,1)S(1)}, bf16[48,512]{1,0:T(8,128)(2,1)S(1)}, u32[]{:S(2)}, u32[]{:S(2)}) collective-permute-start(bf16[48,512]{1,0:T(8,128)(2,1)S(1)} %get-tuple-element.55), channel_id=1, source_target_pairs={{0,8},{1,9},{2,10},{3,11},{4,12},{5,13},{6,14},{7,15},{8,0},{9,1},... | collective-permute-start | bytes 147464 | tf_op jit(solution)/shard_map/ppermute | solution.py:43
  6.5 8.3 %collective-permute-start.1 = (bf16[48,512]{1,0:T(8,128)(2,1)S(1)}, bf16[48,512]{1,0:T(8,128)(2,1)S(1)}, u32[]{:S(2)}, u32[]{:S(2)}) collective-permute-start(bf16[48,512]{1,0:T(8,128)(2,1)S(1)} %get-tuple-element.56), channel_id=1, source_target_pairs={{0,2},{1,3},{2,0},{3,1},{4,6},{5,7},{6,4},{7,5},{8,10},{9,11},{10,... | collective-permute-start | bytes 147464 | tf_op jit(solution)/shard_map/ppermute | solution.py:43
  9.5 17.1 %collective-permute-start.6 = (bf16[256,512]{1,0:T(8,128)(2,1)S(1)}, bf16[256,512]{1,0:T(8,128)(2,1)S(1)}, u32[]{:S(2)}, u32[]{:S(2)}) collective-permute-start(bf16[256,512]{1,0:T(8,128)(2,1)S(1)} %pad_maximum_fusion.5), channel_id=1, source_target_pairs={{0,16},{16,0},{1,17},{17,1},{2,18},{18,2},{3,19},{19,3},{4,20},{20... | collective-permute-start | bytes 786440 | tf_op jit(solution)/shard_map/ppermute | solution.py:43
  14.9 9.9 %collective-permute-start.2 = (bf16[96,512]{1,0:T(8,128)(2,1)S(1)}, bf16[96,512]{1,0:T(8,128)(2,1)S(1)}, u32[]{:S(2)}, u32[]{:S(2)}) collective-permute-start(bf16[96,512]{1,0:T(8,128)(2,1)S(1)} %get-tuple-element.59), channel_id=1, source_target_pairs={{0,4},{1,5},{2,6},{3,7},{4,0},{5,1},{6,2},{7,3},{8,12},{9,13},{10,... | collective-permute-start | bytes 294920 | tf_op jit(solution)/shard_map/ppermute | solution.py:43
  16.5 8.3 %collective-permute-start.3 = (bf16[96,512]{1,0:T(8,128)(2,1)S(1)}, bf16[96,512]{1,0:T(8,128)(2,1)S(1)}, u32[]{:S(2)}, u32[]{:S(2)}) collective-permute-start(bf16[96,512]{1,0:T(8,128)(2,1)S(1)} %get-tuple-element.60), channel_id=1, source_target_pairs={{0,8},{1,9},{2,10},{3,11},{4,12},{5,13},{6,14},{7,15},{8,0},{9,1},... | collective-permute-start | bytes 294920 | tf_op jit(solution)/shard_map/ppermute | solution.py:43
  24.9 5.7 %collective-permute-start.4 = (bf16[192,512]{1,0:T(8,128)(2,1)S(1)}, bf16[192,512]{1,0:T(8,128)(2,1)S(1)}, u32[]{:S(2)}, u32[]{:S(2)}) collective-permute-start(bf16[192,512]{1,0:T(8,128)(2,1)S(1)} %pad_maximum_fusion.7), channel_id=1, source_target_pairs={{0,2},{1,3},{2,0},{3,1},{4,6},{5,7},{6,4},{7,5},{8,10},{9,11},{10,... | collective-permute-start | bytes 589832 | tf_op jit(solution)/shard_map/ppermute | solution.py:43
  25.5 5.7 %collective-permute-start.5 = (bf16[192,512]{1,0:T(8,128)(2,1)S(1)}, bf16[192,512]{1,0:T(8,128)(2,1)S(1)}, u32[]{:S(2)}, u32[]{:S(2)}) collective-permute-start(bf16[192,512]{1,0:T(8,128)(2,1)S(1)} %pad_maximum_fusion.8), channel_id=1, source_target_pairs={{0,4},{1,5},{2,6},{3,7},{4,0},{5,1},{6,2},{7,3},{8,12},{9,13},{10,... | collective-permute-start | bytes 589832 | tf_op jit(solution)/shard_map/ppermute | solution.py:43
  31.3 2.4 %collective-permute-start.7 = (bf16[768,512]{1,0:T(8,128)(2,1)S(1)}, bf16[768,512]{1,0:T(8,128)(2,1)S(1)}, u32[]{:S(2)}, u32[]{:S(2)}) collective-permute-start(bf16[768,512]{1,0:T(8,128)(2,1)S(1)} %pad_maximum_fusion.1), channel_id=1, source_target_pairs={{0,1},{1,0},{2,3},{3,2},{4,5},{5,4},{6,7},{7,6},{8,9},{9,8},{10,11... | collective-permute-start | bytes 2359304 | tf_op jit(solution)/shard_map/ppermute | solution.py:43
  61.3 17.8 %collective-permute-start.8 = (f32[2432,128]{1,0:T(8,128)}, f32[2432,128]{1,0:T(8,128)S(1)}, u32[]{:S(2)}, u32[]{:S(2)}) collective-permute-start(f32[2432,128]{1,0:T(8,128)} %get-tuple-element.77), channel_id=1, source_target_pairs={{0,1},{1,0},{2,3},{3,2},{4,5},{5,4},{6,7},{7,6},{8,9},{9,8},{10,11... | collective-permute-start | bytes 3735560 | tf_op jit(solution)/shard_map/ppermute | solution.py:43
  72.2 1.8 %collective-permute-start.9 = (f32[104,128]{1,0:T(8,128)S(1)}, f32[104,128]{1,0:T(8,128)S(1)}, u32[]{:S(2)}, u32[]{:S(2)}) collective-permute-start(f32[104,128]{1,0:T(8,128)S(1)} %slice_select_fusion.2), channel_id=1, source_target_pairs={{0,1},{1,0},{2,3},{3,2},{4,5},{5,4},{6,7},{7,6},{8,9},{9,8},{10,11... | collective-permute-start | bytes 159752 | tf_op jit(solution)/shard_map/ppermute | solution.py:43
  74.9 4.2 %collective-permute-start.10 = (f32[104,128]{1,0:T(8,128)S(1)}, f32[104,128]{1,0:T(8,128)S(1)}, u32[]{:S(2)}, u32[]{:S(2)}) collective-permute-start(f32[104,128]{1,0:T(8,128)S(1)} %select_add_fusion), channel_id=1, source_target_pairs={{0,16},{16,0},{1,17},{17,1},{2,18},{18,2},{3,19},{19,3},{4,20},{20... | collective-permute-start | bytes 159752 | tf_op jit(solution)/shard_map/ppermute | solution.py:43
  80.7 9.3 %collective-permute-start.12 = (f32[608,128]{1,0:T(8,128)S(1)}, f32[608,128]{1,0:T(8,128)S(1)}, u32[]{:S(2)}, u32[]{:S(2)}) collective-permute-start(f32[608,128]{1,0:T(8,128)S(1)} %slice.138), channel_id=1, source_target_pairs={{0,4},{1,5},{2,6},{3,7},{4,0},{5,1},{6,2},{7,3},{8,12},{9,13},{10,... | collective-permute-start | bytes 933896 | tf_op jit(solution)/shard_map/ppermute | solution.py:43
  81.5 9.2 %collective-permute-start.11 = (f32[712,128]{1,0:T(8,128)S(1)}, f32[712,128]{1,0:T(8,128)S(1)}, u32[]{:S(2)}, u32[]{:S(2)}) collective-permute-start(f32[712,128]{1,0:T(8,128)S(1)} %slice.137), channel_id=1, source_target_pairs={{0,2},{1,3},{2,0},{3,1},{4,6},{5,7},{6,4},{7,5},{8,10},{9,11},{10,... | collective-permute-start | bytes 1093640 | tf_op jit(solution)/shard_map/ppermute | solution.py:43
  90.8 8.8 %collective-permute-start.13 = (f32[408,128]{1,0:T(8,128)S(1)}, f32[408,128]{1,0:T(8,128)S(1)}, u32[]{:S(2)}, u32[]{:S(2)}) collective-permute-start(f32[408,128]{1,0:T(8,128)S(1)} %slice.144), channel_id=1, source_target_pairs={{0,4},{1,5},{2,6},{3,7},{4,0},{5,1},{6,2},{7,3},{8,12},{9,13},{10,... | collective-permute-start | bytes 626696 | tf_op jit(solution)/shard_map/ppermute | solution.py:43
  92.5 7.2 %collective-permute-start.14 = (f32[304,128]{1,0:T(8,128)S(1)}, f32[304,128]{1,0:T(8,128)S(1)}, u32[]{:S(2)}, u32[]{:S(2)}) collective-permute-start(f32[304,128]{1,0:T(8,128)S(1)} %slice.145), channel_id=1, source_target_pairs={{0,8},{1,9},{2,10},{3,11},{4,12},{5,13},{6,14},{7,15},{8,0},{9,1},... | collective-permute-start | bytes 466952 | tf_op jit(solution)/shard_map/ppermute | solution.py:43
  99.8 7.8 %collective-permute-start.15 = (f32[256,128]{1,0:T(8,128)S(1)}, f32[256,128]{1,0:T(8,128)S(1)}, u32[]{:S(2)}, u32[]{:S(2)}) collective-permute-start(f32[256,128]{1,0:T(8,128)S(1)} %slice.151), channel_id=1, source_target_pairs={{0,8},{1,9},{2,10},{3,11},{4,12},{5,13},{6,14},{7,15},{8,0},{9,1},... | collective-permute-start | bytes 393224 | tf_op jit(solution)/shard_map/ppermute | solution.py:43
  103.1 4.4 %collective-permute-start.16 = (f32[152,128]{1,0:T(8,128)S(1)}, f32[152,128]{1,0:T(8,128)S(1)}, u32[]{:S(2)}, u32[]{:S(2)}) collective-permute-start(f32[152,128]{1,0:T(8,128)S(1)} %get-tuple-element.117), channel_id=1, source_target_pairs={{0,2},{1,3},{2,0},{3,1},{4,6},{5,7},{6,4},{7,5},{8,10},{9,11},{10,... | collective-permute-start | bytes 233480 | tf_op jit(solution)/shard_map/ppermute | solution.py:43
  104.4 10.3 %collective-permute-start.17 = (f32[256,512]{1,0:T(8,128)S(1)}, f32[256,512]{1,0:T(8,128)S(1)}, u32[]{:S(2)}, u32[]{:S(2)}) collective-permute-start(f32[256,512]{1,0:T(8,128)S(1)} %slice.156), channel_id=1, source_target_pairs={{0,16},{16,0},{1,17},{17,1},{2,18},{18,2},{3,19},{19,3},{4,20},{20... | collective-permute-start | bytes 1572872 | tf_op jit(solution)/shard_map/ppermute | solution.py:43
  107.6 3.4 %collective-permute-start.18 = (f32[104,128]{1,0:T(8,128)S(1)}, f32[104,128]{1,0:T(8,128)S(1)}, u32[]{:S(2)}, u32[]{:S(2)}) collective-permute-start(f32[104,128]{1,0:T(8,128)S(1)} %slice_add_fusion.7), channel_id=1, source_target_pairs={{0,1},{1,0},{2,3},{3,2},{4,5},{5,4},{6,7},{7,6},{8,9},{9,8},{10,11... | collective-permute-start | bytes 159752 | tf_op jit(solution)/shard_map/ppermute | solution.py:43
  (7 other events, 40.2 us)

commit v4 on v3

--- a/solution.py
+++ b/solution.py
@@ -13,6 +13,7 @@
 SUB = 512
 WINDOW = 128
 SPAN = 512
+RIGHT_CHUNK = 64
 
 learn_rate = 0.1
 epsilon = 1e-10
@@ -92,11 +93,16 @@
     return (apart & 1) * (2 * quarter) + jnp.where(within < half, first + within, second + within + (quarter - half))
 
 
-def prep_kernel(n_row, n_col, left_share, rows, where_ref, raw_ref, ids_ref, mult_ref, bound_ref):
+def prep_kernel(n_row, n_col, left_share, rows, where_ref, left_ref, rel_ref, right_ref, neg_ref, ids_ref, mult_ref, bound_ref, raw_ref):
     groups, _, edges = raw_ref.shape
     n_right = mult_ref.shape[2]
     n_left = left_share * n_col
     count, me_col, me_row = where_ref[0], where_ref[1], where_ref[2]
+    raw_ref[...] = jnp.zeros_like(raw_ref)
+    for g in range(groups):
+        for k, ref in enumerate((left_ref, rel_ref, right_ref)):
+            raw_ref[g, k : k + 1, :CH] = ref[0:1, g * CH : (g + 1) * CH]
+        raw_ref[g, 3:4, :CH] = neg_ref[g : g + 1, :]
 
     def group_step(g, carry):
         raw = raw_ref[g]
@@ -172,18 +178,18 @@
     return first, jnp.where(lane < tail, mixed, turned), jnp.where(lane < tail, turned, mixed), fourth
 
 
-def finish_kernel(parts, chunk, tail, *refs):
+def finish_kernel(parts, size, chunk, tail, flip, turned, where_ref, *refs):
     n_grads = sum(len(p) for p in parts)
     grads, (emb_ref, state_ref, new_ref, new_state_ref) = refs[:n_grads], refs[n_grads:]
-    width = emb_ref.shape[1]
+    width = emb_ref.shape[0 if turned else 1]
+    totals = [sum(grads[k][:size] for k in part) for part in parts]
+    if flip:
+        odd = lax.rem(where_ref[1], 2) == 1
+        totals = [jnp.where(odd, totals[1], totals[0]), jnp.where(odd, totals[0], totals[1])]
     means, tiles_of = [], []
-    for part in parts:
-        total = grads[part[0]][...]
-        for k in part[1:]:
-            total = total + grads[k][...]
-        size = packed_rows(chunk)
-        for k in range(total.shape[0] // size):
-            tiles = unpack(total[k * size : (k + 1) * size], chunk, tail)
+    for total in totals:
+        for k in range(size // packed_rows(chunk)):
+            tiles = unpack(total[k * packed_rows(chunk) : (k + 1) * packed_rows(chunk)], chunk, tail)
             squares = sum(t * t for t in tiles)
             means.append(jnp.sum(squares, axis=1, keepdims=True) / width)
             tiles_of.append(tiles)
@@ -193,19 +199,28 @@
     accum = state + mean
     new_state_ref[...] = accum.T[0:1, :]
     rate = learn_rate / (jnp.sqrt(accum) + epsilon)
+    if turned:
+        tiles_of = [[jnp.concatenate(tiles, axis=0) for tiles in zip(*tiles_of)]]
+        chunk = rows
     for k, tiles in enumerate(tiles_of):
         here = slice(k * chunk, (k + 1) * chunk)
         for j, tile in enumerate(tiles):
             low, high = j * LANES, min((j + 1) * LANES, width)
-            new_ref[here, low:high] = emb_ref[here, low:high] - (rate[here] * tile)[:, : high - low]
-
-
-def finish(parts, chunk, tail, grads, embedding, state, name):
+            if turned:
+                new_ref[low:high, :] = emb_ref[low:high, :] - (rate * tile).T[: high - low]
+            else:
+                new_ref[here, low:high] = emb_ref[here, low:high] - (rate[here] * tile)[:, : high - low]
+
+
+def finish(parts, size, chunk, tail, where, grads, embedding, state, name, flip=False, turned=False):
+    vmem = pl.BlockSpec(memory_space=pltpu.VMEM)
     return pl.pallas_call(
-        functools.partial(finish_kernel, parts, chunk, tail),
-        out_shape=[jax.ShapeDtypeStruct(embedding.shape, f32), jax.ShapeDtypeStruct((1, embedding.shape[0]), f32)],
+        functools.partial(finish_kernel, parts, size, chunk, tail, flip, turned),
+        in_specs=[pl.BlockSpec(memory_space=pltpu.SMEM)] + [vmem] * (len(grads) + 2),
+        out_specs=[vmem, vmem],
+        out_shape=[jax.ShapeDtypeStruct(embedding.shape, f32), jax.ShapeDtypeStruct((1, state.size), f32)],
         name=name,
-    )(*grads, embedding, state.reshape(1, -1))
+    )(where, *grads, embedding, state.reshape(1, -1))
 
 
 def dot(a, b):
@@ -213,8 +228,8 @@
 
 
 def edge_kernel(
-    rows, chunk, tail, count_ref, bound_ref, ids_ref, mult_ref, left_ref, right_ref, rel_ref,
-    query_ref, c_hi_ref, c_lo_ref, rel_out_ref, near_ref, far_ref,
+    rows, chunk, tail, where_ref, bound_ref, ids_ref, mult_ref, own_ref, other_ref, right_ref, rel_ref,
+    query_ref, c_hi_ref, c_lo_ref, near_ref, far_ref,
     rel_parts, right_t, d_hi_ref, d_lo_ref, grad_rel_ref, piece_ref,
 ):
     step = pl.program_id(0)
@@ -223,7 +238,8 @@
     tiles_in_group = pl.num_programs(0) // mult_ref.shape[0]
     n_rel, wide = rel_ref.shape
     half = wide // 2
-    n_left, n_right = left_ref.shape[0], right_ref.shape[0]
+    n_own, n_right = own_ref.shape[0], right_ref.shape[0]
+    n_left = 2 * n_own
     rel_rows = rel_parts.shape[0]
 
     @pl.when(step == 0)
@@ -240,7 +256,7 @@
     group = step // tiles_in_group
     start = group * CH + (step - group * tiles_in_group) * tile
 
-    @pl.when(start >= count_ref[0])
+    @pl.when(start >= where_ref[0])
     def _():
         for ref in (query_ref, c_hi_ref, c_lo_ref):
             ref[...] = jnp.zeros_like(ref)
@@ -248,7 +264,7 @@
         d_hi_ref[here, :] = jnp.zeros((tile, wide), bf16)
         d_lo_ref[here, :] = jnp.zeros((tile, wide), bf16)
 
-    @pl.when(start < count_ref[0])
+    @pl.when(start < where_ref[0])
     def _():
         place = pl.multiple_of((step - group * tiles_in_group) * tile, tile)
         ids = ids_ref[group, :, pl.ds(place, tile)]
@@ -264,7 +280,7 @@
             rel_vec = dot(rel_hot, rel_parts[...])
             left_iota = lax.broadcasted_iota(jnp.int32, (SUB, n_left), 1)
             left_hot = jnp.where(left_iota == left_col, 1.0, 0.0).astype(bf16)
-            left_vec = dot(left_hot, left_ref[...])
+            left_vec = dot(left_hot[:, :n_own], own_ref[...]) + dot(left_hot[:, n_own:], other_ref[...])
             a_re, a_im = left_vec[:, :half], left_vec[:, half:]
             b_re, b_im = rel_vec[:, :half], rel_vec[:, half:]
             query = jnp.concatenate([a_re * b_re - a_im * b_im, a_re * b_im + a_im * b_re], axis=1).astype(bf16)
@@ -328,9 +344,10 @@
             return jnp.minimum(bound_ref[g, piece] // WINDOW * WINDOW, edges - SPAN)
 
         few = n_rel // 2
-        for k in range(2):
-            size = packed_rows(few)
-            rel_out_ref[k * size : (k + 1) * size, :] = pack(grad_rel_ref[k * few : (k + 1) * few, :], tail)
+        odd = lax.rem(where_ref[1], 2)
+        rel_size = packed_rows(few)
+        near_ref[-rel_size:, :] = pack(grad_rel_ref[pl.ds(pl.multiple_of(odd * few, few), few), :], tail)
+        far_ref[-rel_size:, :] = pack(grad_rel_ref[pl.ds(pl.multiple_of((1 - odd) * few, few), few), :], tail)
 
         def piece_step(piece, out_ref, shift):
             base = pl.multiple_of(piece * rows, rows)
@@ -368,7 +385,7 @@
             lax.fori_loop(0, n_pieces // 2, each, 0)
 
 
-def right_kernel(query_ref, c_hi_ref, c_lo_ref, out_ref, total):
+def right_kernel(tail, query_ref, c_hi_ref, c_lo_ref, out_ref, total):
     step = pl.program_id(0)
 
     @pl.when(step == 0)
@@ -383,7 +400,10 @@
 
     @pl.when(step == pl.num_programs(0) - 1)
     def _():
-        out_ref[...] = total[...].T
+        size = packed_rows(RIGHT_CHUNK)
+        whole_sum = total[...].T
+        for k in range(total.shape[1] // RIGHT_CHUNK):
+            out_ref[k * size : (k + 1) * size, :] = pack(whole_sum[k * RIGHT_CHUNK : (k + 1) * RIGHT_CHUNK], tail)
 
 
 def whole(shape):
@@ -404,24 +424,23 @@
 
     smem = pl.BlockSpec(memory_space=pltpu.SMEM)
     rows = left_share * 4
-    count_arg = counts.reshape(1)
     where = jnp.stack([counts[0, 0], lax.axis_index("col"), lax.axis_index("row")])
-    raw = jnp.stack([a.reshape(groups, CH) for a in (left_ids, rel_ids, right_ids, neg_ids)], axis=1)
-    raw = jnp.pad(raw, ((0, 0), (0, 0), (0, edges - CH)))
-    ids, mult, bound = pl.pallas_call(
-        functools.partial(prep_kernel, n_row, n_col, left_share, rows),
-        in_specs=[smem, whole((groups, 4, edges))],
-        out_specs=[whole((groups, 8, edges)), whole((groups, 1, n_right)), whole((groups, 1, LANES))],
-        out_shape=[
-            jax.ShapeDtypeStruct((groups, 8, edges), jnp.int32),
-            jax.ShapeDtypeStruct((groups, 1, n_right), f32),
-            jax.ShapeDtypeStruct((groups, 1, LANES), jnp.int32),
-        ],
-        cost_estimate=pl.CostEstimate(flops=16 * slots * edges, bytes_accessed=32 * slots, transcendentals=0),
-        compiler_params=pltpu.CompilerParams(vmem_limit_bytes=32 << 20),
-        name="prep",
-    )(where, raw)
-    bound = bound.reshape(groups, LANES)
+
+    def prepare(where, left_ids, rel_ids, right_ids, neg_ids):
+        return pl.pallas_call(
+            functools.partial(prep_kernel, n_row, n_col, left_share, rows),
+            in_specs=[smem] + [whole((1, groups * CH))] * 3 + [whole((groups, CH))],
+            out_specs=[whole((groups, 8, edges)), whole((groups, 1, n_right)), whole((groups, 1, LANES))],
+            out_shape=[
+                jax.ShapeDtypeStruct((groups, 8, edges), jnp.int32),
+                jax.ShapeDtypeStruct((groups, 1, n_right), f32),
+                jax.ShapeDtypeStruct((groups, 1, LANES), jnp.int32),
+            ],
+            scratch_shapes=[pltpu.VMEM((groups, 8, edges), jnp.int32)],
+            cost_estimate=pl.CostEstimate(flops=16 * slots * edges, bytes_accessed=32 * slots, transcendentals=0),
+            compiler_params=pltpu.CompilerParams(vmem_limit_bytes=32 << 20),
+            name="prep",
+        )(where, left_ids[0], rel_ids[0], right_ids[0], neg_ids[0, 0])
 
     rel_wide = to_halves(relation, half_pad)
     right_mine = to_halves(right_emb[0].astype(bf16), half_pad)
@@ -431,18 +450,26 @@
     right_part = gather_chunks(right_mine, "row", n_row)
     for step, (bit_a, bit_b) in enumerate(zip(reversed(route_a), reversed(route_b))):
         part_a, part_b = tie(part_a, part_b)
-        more_a, more_b = tie(swap(part_a, "col", n_col, bit_a), swap(part_b, "col", n_col, bit_b))
+        more_a, more_b = swap(part_a, "col", n_col, bit_a), swap(part_b, "col", n_col, bit_b)
+        if step == 1:
+            ids, mult, bound = prepare(*raw)
+            more_a, more_b, ids, mult, bound = tie(more_a, more_b, ids, mult, bound)
+        else:
+            more_a, more_b = tie(more_a, more_b)
         part_a = jnp.concatenate([part_a, more_a], axis=0)
         part_b = jnp.concatenate([part_b, more_b], axis=0)
+        if step == 0:
+            part_a, part_b, *raw = tie(part_a, part_b, where, left_ids, rel_ids, right_ids, neg_ids)
     own = jnp.concatenate([part_a, part_b], axis=0)
+    bound = bound.reshape(groups, LANES)
     own, ids, mult, bound, right_part, rel_wide = tie(own, ids, mult, bound, right_part, rel_wide)
-    left_part = jnp.concatenate([own, swap(own, "col", n_col, 1)], axis=0)
+    other = swap(own, "col", n_col, 1)
 
     tile_block = lambda lanes: pl.BlockSpec((tile, lanes), lambda i: (i, 0))
     chunk, tail = left_share // 2, width // 2 - LANES
     packed_half = n_left // 2 // chunk * packed_rows(chunk)
-    packed_rel = 2 * packed_rows(n_rel // 2)
-    query, c_hi, c_lo, grad_rel, near, far = pl.pallas_call(
+    packed_rel = packed_rows(n_rel // 2)
+    query, c_hi, c_lo, near, far = pl.pallas_call(
         functools.partial(edge_kernel, rows, chunk, tail),
         grid=(groups * tiles,),
         in_specs=[
@@ -450,7 +477,8 @@
             smem,
             whole((groups, 8, edges)),
             whole((groups, 1, n_right)),
-            whole((n_left, wide)),
+            whole((n_left // 2, wide)),
+            whole((n_left // 2, wide)),
             whole((n_right, wide)),
             whole((n_rel, wide)),
         ],
@@ -458,17 +486,15 @@
             tile_block(wide),
             tile_block(n_right),
             tile_block(n_right),
-            whole((packed_rel, LANES)),
-            whole((packed_half, LANES)),
-            whole((packed_half, LANES)),
+            whole((packed_half + packed_rel, LANES)),
+            whole((packed_half + packed_rel, LANES)),
         ],
         out_shape=[
             jax.ShapeDtypeStruct((slots, wide), bf16),
             jax.ShapeDtypeStruct((slots, n_right), bf16),
             jax.ShapeDtypeStruct((slots, n_right), bf16),
-            jax.ShapeDtypeStruct((packed_rel, LANES), f32),
-            jax.ShapeDtypeStruct((packed_half, LANES), f32),
-            jax.ShapeDtypeStruct((packed_half, LANES), f32),
+            jax.ShapeDtypeStruct((packed_half + packed_rel, LANES), f32),
+            jax.ShapeDtypeStruct((packed_half + packed_rel, LANES), f32),
         ],
         scratch_shapes=[
             pltpu.VMEM((round_up(3 * n_rel, LANES), wide), bf16),
@@ -480,63 +506,66 @@
         ],
         compiler_params=pltpu.CompilerParams(vmem_limit_bytes=56 << 20),
         name="edges",
-    )(count_arg, bound, ids, mult, left_part, right_part, rel_wide)
+    )(where, bound, ids, mult, own, other, right_part, rel_wide)
+
+    packed_right = n_right // RIGHT_CHUNK * packed_rows(RIGHT_CHUNK)
 
     def right_sum(query, c_hi, c_lo):
         group_block = lambda lanes: pl.BlockSpec((edges, lanes), lambda i: (i, 0))
         return pl.pallas_call(
-            right_kernel,
+            functools.partial(right_kernel, tail),
             grid=(groups,),
             in_specs=[group_block(wide), group_block(n_right), group_block(n_right)],
-            out_specs=whole((n_right, wide)),
-            out_shape=jax.ShapeDtypeStruct((n_right, wide), f32),
+            out_specs=whole((packed_right, LANES)),
+            out_shape=jax.ShapeDtypeStruct((packed_right, LANES), f32),
             scratch_shapes=[pltpu.VMEM((wide, n_right), f32)],
             compiler_params=pltpu.CompilerParams(vmem_limit_bytes=48 << 20),
             cost_estimate=pl.CostEstimate(flops=4 * slots * wide * n_right, bytes_accessed=6 * slots * wide, transcendentals=0),
             name="right_sum",
         )(query, c_hi, c_lo)
 
-    odd = lax.rem(lax.axis_index("col"), 2) == 1
-    few = packed_rel // 2
-    grad_rel = jnp.where(odd, grad_rel[few:], grad_rel[:few]) + swap(
-        jnp.where(odd, grad_rel[:few], grad_rel[few:]), "col", n_col, 1
+    come = swap(far, "col", n_col, 1)
+    half = packed_half // 2
+    sum_a, sum_b = near[:half] + come[:half], near[half : 2 * half] + come[half : 2 * half]
+    grad_rel = near[2 * half :] + come[2 * half :]
+    sum_a, sum_b, grad_rel, query, c_hi, c_lo = tie(sum_a, sum_b, grad_rel, query, c_hi, c_lo)
+    stages = len(route_a)
+    carried = [route_a[k] if k % 2 else route_b[k] for k in range(1, stages)]
+    alone = [("col", n_col, bit) for bit in route_a if bit not in carried]
+    half = half // 2
+    more_a, more_b = swap(sum_a[half:], "col", n_col, route_a[0]), swap(sum_b[half:], "col", n_col, route_b[0])
+    for step in [("row", n_row, bit) for bit in bits_of(n_row)] + alone[:-1]:
+        grad_rel = grad_rel + swap(grad_rel, *step)
+    grad_rel, query, c_hi, c_lo = tie(grad_rel, query, c_hi, c_lo)
+    more_rel = swap(grad_rel, *alone[-1])
+    more_a, more_b, more_rel, grad_right = tie(more_a, more_b, more_rel, right_sum(query, c_hi, c_lo))
+    sum_a, sum_b, grad_rel, grad_right = tie(sum_a[:half] + more_a, sum_b[:half] + more_b, grad_rel + more_rel, grad_right)
+    for stage in range(1, stages):
+        half = sum_b.shape[0] // 2
+        far_a, far_b = sum_a[half:], sum_b[half:]
+        if stage % 2:
+            far_a = jnp.concatenate([far_a, grad_rel], axis=0)
+        else:
+            far_b = jnp.concatenate([far_b, grad_rel], axis=0)
+        more_a, more_b = swap(far_a, "col", n_col, route_a[stage]), swap(far_b, "col", n_col, route_b[stage])
+        if stage == 1:
+            more_a, more_b, grad_right = tie(more_a, more_b, reduce_chunks(grad_right, "row", n_row))
+        elif stage == 2:
+            new_right, new_right_state = finish(
+                ((0,),), packed_right // n_row, RIGHT_CHUNK, tail, where, (grad_right,), right_emb[0].T, right_state, "new_right", turned=True
+            )
+            more_a, more_b, new_right, new_right_state = tie(more_a, more_b, new_right, new_right_state)
+        grad_rel = grad_rel + (more_a if stage % 2 else more_b)[half:]
+        if stage < stages - 1:
+            sum_a, sum_b, grad_rel = tie(sum_a[:half] + more_a[:half], sum_b[:half] + more_b[:half], grad_rel)
+    other_rel = swap(grad_rel, "col", n_col, 1)
+    new_left, new_left_state = finish(
+        ((0, 1), (2, 3)), half, chunk, tail, where, (sum_a, more_a, sum_b, more_b), left_emb[0], left_state, "new_left"
     )
-    for bit in bits_of(n_row):
-        grad_rel = grad_rel + swap(grad_rel, "row", n_row, bit)
-    come, grad_rel = tie(swap(far, "col", n_col, 1), grad_rel)
-    half = packed_half // 2
-    sum_a = jnp.concatenate([near[:half] + come[:half], grad_rel], axis=0)
-    sum_b = near[half:] + come[half:]
-    sum_a, sum_b, query, c_hi, c_lo = tie(sum_a, sum_b, query, c_hi, c_lo)
-    grad_right = None
-    for bit_a, bit_b in zip(route_a, route_b):
-        half = sum_b.shape[0] // 2
-        more_a, more_b = swap(sum_a[half:], "col", n_col, bit_a), swap(sum_b[half:], "col", n_col, bit_b)
-        if grad_right is None:
-            grad_right = right_sum(query, c_hi, c_lo)
-            more_a, more_b, grad_right = tie(more_a, more_b, grad_right)
-        else:
-            more_a, more_b = tie(more_a, more_b)
-        keep_a, keep_b, keep_rel = sum_a[:half], sum_b[:half], sum_a[2 * half :]
-        if half > packed_rows(chunk):
-            sum_a = jnp.concatenate([keep_a + more_a[:half], keep_rel + more_a[half:]], axis=0)
-            sum_a, sum_b = tie(sum_a, keep_b + more_b)
-    grad_rel = keep_rel + more_a[half:]
-    other = swap(grad_rel, "col", n_col, 1)
-    new_left, new_left_state = finish(
-        ((0, 1), (2, 3)), chunk, tail, (keep_a, more_a[:half], keep_b, more_b), left_emb[0], left_state, "new_left"
+    new_rel, new_rel_state = finish(
+        ((0,), (1,)), packed_rel, n_rel // 2, tail, where, (grad_rel, other_rel), relation, rel_state, "new_rel", flip=True
     )
-    grad_rel = jnp.concatenate([jnp.where(odd, other, grad_rel), jnp.where(odd, grad_rel, other)], axis=0)
-    new_rel, new_rel_state = finish(((0,),), n_rel // 2, tail, (grad_rel,), relation, rel_state, "new_rel")
-    grad_right = reduce_chunks(grad_right, "row", n_row)
-
-    def adagrad(embedding, accumulator, gradient):
-        new_accum = accumulator + jnp.sum(gradient * gradient, axis=-1) / width
-        gradient = from_halves(gradient, width)
-        return embedding - learn_rate * gradient / (jnp.sqrt(new_accum)[..., None] + epsilon), new_accum
-
-    new_right, new_right_state = adagrad(right_emb[0], right_state[0], grad_right)
-    return new_left[None], new_left_state, new_right[None], new_right_state[None], new_rel, new_rel_state[0]
+    return new_left[None], new_left_state, new_right.T[None], new_right_state, new_rel, new_rel_state[0]
 
 
 def solution(mesh):

time: 117 us -> 112 us (0.957)
  Pallas kernels: 45.7 us -> 53 us
  starting transfers between devices: 31.7 us -> 24.8 us
  other arithmetic: 11.8 us -> 7.06 us
  local copies, waits for them, and re-layouts: 5.36 us -> 3.43 us
  waiting for transfers between devices: 20.2 us -> 21.4 us
    ppermute x19, starting transfers between devices: 31.7 us -> 24.8 us  [swap(): return lax.ppermute(array, axis, [(i, i ^ bit) for i in range(size)])]
    pallas_call x1, Pallas kernels: 26.4 us -> 30.8 us  [body(): pl.pallas_call(functools.partial(edge_kernel, rows, chunk, tail), grid=(g...]
    pallas_call x4 -> x5, Pallas kernels: 19.3 us -> 22.2 us  [the longest x1 7.96 us: prepare(): pl.pallas_call(functools.partial(prep_kernel, n_row, n_col, left_share, r...]
    unnamed x3 -> x0, other arithmetic: 2.06 us -> none
    concatenate x5 -> x2, other arithmetic: 2 us -> 0.03 us  [the longest x1 0.01 us: body(): far_a = jnp.concatenate([far_a, grad_rel], axis=0)]
    slice x3 -> x4, local copies, waits for them, and re-layouts: 1.93 us -> 0.04 us  [body(): far_a, far_b = (sum_a[half:], sum_b[half:])]
    ppermute x19, waiting for transfers between devices: 20.2 us -> 21.4 us  [swap(): return lax.ppermute(array, axis, [(i, i ^ bit) for i in range(size)])]
    unnamed x27 -> x38, local copies, waits for them, and re-layouts: 2.7 us -> 2.12 us
  transfers between devices with their start and end apart: 19 -> 19, of which waited for: 9 -> 8; matrix products, arithmetic and copies ran while one was open for 9% -> 4% of each run, Pallas kernels for 17% -> 18%
where the time goes in v4:
time: 112 us
  Pallas kernels  53 us (47%)
  starting transfers between devices  24.8 us (22%)
  waiting for transfers between devices  21.4 us (19%)
  other arithmetic  7.06 us (6%)
  local copies, waits for them, and re-layouts  3.43 us (3%)
  between operations  1.77 us (2%)
    pallas_call x1, Pallas kernels, body(): pl.pallas_call(functools.partial(edge_kernel, rows, chunk, tail), grid=(g...  30.8 us
    ppermute x19, starting transfers between devices, swap(): return lax.ppermute(array, axis, [(i, i ^ bit) for i in range(size)])  24.8 us
    ppermute x19, waiting for transfers between devices, swap(): return lax.ppermute(array, axis, [(i, i ^ bit) for i in range(size)])  21.4 us
    pallas_call x1, Pallas kernels, prepare(): pl.pallas_call(functools.partial(prep_kernel, n_row, n_col, left_share, r...  7.96 us
    pallas_call x1, Pallas kernels, right_sum(): pl.pallas_call(functools.partial(right_kernel, tail), grid=(groups,), in_...  7.56 us
    pallas_call x3, Pallas kernels, finish(): pl.pallas_call(functools.partial(finish_kernel, parts, size, chunk, tail,...  6.73 us
  transfers between devices with their start and end apart: 19, of which 8 were waited for; matrix products, arithmetic and copies ran while one was open for 4% of the time, Pallas kernels for 18%

profile of v4, /device:TPU:0, one launch (start us, length us, event | category | flops | bytes accessed | tf_op | source)
XLA Modules:
  0.0 111.5 jit_solution(1016891967536924382)
XLA Ops:
  2.5 4.1 %collective-permute-start = (bf16[48,512]{1,0:T(8,128)(2,1)S(1)}, bf16[48,512]{1,0:T(8,128)(2,1)S(1)}, u32[]{:S(2)}, u32[]{:S(2)}) collective-permute-start(bf16[48,512]{1,0:T(8,128)(2,1)S(1)} %get-tuple-element.76), channel_id=1, source_target_pairs={{0,8},{1,9},{2,10},{3,11},{4,12},{5,13},{6,14},{7,15},{8,0},{9,1},... | collective-permute-start | bytes 147464 | tf_op jit(solution)/shard_map/ppermute | solution.py:44
  6.6 1.5 %collective-permute-start.1 = (bf16[48,512]{1,0:T(8,128)(2,1)S(1)}, bf16[48,512]{1,0:T(8,128)(2,1)S(1)}, u32[]{:S(2)}, u32[]{:S(2)}) collective-permute-start(bf16[48,512]{1,0:T(8,128)(2,1)S(1)} %get-tuple-element.77), channel_id=1, source_target_pairs={{0,2},{1,3},{2,0},{3,1},{4,6},{5,7},{6,4},{7,5},{8,10},{9,11},{10,... | collective-permute-start | bytes 147464 | tf_op jit(solution)/shard_map/ppermute | solution.py:44
  9.3 1.6 %collective-permute-start.6 = (bf16[256,512]{0,1:T(8,128)(2,1)S(1)}, bf16[256,512]{0,1:T(8,128)(2,1)S(1)}, u32[]{:S(2)}, u32[]{:S(2)}) collective-permute-start(bf16[256,512]{0,1:T(8,128)(2,1)S(1)} %pad_maximum_fusion.2), channel_id=1, source_target_pairs={{0,16},{16,0},{1,17},{17,1},{2,18},{18,2},{3,19},{19,3},{4,20},{20... | collective-permute-start | bytes 786440 | tf_op jit(solution)/shard_map/ppermute | solution.py:44
  11.6 1.6 %collective-permute-start.2 = (bf16[96,512]{1,0:T(8,128)(2,1)S(1)}, bf16[96,512]{1,0:T(8,128)(2,1)S(1)}, u32[]{:S(2)}, u32[]{:S(2)}) collective-permute-start(bf16[96,512]{1,0:T(8,128)(2,1)S(1)} %get-tuple-element.82), channel_id=1, source_target_pairs={{0,4},{1,5},{2,6},{3,7},{4,0},{5,1},{6,2},{7,3},{8,12},{9,13},{10,... | collective-permute-start | bytes 294920 | tf_op jit(solution)/shard_map/ppermute | solution.py:44
  13.8 8.0 %prep.1 = (s32[4,8,1024]{2,1,0:T(8,128)S(1)}, f32[4,1,512]{2,1,0:T(1,128)S(1)}, s32[4,1,128]{2,1,0:T(1,128)S(1)}) custom-call(s32[3]{0:T(128)S(1)} %pad_add_fusion.where_ref, s32[1,4000]{1,0:T(1,128)S(1)} %bitcast.22, s32[1,4000]{1,0:T(1,128)S(1)} %bitcast.23, s32[1,4000]{1,0:T(1,128)S(1)} %bitcast.24, s32[4,1000]{1,0:T(4,128)S(1)} %bitcast.25), custom_call_target="tpu_custom_call" | custom-call | flops 67108864 | bytes 131072 | tf_op jit(solution)/shard_map/prep/pallas_call | solution.py:430
  21.8 1.6 %collective-permute-start.4 = (bf16[192,512]{1,0:T(8,128)(2,1)S(1)}, bf16[192,512]{1,0:T(8,128)(2,1)S(1)}, u32[]{:S(2)}, u32[]{:S(2)}) collective-permute-start(bf16[192,512]{1,0:T(8,128)(2,1)S(1)} %pad_maximum_fusion.4), channel_id=1, source_target_pairs={{0,2},{1,3},{2,0},{3,1},{4,6},{5,7},{6,4},{7,5},{8,10},{9,11},{10,... | collective-permute-start | bytes 589832 | tf_op jit(solution)/shard_map/ppermute | solution.py:44
  24.2 3.4 %collective-permute-done.4 = bf16[192,512]{1,0:T(8,128)(2,1)S(1)} collective-permute-done((bf16[192,512]{1,0:T(8,128)(2,1)S(1)}, bf16[192,512]{1,0:T(8,128)(2,1)S(1)}, u32[]{:S(2)}, u32[]{:S(2)}) %collective-permute-start.4) | collective-permute-done | bytes 196640 | tf_op jit(solution)/shard_map/ppermute | solution.py:44
  27.6 1.5 %collective-permute-done.5 = bf16[192,512]{1,0:T(8,128)(2,1)S(1)} collective-permute-done((bf16[192,512]{1,0:T(8,128)(2,1)S(1)}, bf16[192,512]{1,0:T(8,128)(2,1)S(1)}, u32[]{:S(2)}, u32[]{:S(2)}) %collective-permute-start.5) | collective-permute-done | bytes 196640 | tf_op jit(solution)/shard_map/ppermute | solution.py:44
  30.3 1.3 %collective-permute-done.7.other_ref = bf16[768,512]{1,0:T(8,128)(2,1)S(1)} collective-permute-done((bf16[768,512]{1,0:T(8,128)(2,1)S(1)}, bf16[768,512]{1,0:T(8,128)(2,1)S(1)}, u32[]{:S(2)}, u32[]{:S(2)}) %collective-permute-start.7) | collective-permute-done | bytes 786464 | tf_op jit(solution)/shard_map/ppermute | solution.py:44
  32.4 30.8 %edges.1 = (bf16[4096,512]{1,0:T(8,128)(2,1)}, bf16[4096,512]{1,0:T(8,128)(2,1)}, bf16[4096,512]{1,0:T(8,128)(2,1)}, f32[2536,128]{1,0:T(8,128)}, f32[2536,128]{1,0:T(8,128)}) custom-call(s32[3]{0:T(128)} %copy-done.1, s32[4,128]{1,0:T(4,128)} %bitcast.21, s32[4,8,1024]{2,1,0:T(8,128)} %copy-done, f32[4,1,512]{2,1,0:T(1,128)} %copy-done.2, ...), custom_call_target="tpu_custom_call" | custom-call | tf_op jit(solution)/shard_map/edges/pallas_call | solution.py:472
  63.4 3.1 %collective-permute-done.8 = f32[2536,128]{1,0:T(8,128)S(1)} collective-permute-done((f32[2536,128]{1,0:T(8,128)}, f32[2536,128]{1,0:T(8,128)S(1)}, u32[]{:S(2)}, u32[]{:S(2)}) %collective-permute-start.8) | collective-permute-done | bytes 1298464 | tf_op jit(solution)/shard_map/ppermute | solution.py:44
  67.3 1.6 %slice_add_fusion = (f32[1216,128]{1,0:T(8,128)S(1)}, f32[1216,128]{1,0:T(8,128)S(1)}) fusion(f32[2536,128]{1,0:T(8,128)S(1)} %collective-permute-done.8, f32[2536,128]{1,0:T(8,128)} %get-tuple-element.107), kind=kLoop, calls=%fused_computation.1 | loop fusion | flops 311296 | bytes 3735552 | tf_op jit(solution)/shard_map/add | solution.py:529
  68.9 6.9 %collective-permute-start.11 = (f32[104,128]{1,0:T(8,128)S(1)}, f32[104,128]{1,0:T(8,128)S(1)}, u32[]{:S(2)}, u32[]{:S(2)}) collective-permute-start(f32[104,128]{1,0:T(8,128)S(1)} %slice_add_fusion.7), channel_id=1, source_target_pairs={{0,16},{16,0},{1,17},{17,1},{2,18},{18,2},{3,19},{19,3},{4,20},{20... | collective-permute-start | bytes 159752 | tf_op jit(solution)/shard_map/ppermute | solution.py:44
  76.2 1.9 %collective-permute-done.11 = f32[104,128]{1,0:T(8,128)S(1)} collective-permute-done((f32[104,128]{1,0:T(8,128)S(1)}, f32[104,128]{1,0:T(8,128)S(1)}, u32[]{:S(2)}, u32[]{:S(2)}) %collective-permute-start.11) | collective-permute-done | bytes 53280 | tf_op jit(solution)/shard_map/ppermute | solution.py:44
  78.2 1.7 %collective-permute-start.12 = (f32[104,128]{1,0:T(8,128)S(1)}, f32[104,128]{1,0:T(8,128)S(1)}, u32[]{:S(2)}, u32[]{:S(2)}) collective-permute-start(f32[104,128]{1,0:T(8,128)S(1)} %add.45), channel_id=1, source_target_pairs={{0,8},{1,9},{2,10},{3,11},{4,12},{5,13},{6,14},{7,15},{8,0},{9,1},... | collective-permute-start | bytes 159752 | tf_op jit(solution)/shard_map/ppermute | solution.py:44
  79.8 7.6 %right_sum.1 = f32[1600,128]{1,0:T(8,128)S(1)} custom-call(bf16[4096,512]{1,0:T(8,128)(2,1)S(1)} %copy-done.4, bf16[4096,512]{1,0:T(8,128)(2,1)} %get-tuple-element.120.c_hi_ref, bf16[4096,512]{1,0:T(8,128)(2,1)} %get-tuple-element.121.c_lo_ref), custom_call_target="tpu_custom_call" | custom-call | flops 4294967296 | bytes 12582912 | tf_op jit(solution)/shard_map/right_sum/pallas_call | solution.py:515
  87.6 2.1 %collective-permute-start.15 = (f32[800,128]{1,0:T(8,128)S(1)}, f32[800,128]{1,0:T(8,128)S(1)}, u32[]{:S(2)}, u32[]{:S(2)}) collective-permute-start(f32[800,128]{1,0:T(8,128)S(1)} %slice.112), channel_id=1, source_target_pairs={{0,16},{16,0},{1,17},{17,1},{2,18},{18,2},{3,19},{19,3},{4,20},{20... | collective-permute-start | bytes 1228808 | tf_op jit(solution)/shard_map/ppermute | solution.py:44
  89.7 1.2 %collective-permute-start.14 = (f32[304,128]{1,0:T(8,128)S(1)}, f32[304,128]{1,0:T(8,128)S(1)}, u32[]{:S(2)}, u32[]{:S(2)}) collective-permute-start(f32[304,128]{1,0:T(8,128)S(1)} %slice.110), channel_id=1, source_target_pairs={{0,8},{1,9},{2,10},{3,11},{4,12},{5,13},{6,14},{7,15},{8,0},{9,1},... | collective-permute-start | bytes 466952 | tf_op jit(solution)/shard_map/ppermute | solution.py:44
  91.2 7.1 %collective-permute-done.15 = f32[800,128]{1,0:T(8,128)S(1)} collective-permute-done((f32[800,128]{1,0:T(8,128)S(1)}, f32[800,128]{1,0:T(8,128)S(1)}, u32[]{:S(2)}, u32[]{:S(2)}) %collective-permute-start.15) | collective-permute-done | bytes 409632 | tf_op jit(solution)/shard_map/ppermute | solution.py:44
  99.9 1.0 collective-permute-start.16
  100.9 2.6 %new_right.1 = (f32[400,256]{1,0:T(8,128)}, f32[1,256]{1,0:T(1,128)}) custom-call(s32[3]{0:T(128)} %copy-done.1, f32[800,128]{1,0:T(8,128)} %slice_add_fusion.2.refs_0_, f32[400,256]{1,0:T(8,128)} %bitcast.26, f32[1,256]{1,0:T(1,128)} %refs_2_.2), custom_call_target="tpu_custom_call" | custom-call | tf_op jit(solution)/shard_map/new_right/pallas_call | solution.py:217
  103.5 2.6 %collective-permute-done.16.refs_1_ = f32[152,128]{1,0:T(8,128)S(1)} collective-permute-done((f32[152,128]{1,0:T(8,128)S(1)}, f32[152,128]{1,0:T(8,128)S(1)}, u32[]{:S(2)}, u32[]{:S(2)}) %collective-permute-start.16) | collective-permute-done | bytes 77856 | tf_op jit(solution)/shard_map/ppermute | solution.py:44
  106.8 2.2 %new_left.1 = (f32[96,400]{1,0:T(8,128)}, f32[1,96]{1,0:T(1,128)}) custom-call(s32[3]{0:T(128)} %copy-done.1, f32[304,128]{1,0:T(8,128)} %copy-done.10, f32[152,128]{1,0:T(8,128)} %copy-done.16, f32[304,128]{1,0:T(8,128)} %copy-done.11, f32[256,128]{1,0:T(8,128)} %copy-done.14, f32[96,400]{1,0:T(8,128)} %bitcast.27, f32[1,96]{1,0:T(1,128)} %refs_5_.1), custom_call_target="tpu_custom_call" | custom-call | tf_op jit(solution)/shard_map/new_left/pallas_call | solution.py:217
  109.6 2.0 %new_rel.1 = (f32[64,400]{1,0:T(8,128)}, f32[1,64]{1,0:T(1,128)}) custom-call(s32[3]{0:T(128)} %copy-done.1, f32[104,128]{1,0:T(8,128)} %copy-done.15, f32[104,128]{1,0:T(8,128)} %copy-done.17, f32[64,400]{1,0:T(8,128)} %refs_2_.3, f32[1,64]{1,0:T(1,128)} %bitcast.28), custom_call_target="tpu_custom_call" | custom-call | tf_op jit(solution)/shard_map/new_rel/pallas_call | solution.py:217
  (98 shorter events, 11.1 us)
Async XLA Ops:
  0.6 13.0 %copy-start.13 = (f32[64,400]{1,0:T(8,128)S(1)}, f32[64,400]{1,0:T(8,128)}, u32[]{:S(2)}) copy-start(f32[64,400]{1,0:T(8,128)} %refs_2_.3) | copy-start | bytes 307204
  1.6 12.1 %copy-start.5 = (s32[1,1,4000]{2,1,0:T(1,128)S(1)}, s32[1,1,4000]{2,1,0:T(1,128)}, u32[]{:S(2)}) copy-start(s32[1,1,4000]{2,1,0:T(1,128)} %param.17) | copy-start | bytes 48004
  1.6 12.1 %copy-start.6 = (s32[1,1,4000]{2,1,0:T(1,128)S(1)}, s32[1,1,4000]{2,1,0:T(1,128)}, u32[]{:S(2)}) copy-start(s32[1,1,4000]{2,1,0:T(1,128)} %param.18) | copy-start | bytes 48004
  2.5 9.1 %collective-permute-start = (bf16[48,512]{1,0:T(8,128)(2,1)S(1)}, bf16[48,512]{1,0:T(8,128)(2,1)S(1)}, u32[]{:S(2)}, u32[]{:S(2)}) collective-permute-start(bf16[48,512]{1,0:T(8,128)(2,1)S(1)} %get-tuple-element.76), channel_id=1, source_target_pairs={{0,8},{1,9},{2,10},{3,11},{4,12},{5,13},{6,14},{7,15},{8,0},{9,1},... | collective-permute-start | bytes 147464 | tf_op jit(solution)/shard_map/ppermute | solution.py:44
  6.6 5.0 %collective-permute-start.1 = (bf16[48,512]{1,0:T(8,128)(2,1)S(1)}, bf16[48,512]{1,0:T(8,128)(2,1)S(1)}, u32[]{:S(2)}, u32[]{:S(2)}) collective-permute-start(bf16[48,512]{1,0:T(8,128)(2,1)S(1)} %get-tuple-element.77), channel_id=1, source_target_pairs={{0,2},{1,3},{2,0},{3,1},{4,6},{5,7},{6,4},{7,5},{8,10},{9,11},{10,... | collective-permute-start | bytes 147464 | tf_op jit(solution)/shard_map/ppermute | solution.py:44
  9.3 14.9 %collective-permute-start.6 = (bf16[256,512]{0,1:T(8,128)(2,1)S(1)}, bf16[256,512]{0,1:T(8,128)(2,1)S(1)}, u32[]{:S(2)}, u32[]{:S(2)}) collective-permute-start(bf16[256,512]{0,1:T(8,128)(2,1)S(1)} %pad_maximum_fusion.2), channel_id=1, source_target_pairs={{0,16},{16,0},{1,17},{17,1},{2,18},{18,2},{3,19},{19,3},{4,20},{20... | collective-permute-start | bytes 786440 | tf_op jit(solution)/shard_map/ppermute | solution.py:44
  11.6 17.5 %copy-start.1 = (s32[3]{0:T(128)}, s32[3]{0:T(128)S(1)}, u32[]{:S(2)}) copy-start(s32[3]{0:T(128)S(1)} %pad_add_fusion.where_ref) | copy-start | bytes 40
  11.6 10.1 %collective-permute-start.2 = (bf16[96,512]{1,0:T(8,128)(2,1)S(1)}, bf16[96,512]{1,0:T(8,128)(2,1)S(1)}, u32[]{:S(2)}, u32[]{:S(2)}) collective-permute-start(bf16[96,512]{1,0:T(8,128)(2,1)S(1)} %get-tuple-element.82), channel_id=1, source_target_pairs={{0,4},{1,5},{2,6},{3,7},{4,0},{5,1},{6,2},{7,3},{8,12},{9,13},{10,... | collective-permute-start | bytes 294920 | tf_op jit(solution)/shard_map/ppermute | solution.py:44
  13.3 8.5 %collective-permute-start.3 = (bf16[96,512]{1,0:T(8,128)(2,1)S(1)}, bf16[96,512]{1,0:T(8,128)(2,1)S(1)}, u32[]{:S(2)}, u32[]{:S(2)}) collective-permute-start(bf16[96,512]{1,0:T(8,128)(2,1)S(1)} %get-tuple-element.83), channel_id=1, source_target_pairs={{0,8},{1,9},{2,10},{3,11},{4,12},{5,13},{6,14},{7,15},{8,0},{9,1},... | collective-permute-start | bytes 294920 | tf_op jit(solution)/shard_map/ppermute | solution.py:44
  21.8 5.7 %collective-permute-start.4 = (bf16[192,512]{1,0:T(8,128)(2,1)S(1)}, bf16[192,512]{1,0:T(8,128)(2,1)S(1)}, u32[]{:S(2)}, u32[]{:S(2)}) collective-permute-start(bf16[192,512]{1,0:T(8,128)(2,1)S(1)} %pad_maximum_fusion.4), channel_id=1, source_target_pairs={{0,2},{1,3},{2,0},{3,1},{4,6},{5,7},{6,4},{7,5},{8,10},{9,11},{10,... | collective-permute-start | bytes 589832 | tf_op jit(solution)/shard_map/ppermute | solution.py:44
  23.4 5.7 %collective-permute-start.5 = (bf16[192,512]{1,0:T(8,128)(2,1)S(1)}, bf16[192,512]{1,0:T(8,128)(2,1)S(1)}, u32[]{:S(2)}, u32[]{:S(2)}) collective-permute-start(bf16[192,512]{1,0:T(8,128)(2,1)S(1)} %pad_maximum_fusion.5), channel_id=1, source_target_pairs={{0,4},{1,5},{2,6},{3,7},{4,0},{5,1},{6,2},{7,3},{8,12},{9,13},{10,... | collective-permute-start | bytes 589832 | tf_op jit(solution)/shard_map/ppermute | solution.py:44
  29.2 2.4 %collective-permute-start.7 = (bf16[768,512]{1,0:T(8,128)(2,1)S(1)}, bf16[768,512]{1,0:T(8,128)(2,1)S(1)}, u32[]{:S(2)}, u32[]{:S(2)}) collective-permute-start(bf16[768,512]{1,0:T(8,128)(2,1)S(1)} %pad_maximum_fusion.own_ref), channel_id=1, source_target_pairs={{0,1},{1,0},{2,3},{3,2},{4,5},{5,4},{6,7},{7,6},{8,9},{9,8},{10,11... | collective-permute-start | bytes 2359304 | tf_op jit(solution)/shard_map/ppermute | solution.py:44
  63.2 3.3 %collective-permute-start.8 = (f32[2536,128]{1,0:T(8,128)}, f32[2536,128]{1,0:T(8,128)S(1)}, u32[]{:S(2)}, u32[]{:S(2)}) collective-permute-start(f32[2536,128]{1,0:T(8,128)} %get-tuple-element.108), channel_id=1, source_target_pairs={{0,1},{1,0},{2,3},{3,2},{4,5},{5,4},{6,7},{7,6},{8,9},{9,8},{10,11... | collective-permute-start | bytes 3895304 | tf_op jit(solution)/shard_map/ppermute | solution.py:44
  67.3 12.5 %copy-start.4 = (bf16[4096,512]{1,0:T(8,128)(2,1)S(1)}, bf16[4096,512]{1,0:T(8,128)(2,1)}, u32[]{:S(2)}) copy-start(bf16[4096,512]{1,0:T(8,128)(2,1)} %get-tuple-element.119.query_ref) | copy-start | bytes 12582916
  68.9 9.3 %collective-permute-start.11 = (f32[104,128]{1,0:T(8,128)S(1)}, f32[104,128]{1,0:T(8,128)S(1)}, u32[]{:S(2)}, u32[]{:S(2)}) collective-permute-start(f32[104,128]{1,0:T(8,128)S(1)} %slice_add_fusion.7), channel_id=1, source_target_pairs={{0,16},{16,0},{1,17},{17,1},{2,18},{18,2},{3,19},{19,3},{4,20},{20... | collective-permute-start | bytes 159752 | tf_op jit(solution)/shard_map/ppermute | solution.py:44
  75.8 11.6 %collective-permute-start.10 = (f32[608,128]{1,0:T(8,128)S(1)}, f32[608,128]{1,0:T(8,128)S(1)}, u32[]{:S(2)}, u32[]{:S(2)}) collective-permute-start(f32[608,128]{1,0:T(8,128)S(1)} %slice.106), channel_id=1, source_target_pairs={{0,4},{1,5},{2,6},{3,7},{4,0},{5,1},{6,2},{7,3},{8,12},{9,13},{10,... | collective-permute-start | bytes 933896 | tf_op jit(solution)/shard_map/ppermute | solution.py:44
  76.2 11.2 %collective-permute-start.9 = (f32[608,128]{1,0:T(8,128)S(1)}, f32[608,128]{1,0:T(8,128)S(1)}, u32[]{:S(2)}, u32[]{:S(2)}) collective-permute-start(f32[608,128]{1,0:T(8,128)S(1)} %slice.105), channel_id=1, source_target_pairs={{0,2},{1,3},{2,0},{3,1},{4,6},{5,7},{6,4},{7,5},{8,10},{9,11},{10,... | collective-permute-start | bytes 933896 | tf_op jit(solution)/shard_map/ppermute | solution.py:44
  78.2 9.2 %collective-permute-start.12 = (f32[104,128]{1,0:T(8,128)S(1)}, f32[104,128]{1,0:T(8,128)S(1)}, u32[]{:S(2)}, u32[]{:S(2)}) collective-permute-start(f32[104,128]{1,0:T(8,128)S(1)} %add.45), channel_id=1, source_target_pairs={{0,8},{1,9},{2,10},{3,11},{4,12},{5,13},{6,14},{7,15},{8,0},{9,1},... | collective-permute-start | bytes 159752 | tf_op jit(solution)/shard_map/ppermute | solution.py:44
  87.6 10.8 %collective-permute-start.15 = (f32[800,128]{1,0:T(8,128)S(1)}, f32[800,128]{1,0:T(8,128)S(1)}, u32[]{:S(2)}, u32[]{:S(2)}) collective-permute-start(f32[800,128]{1,0:T(8,128)S(1)} %slice.112), channel_id=1, source_target_pairs={{0,16},{16,0},{1,17},{17,1},{2,18},{18,2},{3,19},{19,3},{4,20},{20... | collective-permute-start | bytes 1228808 | tf_op jit(solution)/shard_map/ppermute | solution.py:44
  89.7 9.5 %collective-permute-start.14 = (f32[304,128]{1,0:T(8,128)S(1)}, f32[304,128]{1,0:T(8,128)S(1)}, u32[]{:S(2)}, u32[]{:S(2)}) collective-permute-start(f32[304,128]{1,0:T(8,128)S(1)} %slice.110), channel_id=1, source_target_pairs={{0,8},{1,9},{2,10},{3,11},{4,12},{5,13},{6,14},{7,15},{8,0},{9,1},... | collective-permute-start | bytes 466952 | tf_op jit(solution)/shard_map/ppermute | solution.py:44
  90.9 8.8 %collective-permute-start.13 = (f32[408,128]{1,0:T(8,128)S(1)}, f32[408,128]{1,0:T(8,128)S(1)}, u32[]{:S(2)}, u32[]{:S(2)}) collective-permute-start(f32[408,128]{1,0:T(8,128)S(1)} %pad_maximum_fusion.3), channel_id=1, source_target_pairs={{0,4},{1,5},{2,6},{3,7},{4,0},{5,1},{6,2},{7,3},{8,12},{9,13},{10,... | collective-permute-start | bytes 626696 | tf_op jit(solution)/shard_map/ppermute | solution.py:44
  99.8 6.3 %collective-permute-start.17 = (f32[256,128]{1,0:T(8,128)S(1)}, f32[256,128]{1,0:T(8,128)S(1)}, u32[]{:S(2)}, u32[]{:S(2)}) collective-permute-start(f32[256,128]{1,0:T(8,128)S(1)} %pad_maximum_fusion.6), channel_id=1, source_target_pairs={{0,2},{1,3},{2,0},{3,1},{4,6},{5,7},{6,4},{7,5},{8,10},{9,11},{10,... | collective-permute-start | bytes 393224 | tf_op jit(solution)/shard_map/ppermute | solution.py:44
  99.9 6.2 %collective-permute-start.16 = (f32[152,128]{1,0:T(8,128)S(1)}, f32[152,128]{1,0:T(8,128)S(1)}, u32[]{:S(2)}, u32[]{:S(2)}) collective-permute-start(f32[152,128]{1,0:T(8,128)S(1)} %slice.116), channel_id=1, source_target_pairs={{0,8},{1,9},{2,10},{3,11},{4,12},{5,13},{6,14},{7,15},{8,0},{9,1},... | collective-permute-start | bytes 233480 | tf_op jit(solution)/shard_map/ppermute | solution.py:44
  106.1 2.8 %collective-permute-start.18 = (f32[104,128]{1,0:T(8,128)S(1)}, f32[104,128]{1,0:T(8,128)S(1)}, u32[]{:S(2)}, u32[]{:S(2)}) collective-permute-start(f32[104,128]{1,0:T(8,128)S(1)} %slice_add_fusion.8.refs_0_), channel_id=1, source_target_pairs={{0,1},{1,0},{2,3},{3,2},{4,5},{5,4},{6,7},{7,6},{8,9},{9,8},{10,11... | collective-permute-start | bytes 159752 | tf_op jit(solution)/shard_map/ppermute | solution.py:44
  (14 other events, 75.8 us)

commit v5 on v4

--- a/solution.py
+++ b/solution.py
@@ -14,6 +14,7 @@
 WINDOW = 128
 SPAN = 512
 RIGHT_CHUNK = 64
+THIRDS = 64
 
 learn_rate = 0.1
 epsilon = 1e-10
@@ -54,8 +55,8 @@
     return array
 
 
-def reduce_chunks(array, axis, size):
-    for bit in bits_of(size):
+def reduce_chunks(array, axis, size, skip=0):
+    for bit in bits_of(size)[skip:]:
         half = array.shape[0] // 2
         array = array[:half] + swap(array[half:], axis, size, bit)
     return array
@@ -119,7 +120,8 @@
         rank = jnp.zeros((8, edges), jnp.int32)
         mult = jnp.zeros((8, n_right), f32)
         bound = jnp.zeros((8, LANES), jnp.int32)
-        lane_start = lax.broadcasted_iota(jnp.int32, (LANES, LANES), 1) * rows
+        lane = lax.broadcasted_iota(jnp.int32, (LANES, LANES), 1)
+        lane_start = jnp.where(lane < THIRDS, lane * rows, (lane - THIRDS) * (n_left // 3))
         lane_right = lax.broadcasted_iota(jnp.int32, (LANES, n_right), 1)
         for k in range(edges // LANES):
             part = cols[k * LANES : (k + 1) * LANES]
@@ -178,11 +180,10 @@
     return first, jnp.where(lane < tail, mixed, turned), jnp.where(lane < tail, turned, mixed), fourth
 
 
-def finish_kernel(parts, size, chunk, tail, flip, turned, where_ref, *refs):
-    n_grads = sum(len(p) for p in parts)
-    grads, (emb_ref, state_ref, new_ref, new_state_ref) = refs[:n_grads], refs[n_grads:]
+def finish_rows(job, tail, where_ref, grads, emb_ref, state_ref, new_ref, new_state_ref):
+    parts, size, chunk, flip, turned = job
     width = emb_ref.shape[0 if turned else 1]
-    totals = [sum(grads[k][:size] for k in part) for part in parts]
+    totals = [sum(grads[k][start : start + size] for k, start in part) for part in parts]
     if flip:
         odd = lax.rem(where_ref[1], 2) == 1
         totals = [jnp.where(odd, totals[1], totals[0]), jnp.where(odd, totals[0], totals[1])]
@@ -212,15 +213,25 @@
                 new_ref[here, low:high] = emb_ref[here, low:high] - (rate[here] * tile)[:, : high - low]
 
 
-def finish(parts, size, chunk, tail, where, grads, embedding, state, name, flip=False, turned=False):
+def finish_kernel(jobs, tail, n_grads, where_ref, *refs):
+    grads, ins, outs = refs[:n_grads], refs[n_grads : n_grads + 2 * len(jobs)], refs[n_grads + 2 * len(jobs) :]
+    for k, job in enumerate(jobs):
+        finish_rows(job, tail, where_ref, grads, *ins[2 * k : 2 * k + 2], *outs[2 * k : 2 * k + 2])
+
+
+def finish(jobs, tail, where, grads, tables, name):
     vmem = pl.BlockSpec(memory_space=pltpu.VMEM)
+    shapes, operands = [], []
+    for embedding, state in tables:
+        operands += [embedding, state.reshape(1, -1)]
+        shapes += [jax.ShapeDtypeStruct(embedding.shape, f32), jax.ShapeDtypeStruct((1, state.size), f32)]
     return pl.pallas_call(
-        functools.partial(finish_kernel, parts, size, chunk, tail, flip, turned),
-        in_specs=[pl.BlockSpec(memory_space=pltpu.SMEM)] + [vmem] * (len(grads) + 2),
-        out_specs=[vmem, vmem],
-        out_shape=[jax.ShapeDtypeStruct(embedding.shape, f32), jax.ShapeDtypeStruct((1, state.size), f32)],
+        functools.partial(finish_kernel, jobs, tail, len(grads)),
+        in_specs=[pl.BlockSpec(memory_space=pltpu.SMEM)] + [vmem] * (len(grads) + len(operands)),
+        out_specs=[vmem] * len(shapes),
+        out_shape=shapes,
         name=name,
-    )(where, *grads, embedding, state.reshape(1, -1))
+    )(where, *grads, *operands)
 
 
 def dot(a, b):
@@ -228,9 +239,9 @@
 
 
 def edge_kernel(
-    rows, chunk, tail, where_ref, bound_ref, ids_ref, mult_ref, own_ref, other_ref, right_ref, rel_ref,
+    rows, chunk, tail, where_ref, bound_ref, ids_ref, mult_ref, own_ref, other_ref, right_ref, right_t, rel_ref,
     query_ref, c_hi_ref, c_lo_ref, near_ref, far_ref,
-    rel_parts, right_t, d_hi_ref, d_lo_ref, grad_rel_ref, piece_ref,
+    rel_parts, d_hi_ref, d_lo_ref, grad_rel_ref, piece_ref,
 ):
     step = pl.program_id(0)
     tile = query_ref.shape[0]
@@ -251,7 +262,6 @@
             piece = rest.astype(bf16)
             rel_parts[part * n_rel : (part + 1) * n_rel, :] = piece
             rest = rest - piece.astype(f32)
-        right_t[...] = right_ref[...].T
 
     group = step // tiles_in_group
     start = group * CH + (step - group * tiles_in_group) * tile
@@ -264,8 +274,7 @@
         d_hi_ref[here, :] = jnp.zeros((tile, wide), bf16)
         d_lo_ref[here, :] = jnp.zeros((tile, wide), bf16)
 
-    @pl.when(start < where_ref[0])
-    def _():
+    def run(spans):
         place = pl.multiple_of((step - group * tiles_in_group) * tile, tile)
         ids = ids_ref[group, :, pl.ds(place, tile)]
         all_cols = ids.T
@@ -278,9 +287,10 @@
             rel_iota = lax.broadcasted_iota(jnp.int32, (SUB, rel_rows), 1) % n_rel
             rel_hot = jnp.where(rel_iota == rel_col, 1.0, 0.0).astype(bf16)
             rel_vec = dot(rel_hot, rel_parts[...])
-            left_iota = lax.broadcasted_iota(jnp.int32, (SUB, n_left), 1)
+            low, high = spans[sub]
+            left_iota = lax.broadcasted_iota(jnp.int32, (SUB, high - low), 1) + low
             left_hot = jnp.where(left_iota == left_col, 1.0, 0.0).astype(bf16)
-            left_vec = dot(left_hot[:, :n_own], own_ref[...]) + dot(left_hot[:, n_own:], other_ref[...])
+            left_vec = dot(left_hot[:, : n_own - low], own_ref[low:, :]) + dot(left_hot[:, n_own - low :], other_ref[: high - n_own, :])
             a_re, a_im = left_vec[:, :half], left_vec[:, half:]
             b_re, b_im = rel_vec[:, :half], rel_vec[:, half:]
             query = jnp.concatenate([a_re * b_re - a_im * b_im, a_re * b_im + a_im * b_re], axis=1).astype(bf16)
@@ -321,16 +331,31 @@
             rel_hot_t = jnp.where(row_iota == ids[1:2, sub * SUB : (sub + 1) * SUB], 1.0, 0.0).astype(bf16)
             return dot(rel_hot_t, r_hi) + dot(rel_hot_t, r_lo)
 
-        subs = tile // SUB
         fetched, weighed, rel_total = {}, {}, 0.0
-        for turn in range(subs + 2):
-            if turn < subs:
+        for turn in range(len(spans) + 2):
+            if turn < len(spans):
                 fetched[turn] = fetch(turn)
-            if 0 <= turn - 1 < subs:
+            if 0 <= turn - 1 < len(spans):
                 weighed[turn - 1] = weigh(turn - 1, fetched[turn - 1][1])
-            if 0 <= turn - 2 < subs:
+            if 0 <= turn - 2 < len(spans):
                 rel_total += back(turn - 2, fetched[turn - 2][0], weighed[turn - 2])
         grad_rel_ref[...] += rel_total
+
+    active = start < where_ref[0]
+    subs = tile // SUB
+    third = n_left // 3
+    if subs == 2 and tile == edges and third % LANES == 0:
+        narrow = (bound_ref[group, THIRDS + 2] >= SUB) & (bound_ref[group, THIRDS + 1] <= SUB)
+
+        @pl.when(active & narrow)
+        def _():
+            run(((0, 2 * third), (third, n_left)))
+
+        active = active & jnp.logical_not(narrow)
+
+    @pl.when(active)
+    def _():
+        run(((0, n_left),) * subs)
 
     @pl.when(step == pl.num_programs(0) - 1)
     def _():
@@ -480,6 +505,7 @@
             whole((n_left // 2, wide)),
             whole((n_left // 2, wide)),
             whole((n_right, wide)),
+            whole((wide, n_right)),
             whole((n_rel, wide)),
         ],
         out_specs=[
@@ -498,7 +524,6 @@
         ],
         scratch_shapes=[
             pltpu.VMEM((round_up(3 * n_rel, LANES), wide), bf16),
-            pltpu.VMEM((wide, n_right), bf16),
             pltpu.VMEM((slots, wide), bf16),
             pltpu.VMEM((slots, wide), bf16),
             pltpu.VMEM((n_rel, wide), f32),
@@ -506,25 +531,26 @@
         ],
         compiler_params=pltpu.CompilerParams(vmem_limit_bytes=56 << 20),
         name="edges",
-    )(where, bound, ids, mult, own, other, right_part, rel_wide)
+    )(where, bound, ids, mult, own, other, right_part, right_part.T, rel_wide)
 
     packed_right = n_right // RIGHT_CHUNK * packed_rows(RIGHT_CHUNK)
 
-    def right_sum(query, c_hi, c_lo):
-        group_block = lambda lanes: pl.BlockSpec((edges, lanes), lambda i: (i, 0))
+    def right_sum(part, query, c_hi, c_lo):
         return pl.pallas_call(
             functools.partial(right_kernel, tail),
             grid=(groups,),
-            in_specs=[group_block(wide), group_block(n_right), group_block(n_right)],
-            out_specs=whole((packed_right, LANES)),
-            out_shape=jax.ShapeDtypeStruct((packed_right, LANES), f32),
-            scratch_shapes=[pltpu.VMEM((wide, n_right), f32)],
+            in_specs=[pl.BlockSpec((edges, wide), lambda i: (i, 0))] + [pl.BlockSpec((edges, n_right // 2), lambda i: (i, part))] * 2,
+            out_specs=whole((packed_right // 2, LANES)),
+            out_shape=jax.ShapeDtypeStruct((packed_right // 2, LANES), f32),
+            scratch_shapes=[pltpu.VMEM((wide, n_right // 2), f32)],
             compiler_params=pltpu.CompilerParams(vmem_limit_bytes=48 << 20),
-            cost_estimate=pl.CostEstimate(flops=4 * slots * wide * n_right, bytes_accessed=6 * slots * wide, transcendentals=0),
+            cost_estimate=pl.CostEstimate(flops=2 * slots * wide * n_right, bytes_accessed=4 * slots * wide, transcendentals=0),
             name="right_sum",
         )(query, c_hi, c_lo)
 
-    come = swap(far, "col", n_col, 1)
+    come, near, far_right, query, c_hi, c_lo = tie(
+        swap(far, "col", n_col, 1), near, right_sum(1, query, c_hi, c_lo), query, c_hi, c_lo
+    )
     half = packed_half // 2
     sum_a, sum_b = near[:half] + come[:half], near[half : 2 * half] + come[half : 2 * half]
     grad_rel = near[2 * half :] + come[2 * half :]
@@ -534,12 +560,14 @@
     alone = [("col", n_col, bit) for bit in route_a if bit not in carried]
     half = half // 2
     more_a, more_b = swap(sum_a[half:], "col", n_col, route_a[0]), swap(sum_b[half:], "col", n_col, route_b[0])
-    for step in [("row", n_row, bit) for bit in bits_of(n_row)] + alone[:-1]:
+    lone = [("row", n_row, bit) for bit in bits_of(n_row)] + alone[:-1]
+    for step in lone[:-1]:
         grad_rel = grad_rel + swap(grad_rel, *step)
-    grad_rel, query, c_hi, c_lo = tie(grad_rel, query, c_hi, c_lo)
+    grad_rel, query, c_hi, c_lo = tie(grad_rel + swap(grad_rel, *lone[-1]), query, c_hi, c_lo)
     more_rel = swap(grad_rel, *alone[-1])
-    more_a, more_b, more_rel, grad_right = tie(more_a, more_b, more_rel, right_sum(query, c_hi, c_lo))
-    sum_a, sum_b, grad_rel, grad_right = tie(sum_a[:half] + more_a, sum_b[:half] + more_b, grad_rel + more_rel, grad_right)
+    come_right = swap(far_right, "row", n_row, 1)
+    more_a, more_b, more_rel, near_right = tie(more_a, more_b, more_rel, right_sum(0, query, c_hi, c_lo))
+    sum_a, sum_b, grad_rel, near_right = tie(sum_a[:half] + more_a, sum_b[:half] + more_b, grad_rel + more_rel, near_right)
     for stage in range(1, stages):
         half = sum_b.shape[0] // 2
         far_a, far_b = sum_a[half:], sum_b[half:]
@@ -548,22 +576,29 @@
         else:
             far_b = jnp.concatenate([far_b, grad_rel], axis=0)
         more_a, more_b = swap(far_a, "col", n_col, route_a[stage]), swap(far_b, "col", n_col, route_b[stage])
+        if stage == stages - 1:
+            other_rel = swap(grad_rel, "col", n_col, 1)
+            cross_rel = swap(grad_rel, "col", n_col, carried[-1] | 1)
+            more_a, more_b, other_rel, cross_rel = tie(more_a, more_b, other_rel, cross_rel)
         if stage == 1:
-            more_a, more_b, grad_right = tie(more_a, more_b, reduce_chunks(grad_right, "row", n_row))
+            more_a, more_b, grad_right = tie(
+                more_a, more_b, reduce_chunks(near_right + come_right, "row", n_row, skip=1)
+            )
         elif stage == 2:
-            new_right, new_right_state = finish(
-                ((0,),), packed_right // n_row, RIGHT_CHUNK, tail, where, (grad_right,), right_emb[0].T, right_state, "new_right", turned=True
-            )
+            job = (((0, 0),),), packed_right // n_row, RIGHT_CHUNK, False, True
+            new_right, new_right_state = finish((job,), tail, where, (grad_right,), ((right_emb[0].T, right_state),), "new_right")
             more_a, more_b, new_right, new_right_state = tie(more_a, more_b, new_right, new_right_state)
-        grad_rel = grad_rel + (more_a if stage % 2 else more_b)[half:]
         if stage < stages - 1:
+            grad_rel = grad_rel + (more_a if stage % 2 else more_b)[half:]
             sum_a, sum_b, grad_rel = tie(sum_a[:half] + more_a[:half], sum_b[:half] + more_b[:half], grad_rel)
-    other_rel = swap(grad_rel, "col", n_col, 1)
-    new_left, new_left_state = finish(
-        ((0, 1), (2, 3)), half, chunk, tail, where, (sum_a, more_a, sum_b, more_b), left_emb[0], left_state, "new_left"
+    jobs = (
+        (((0, 0), (1, 0)), ((2, 0), (3, 0))), half, chunk, False, False
+    ), (
+        (((4, 0), (1 if stage % 2 else 3, half)), ((5, 0), (6, 0))), packed_rel, n_rel // 2, True, False
     )
-    new_rel, new_rel_state = finish(
-        ((0,), (1,)), packed_rel, n_rel // 2, tail, where, (grad_rel, other_rel), relation, rel_state, "new_rel", flip=True
+    new_left, new_left_state, new_rel, new_rel_state = finish(
+        jobs, tail, where, (sum_a, more_a, sum_b, more_b, grad_rel, other_rel, cross_rel),
+        ((left_emb[0], left_state), (relation, rel_state)), "new_left_rel",
     )
     return new_left[None], new_left_state, new_right.T[None], new_right_state, new_rel, new_rel_state[0]
 

time: 112 us -> 108 us (0.964)
  waiting for transfers between devices: 21.4 us -> 15.5 us
  starting transfers between devices: 24.8 us -> 27.6 us
  other arithmetic: 7.06 us -> 4.85 us
  local copies, waits for them, and re-layouts: 3.43 us -> 5.11 us
    ppermute x19 -> x20, waiting for transfers between devices: 21.4 us -> 15.5 us  [swap(): return lax.ppermute(array, axis, [(i, i ^ bit) for i in range(size)])]
    ppermute x19 -> x20, starting transfers between devices: 24.8 us -> 27.6 us  [swap(): return lax.ppermute(array, axis, [(i, i ^ bit) for i in range(size)])]
    pallas_call x1 -> x2, Pallas kernels: 7.56 us -> 10.2 us  [right_sum(): pl.pallas_call(functools.partial(right_kernel, tail), grid=(groups,), in_...]
    pallas_call x3 -> x2, Pallas kernels: 6.73 us -> 5.01 us  [finish(): pl.pallas_call(functools.partial(finish_kernel, jobs, tail, len(grads)),...]
    unnamed x38 -> x44, local copies, waits for them, and re-layouts: 2.12 us -> 3.83 us
    add x1, other arithmetic: 1.57 us -> 0.19 us  [body(): near[half:2 * half] + come[half:2 * half]]
  transfers between devices with their start and end apart: 19 -> 20, of which waited for: 8 -> 7; matrix products, arithmetic and copies ran while one was open for 4% -> 4% of each run, Pallas kernels for 18% -> 19%
where the time goes in v5:
time: 108 us
  Pallas kernels  52.8 us (49%)
  starting transfers between devices  27.6 us (26%)
  waiting for transfers between devices  15.5 us (14%)
  local copies, waits for them, and re-layouts  5.11 us (5%)
  other arithmetic  4.85 us (4%)
  between operations  1.79 us (2%)
    pallas_call x1, Pallas kernels, body(): pl.pallas_call(functools.partial(edge_kernel, rows, chunk, tail), grid=(g...  29.7 us
    ppermute x20, starting transfers between devices, swap(): return lax.ppermute(array, axis, [(i, i ^ bit) for i in range(size)])  27.6 us
    ppermute x20, waiting for transfers between devices, swap(): return lax.ppermute(array, axis, [(i, i ^ bit) for i in range(size)])  15.5 us
    pallas_call x2, Pallas kernels, right_sum(): pl.pallas_call(functools.partial(right_kernel, tail), grid=(groups,), in_...  10.2 us
    pallas_call x1, Pallas kernels, prepare(): pl.pallas_call(functools.partial(prep_kernel, n_row, n_col, left_share, r...  7.88 us
    pallas_call x2, Pallas kernels, finish(): pl.pallas_call(functools.partial(finish_kernel, jobs, tail, len(grads)),...  5.01 us
    unnamed x44, local copies, waits for them, and re-layouts  3.83 us
  transfers between devices with their start and end apart: 20, of which 7 were waited for; matrix products, arithmetic and copies ran while one was open for 4% of the time, Pallas kernels for 19%

profile of v5, /device:TPU:0, one launch (start us, length us, event | category | flops | bytes accessed | tf_op | source)
XLA Modules:
  0.0 107.6 jit_solution(15626204992321355854)
XLA Ops:
  2.5 4.1 %collective-permute-start = (bf16[48,512]{1,0:T(8,128)(2,1)S(1)}, bf16[48,512]{1,0:T(8,128)(2,1)S(1)}, u32[]{:S(2)}, u32[]{:S(2)}) collective-permute-start(bf16[48,512]{1,0:T(8,128)(2,1)S(1)} %get-tuple-element.86), channel_id=1, source_target_pairs={{0,8},{1,9},{2,10},{3,11},{4,12},{5,13},{6,14},{7,15},{8,0},{9,1},... | collective-permute-start | bytes 147464 | tf_op jit(solution)/shard_map/ppermute | solution.py:45
  6.6 1.5 %collective-permute-start.1 = (bf16[48,512]{1,0:T(8,128)(2,1)S(1)}, bf16[48,512]{1,0:T(8,128)(2,1)S(1)}, u32[]{:S(2)}, u32[]{:S(2)}) collective-permute-start(bf16[48,512]{1,0:T(8,128)(2,1)S(1)} %get-tuple-element.87), channel_id=1, source_target_pairs={{0,2},{1,3},{2,0},{3,1},{4,6},{5,7},{6,4},{7,5},{8,10},{9,11},{10,... | collective-permute-start | bytes 147464 | tf_op jit(solution)/shard_map/ppermute | solution.py:45
  8.1 1.0 bitcast_convert_fusion
  9.3 1.6 %collective-permute-start.6 = (bf16[256,512]{0,1:T(8,128)(2,1)S(1)}, bf16[256,512]{0,1:T(8,128)(2,1)S(1)}, u32[]{:S(2)}, u32[]{:S(2)}) collective-permute-start(bf16[256,512]{0,1:T(8,128)(2,1)S(1)} %pad_maximum_fusion.2), channel_id=1, source_target_pairs={{0,16},{16,0},{1,17},{17,1},{2,18},{18,2},{3,19},{19,3},{4,20},{20... | collective-permute-start | bytes 786440 | tf_op jit(solution)/shard_map/ppermute | solution.py:45
  11.6 1.6 %collective-permute-start.2 = (bf16[96,512]{1,0:T(8,128)(2,1)S(1)}, bf16[96,512]{1,0:T(8,128)(2,1)S(1)}, u32[]{:S(2)}, u32[]{:S(2)}) collective-permute-start(bf16[96,512]{1,0:T(8,128)(2,1)S(1)} %get-tuple-element.92), channel_id=1, source_target_pairs={{0,4},{1,5},{2,6},{3,7},{4,0},{5,1},{6,2},{7,3},{8,12},{9,13},{10,... | collective-permute-start | bytes 294920 | tf_op jit(solution)/shard_map/ppermute | solution.py:45
  13.8 7.9 %prep.1 = (s32[4,8,1024]{2,1,0:T(8,128)S(1)}, f32[4,1,512]{2,1,0:T(1,128)S(1)}, s32[4,1,128]{2,1,0:T(1,128)S(1)}) custom-call(s32[3]{0:T(128)S(1)} %pad_add_fusion.where_ref, s32[1,4000]{1,0:T(1,128)S(1)} %bitcast.23, s32[1,4000]{1,0:T(1,128)S(1)} %bitcast.24, s32[1,4000]{1,0:T(1,128)S(1)} %bitcast.25, s32[4,1000]{1,0:T(4,128)S(1)} %bitcast.26), custom_call_target="tpu_custom_call" | custom-call | flops 67108864 | bytes 131072 | tf_op jit(solution)/shard_map/prep/pallas_call | solution.py:455
  21.8 1.6 %collective-permute-start.4 = (bf16[192,512]{1,0:T(8,128)(2,1)S(1)}, bf16[192,512]{1,0:T(8,128)(2,1)S(1)}, u32[]{:S(2)}, u32[]{:S(2)}) collective-permute-start(bf16[192,512]{1,0:T(8,128)(2,1)S(1)} %pad_maximum_fusion.4), channel_id=1, source_target_pairs={{0,2},{1,3},{2,0},{3,1},{4,6},{5,7},{6,4},{7,5},{8,10},{9,11},{10,... | collective-permute-start | bytes 589832 | tf_op jit(solution)/shard_map/ppermute | solution.py:45
  24.1 3.4 %collective-permute-done.4 = bf16[192,512]{1,0:T(8,128)(2,1)S(1)} collective-permute-done((bf16[192,512]{1,0:T(8,128)(2,1)S(1)}, bf16[192,512]{1,0:T(8,128)(2,1)S(1)}, u32[]{:S(2)}, u32[]{:S(2)}) %collective-permute-start.4) | collective-permute-done | bytes 196640 | tf_op jit(solution)/shard_map/ppermute | solution.py:45
  27.5 1.5 %collective-permute-done.5 = bf16[192,512]{1,0:T(8,128)(2,1)S(1)} collective-permute-done((bf16[192,512]{1,0:T(8,128)(2,1)S(1)}, bf16[192,512]{1,0:T(8,128)(2,1)S(1)}, u32[]{:S(2)}, u32[]{:S(2)}) %collective-permute-start.5) | collective-permute-done | bytes 196640 | tf_op jit(solution)/shard_map/ppermute | solution.py:45
  30.2 1.3 %collective-permute-done.7.other_ref = bf16[768,512]{1,0:T(8,128)(2,1)S(1)} collective-permute-done((bf16[768,512]{1,0:T(8,128)(2,1)S(1)}, bf16[768,512]{1,0:T(8,128)(2,1)S(1)}, u32[]{:S(2)}, u32[]{:S(2)}) %collective-permute-start.7) | collective-permute-done | bytes 786464 | tf_op jit(solution)/shard_map/ppermute | solution.py:45
  32.3 29.7 %edges.1 = (bf16[4096,512]{1,0:T(8,128)(2,1)}, bf16[4096,512]{1,0:T(8,128)(2,1)}, bf16[4096,512]{1,0:T(8,128)(2,1)}, f32[2536,128]{1,0:T(8,128)}, f32[2536,128]{1,0:T(8,128)}) custom-call(s32[3]{0:T(128)} %copy-done.3, s32[4,128]{1,0:T(4,128)} %bitcast.22, s32[4,8,1024]{2,1,0:T(8,128)} %copy-done.1, f32[4,1,512]{2,1,0:T(1,128)} %copy-done.2, ...), custom_call_target="tpu_custom_call" | custom-call | tf_op jit(solution)/shard_map/edges/pallas_call | solution.py:497
  62.1 5.3 %collective-permute-start.8 = (f32[2536,128]{1,0:T(8,128)}, f32[2536,128]{1,0:T(8,128)S(1)}, u32[]{:S(2)}, u32[]{:S(2)}) collective-permute-start(f32[2536,128]{1,0:T(8,128)} %get-tuple-element.117), channel_id=1, source_target_pairs={{0,1},{1,0},{2,3},{3,2},{4,5},{5,4},{6,7},{7,6},{8,9},{9,8},{10,11... | collective-permute-start | bytes 3895304 | tf_op jit(solution)/shard_map/ppermute | solution.py:45
  67.3 2.2 %copy-done = bf16[4096,512]{1,0:T(8,128)(2,1)S(1)} copy-done((bf16[4096,512]{1,0:T(8,128)(2,1)S(1)}, bf16[4096,512]{1,0:T(8,128)(2,1)}, u32[]{:S(2)}) %copy-start) | copy-done | bytes 4194328
  69.5 5.2 %right_sum.2 = f32[800,128]{1,0:T(8,128)S(1)} custom-call(bf16[4096,512]{1,0:T(8,128)(2,1)S(1)} %copy-done, bf16[4096,512]{1,0:T(8,128)(2,1)} %get-tuple-element.135.c_hi_ref, bf16[4096,512]{1,0:T(8,128)(2,1)} %get-tuple-element.136.c_lo_ref), custom_call_target="tpu_custom_call" | custom-call | flops 2147483648 | bytes 8388608 | tf_op jit(solution)/shard_map/right_sum/pallas_call | solution.py:539
  75.5 1.5 %collective-permute-start.11 = (f32[104,128]{1,0:T(8,128)S(1)}, f32[104,128]{1,0:T(8,128)S(1)}, u32[]{:S(2)}, u32[]{:S(2)}) collective-permute-start(f32[104,128]{1,0:T(8,128)S(1)} %slice_add_fusion.7), channel_id=1, source_target_pairs={{0,16},{16,0},{1,17},{17,1},{2,18},{18,2},{3,19},{19,3},{4,20},{20... | collective-permute-start | bytes 159752 | tf_op jit(solution)/shard_map/ppermute | solution.py:45
  77.6 2.3 %collective-permute-done.11 = f32[104,128]{1,0:T(8,128)S(1)} collective-permute-done((f32[104,128]{1,0:T(8,128)S(1)}, f32[104,128]{1,0:T(8,128)S(1)}, u32[]{:S(2)}, u32[]{:S(2)}) %collective-permute-start.11) | collective-permute-done | bytes 53280 | tf_op jit(solution)/shard_map/ppermute | solution.py:45
  79.9 2.9 %collective-permute-start.12 = (f32[104,128]{1,0:T(8,128)S(1)}, f32[104,128]{1,0:T(8,128)S(1)}, u32[]{:S(2)}, u32[]{:S(2)}) collective-permute-start(f32[104,128]{1,0:T(8,128)S(1)} %add.42), channel_id=1, source_target_pairs={{0,8},{1,9},{2,10},{3,11},{4,12},{5,13},{6,14},{7,15},{8,0},{9,1},... | collective-permute-start | bytes 159752 | tf_op jit(solution)/shard_map/ppermute | solution.py:45
  82.8 5.0 %right_sum.3 = f32[800,128]{1,0:T(8,128)S(1)} custom-call(bf16[4096,512]{1,0:T(8,128)(2,1)S(1)} %copy-done, bf16[4096,512]{1,0:T(8,128)(2,1)} %get-tuple-element.135.c_hi_ref, bf16[4096,512]{1,0:T(8,128)(2,1)} %get-tuple-element.136.c_lo_ref), custom_call_target="tpu_custom_call" | custom-call | flops 2147483648 | bytes 8388608 | tf_op jit(solution)/shard_map/right_sum/pallas_call | solution.py:539
  88.2 2.2 %collective-permute-start.14 = (f32[304,128]{1,0:T(8,128)S(1)}, f32[304,128]{1,0:T(8,128)S(1)}, u32[]{:S(2)}, u32[]{:S(2)}) collective-permute-start(f32[304,128]{1,0:T(8,128)S(1)} %slice.101), channel_id=1, source_target_pairs={{0,8},{1,9},{2,10},{3,11},{4,12},{5,13},{6,14},{7,15},{8,0},{9,1},... | collective-permute-start | bytes 466952 | tf_op jit(solution)/shard_map/ppermute | solution.py:45
  91.2 6.2 %collective-permute-done.14 = f32[304,128]{1,0:T(8,128)S(1)} collective-permute-done((f32[304,128]{1,0:T(8,128)S(1)}, f32[304,128]{1,0:T(8,128)S(1)}, u32[]{:S(2)}, u32[]{:S(2)}) %collective-permute-start.14) | collective-permute-done | bytes 155680 | tf_op jit(solution)/shard_map/ppermute | solution.py:45
  97.5 1.6 %collective-permute-start.17 = (f32[256,128]{1,0:T(8,128)S(1)}, f32[256,128]{1,0:T(8,128)S(1)}, u32[]{:S(2)}, u32[]{:S(2)}) collective-permute-start(f32[256,128]{1,0:T(8,128)S(1)} %pad_maximum_fusion.6), channel_id=1, source_target_pairs={{0,2},{1,3},{2,0},{3,1},{4,6},{5,7},{6,4},{7,5},{8,10},{9,11},{10,... | collective-permute-start | bytes 393224 | tf_op jit(solution)/shard_map/ppermute | solution.py:45
  99.1 1.3 %collective-permute-start.16 = (f32[152,128]{1,0:T(8,128)S(1)}, f32[152,128]{1,0:T(8,128)S(1)}, u32[]{:S(2)}, u32[]{:S(2)}) collective-permute-start(f32[152,128]{1,0:T(8,128)S(1)} %slice.105), channel_id=1, source_target_pairs={{0,8},{1,9},{2,10},{3,11},{4,12},{5,13},{6,14},{7,15},{8,0},{9,1},... | collective-permute-start | bytes 233480 | tf_op jit(solution)/shard_map/ppermute | solution.py:45
  101.0 2.6 %new_right.1 = (f32[400,256]{1,0:T(8,128)}, f32[1,256]{1,0:T(1,128)}) custom-call(s32[3]{0:T(128)} %copy-done.3, f32[800,128]{1,0:T(8,128)} %add.46.refs_0_, f32[400,256]{1,0:T(8,128)} %bitcast.28, f32[1,256]{1,0:T(1,128)} %refs_2_.1), custom_call_target="tpu_custom_call" | custom-call | tf_op jit(solution)/shard_map/new_right/pallas_call | solution.py:228
  105.2 2.4 %new_left_rel.1 = (f32[96,400]{1,0:T(8,128)}, f32[1,96]{1,0:T(1,128)}, f32[64,400]{1,0:T(8,128)}, f32[1,64]{1,0:T(1,128)}) custom-call(s32[3]{0:T(128)} %copy-done.3, f32[304,128]{1,0:T(8,128)} %copy-done.12, f32[152,128]{1,0:T(8,128)} %copy-done.18, f32[304,128]{1,0:T(8,128)} %copy-done.13, f32[256,128]{1,0:T(8,128)} %copy-done.17, f32[104,128]{1,0:T(8,128)} %copy-done.16, ...), custom_call_target="tpu_custom_call" | custom-call | tf_op jit(solution)/shard_map/new_left_rel/pallas_call | solution.py:228
  (104 shorter events, 10.1 us)
Async XLA Ops:
  0.6 13.0 %copy-start.15 = (f32[64,400]{1,0:T(8,128)S(1)}, f32[64,400]{1,0:T(8,128)}, u32[]{:S(2)}) copy-start(f32[64,400]{1,0:T(8,128)} %refs_9_.1) | copy-start | bytes 307204
  1.6 12.1 %copy-start.5 = (s32[1,1,4000]{2,1,0:T(1,128)S(1)}, s32[1,1,4000]{2,1,0:T(1,128)}, u32[]{:S(2)}) copy-start(s32[1,1,4000]{2,1,0:T(1,128)} %param.17) | copy-start | bytes 48004
  1.6 12.1 %copy-start.6 = (s32[1,1,4000]{2,1,0:T(1,128)S(1)}, s32[1,1,4000]{2,1,0:T(1,128)}, u32[]{:S(2)}) copy-start(s32[1,1,4000]{2,1,0:T(1,128)} %param.18) | copy-start | bytes 48004
  2.5 9.1 %collective-permute-start = (bf16[48,512]{1,0:T(8,128)(2,1)S(1)}, bf16[48,512]{1,0:T(8,128)(2,1)S(1)}, u32[]{:S(2)}, u32[]{:S(2)}) collective-permute-start(bf16[48,512]{1,0:T(8,128)(2,1)S(1)} %get-tuple-element.86), channel_id=1, source_target_pairs={{0,8},{1,9},{2,10},{3,11},{4,12},{5,13},{6,14},{7,15},{8,0},{9,1},... | collective-permute-start | bytes 147464 | tf_op jit(solution)/shard_map/ppermute | solution.py:45
  6.6 5.0 %collective-permute-start.1 = (bf16[48,512]{1,0:T(8,128)(2,1)S(1)}, bf16[48,512]{1,0:T(8,128)(2,1)S(1)}, u32[]{:S(2)}, u32[]{:S(2)}) collective-permute-start(bf16[48,512]{1,0:T(8,128)(2,1)S(1)} %get-tuple-element.87), channel_id=1, source_target_pairs={{0,2},{1,3},{2,0},{3,1},{4,6},{5,7},{6,4},{7,5},{8,10},{9,11},{10,... | collective-permute-start | bytes 147464 | tf_op jit(solution)/shard_map/ppermute | solution.py:45
  9.3 14.8 %collective-permute-start.6 = (bf16[256,512]{0,1:T(8,128)(2,1)S(1)}, bf16[256,512]{0,1:T(8,128)(2,1)S(1)}, u32[]{:S(2)}, u32[]{:S(2)}) collective-permute-start(bf16[256,512]{0,1:T(8,128)(2,1)S(1)} %pad_maximum_fusion.2), channel_id=1, source_target_pairs={{0,16},{16,0},{1,17},{17,1},{2,18},{18,2},{3,19},{19,3},{4,20},{20... | collective-permute-start | bytes 786440 | tf_op jit(solution)/shard_map/ppermute | solution.py:45
  11.6 17.4 %copy-start.3 = (s32[3]{0:T(128)}, s32[3]{0:T(128)S(1)}, u32[]{:S(2)}) copy-start(s32[3]{0:T(128)S(1)} %pad_add_fusion.where_ref) | copy-start | bytes 40
  11.6 10.1 %collective-permute-start.2 = (bf16[96,512]{1,0:T(8,128)(2,1)S(1)}, bf16[96,512]{1,0:T(8,128)(2,1)S(1)}, u32[]{:S(2)}, u32[]{:S(2)}) collective-permute-start(bf16[96,512]{1,0:T(8,128)(2,1)S(1)} %get-tuple-element.92), channel_id=1, source_target_pairs={{0,4},{1,5},{2,6},{3,7},{4,0},{5,1},{6,2},{7,3},{8,12},{9,13},{10,... | collective-permute-start | bytes 294920 | tf_op jit(solution)/shard_map/ppermute | solution.py:45
  13.3 8.4 %collective-permute-start.3 = (bf16[96,512]{1,0:T(8,128)(2,1)S(1)}, bf16[96,512]{1,0:T(8,128)(2,1)S(1)}, u32[]{:S(2)}, u32[]{:S(2)}) collective-permute-start(bf16[96,512]{1,0:T(8,128)(2,1)S(1)} %get-tuple-element.93), channel_id=1, source_target_pairs={{0,8},{1,9},{2,10},{3,11},{4,12},{5,13},{6,14},{7,15},{8,0},{9,1},... | collective-permute-start | bytes 294920 | tf_op jit(solution)/shard_map/ppermute | solution.py:45
  21.8 5.7 %collective-permute-start.4 = (bf16[192,512]{1,0:T(8,128)(2,1)S(1)}, bf16[192,512]{1,0:T(8,128)(2,1)S(1)}, u32[]{:S(2)}, u32[]{:S(2)}) collective-permute-start(bf16[192,512]{1,0:T(8,128)(2,1)S(1)} %pad_maximum_fusion.4), channel_id=1, source_target_pairs={{0,2},{1,3},{2,0},{3,1},{4,6},{5,7},{6,4},{7,5},{8,10},{9,11},{10,... | collective-permute-start | bytes 589832 | tf_op jit(solution)/shard_map/ppermute | solution.py:45
  23.3 5.7 %collective-permute-start.5 = (bf16[192,512]{1,0:T(8,128)(2,1)S(1)}, bf16[192,512]{1,0:T(8,128)(2,1)S(1)}, u32[]{:S(2)}, u32[]{:S(2)}) collective-permute-start(bf16[192,512]{1,0:T(8,128)(2,1)S(1)} %pad_maximum_fusion.5), channel_id=1, source_target_pairs={{0,4},{1,5},{2,6},{3,7},{4,0},{5,1},{6,2},{7,3},{8,12},{9,13},{10,... | collective-permute-start | bytes 589832 | tf_op jit(solution)/shard_map/ppermute | solution.py:45
  29.1 2.4 %collective-permute-start.7 = (bf16[768,512]{1,0:T(8,128)(2,1)S(1)}, bf16[768,512]{1,0:T(8,128)(2,1)S(1)}, u32[]{:S(2)}, u32[]{:S(2)}) collective-permute-start(bf16[768,512]{1,0:T(8,128)(2,1)S(1)} %pad_maximum_fusion.own_ref), channel_id=1, source_target_pairs={{0,1},{1,0},{2,3},{3,2},{4,5},{5,4},{6,7},{7,6},{8,9},{9,8},{10,11... | collective-permute-start | bytes 2359304 | tf_op jit(solution)/shard_map/ppermute | solution.py:45
  62.1 12.6 %collective-permute-start.8 = (f32[2536,128]{1,0:T(8,128)}, f32[2536,128]{1,0:T(8,128)S(1)}, u32[]{:S(2)}, u32[]{:S(2)}) collective-permute-start(f32[2536,128]{1,0:T(8,128)} %get-tuple-element.117), channel_id=1, source_target_pairs={{0,1},{1,0},{2,3},{3,2},{4,5},{5,4},{6,7},{7,6},{8,9},{9,8},{10,11... | collective-permute-start | bytes 3895304 | tf_op jit(solution)/shard_map/ppermute | solution.py:45
  75.0 12.9 %collective-permute-start.10 = (f32[608,128]{1,0:T(8,128)S(1)}, f32[608,128]{1,0:T(8,128)S(1)}, u32[]{:S(2)}, u32[]{:S(2)}) collective-permute-start(f32[608,128]{1,0:T(8,128)S(1)} %slice.97), channel_id=1, source_target_pairs={{0,4},{1,5},{2,6},{3,7},{4,0},{5,1},{6,2},{7,3},{8,12},{9,13},{10,... | collective-permute-start | bytes 933896 | tf_op jit(solution)/shard_map/ppermute | solution.py:45
  75.1 12.8 %collective-permute-start.9 = (f32[608,128]{1,0:T(8,128)S(1)}, f32[608,128]{1,0:T(8,128)S(1)}, u32[]{:S(2)}, u32[]{:S(2)}) collective-permute-start(f32[608,128]{1,0:T(8,128)S(1)} %slice.96), channel_id=1, source_target_pairs={{0,2},{1,3},{2,0},{3,1},{4,6},{5,7},{6,4},{7,5},{8,10},{9,11},{10,... | collective-permute-start | bytes 933896 | tf_op jit(solution)/shard_map/ppermute | solution.py:45
  75.5 4.3 %collective-permute-start.11 = (f32[104,128]{1,0:T(8,128)S(1)}, f32[104,128]{1,0:T(8,128)S(1)}, u32[]{:S(2)}, u32[]{:S(2)}) collective-permute-start(f32[104,128]{1,0:T(8,128)S(1)} %slice_add_fusion.7), channel_id=1, source_target_pairs={{0,16},{16,0},{1,17},{17,1},{2,18},{18,2},{3,19},{19,3},{4,20},{20... | collective-permute-start | bytes 159752 | tf_op jit(solution)/shard_map/ppermute | solution.py:45
  77.0 13.4 %collective-permute-start.15 = (f32[800,128]{1,0:T(8,128)S(1)}, f32[800,128]{1,0:T(8,128)S(1)}, u32[]{:S(2)}, u32[]{:S(2)}) collective-permute-start(f32[800,128]{1,0:T(8,128)S(1)} %right_sum.2), channel_id=1, source_target_pairs={{0,16},{16,0},{1,17},{17,1},{2,18},{18,2},{3,19},{19,3},{4,20},{20... | collective-permute-start | bytes 1228808 | tf_op jit(solution)/shard_map/ppermute | solution.py:45
  79.9 8.0 %collective-permute-start.12 = (f32[104,128]{1,0:T(8,128)S(1)}, f32[104,128]{1,0:T(8,128)S(1)}, u32[]{:S(2)}, u32[]{:S(2)}) collective-permute-start(f32[104,128]{1,0:T(8,128)S(1)} %add.42), channel_id=1, source_target_pairs={{0,8},{1,9},{2,10},{3,11},{4,12},{5,13},{6,14},{7,15},{8,0},{9,1},... | collective-permute-start | bytes 159752 | tf_op jit(solution)/shard_map/ppermute | solution.py:45
  88.0 9.3 %collective-permute-start.13 = (f32[408,128]{1,0:T(8,128)S(1)}, f32[408,128]{1,0:T(8,128)S(1)}, u32[]{:S(2)}, u32[]{:S(2)}) collective-permute-start(f32[408,128]{1,0:T(8,128)S(1)} %pad_maximum_fusion.3), channel_id=1, source_target_pairs={{0,4},{1,5},{2,6},{3,7},{4,0},{5,1},{6,2},{7,3},{8,12},{9,13},{10,... | collective-permute-start | bytes 626696 | tf_op jit(solution)/shard_map/ppermute | solution.py:45
  88.2 9.1 %collective-permute-start.14 = (f32[304,128]{1,0:T(8,128)S(1)}, f32[304,128]{1,0:T(8,128)S(1)}, u32[]{:S(2)}, u32[]{:S(2)}) collective-permute-start(f32[304,128]{1,0:T(8,128)S(1)} %slice.101), channel_id=1, source_target_pairs={{0,8},{1,9},{2,10},{3,11},{4,12},{5,13},{6,14},{7,15},{8,0},{9,1},... | collective-permute-start | bytes 466952 | tf_op jit(solution)/shard_map/ppermute | solution.py:45
  97.5 7.0 %collective-permute-start.17 = (f32[256,128]{1,0:T(8,128)S(1)}, f32[256,128]{1,0:T(8,128)S(1)}, u32[]{:S(2)}, u32[]{:S(2)}) collective-permute-start(f32[256,128]{1,0:T(8,128)S(1)} %pad_maximum_fusion.6), channel_id=1, source_target_pairs={{0,2},{1,3},{2,0},{3,1},{4,6},{5,7},{6,4},{7,5},{8,10},{9,11},{10,... | collective-permute-start | bytes 393224 | tf_op jit(solution)/shard_map/ppermute | solution.py:45
  99.1 5.4 %collective-permute-start.16 = (f32[152,128]{1,0:T(8,128)S(1)}, f32[152,128]{1,0:T(8,128)S(1)}, u32[]{:S(2)}, u32[]{:S(2)}) collective-permute-start(f32[152,128]{1,0:T(8,128)S(1)} %slice.105), channel_id=1, source_target_pairs={{0,8},{1,9},{2,10},{3,11},{4,12},{5,13},{6,14},{7,15},{8,0},{9,1},... | collective-permute-start | bytes 233480 | tf_op jit(solution)/shard_map/ppermute | solution.py:45
  100.4 3.6 %collective-permute-start.19 = (f32[104,128]{1,0:T(8,128)S(1)}, f32[104,128]{1,0:T(8,128)S(1)}, u32[]{:S(2)}, u32[]{:S(2)}) collective-permute-start(f32[104,128]{1,0:T(8,128)S(1)} %slice_add_fusion.6.refs_4_), channel_id=1, source_target_pairs={{0,3},{1,2},{2,1},{3,0},{4,7},{5,6},{6,5},{7,4},{8,11},{9,10},{10,... | collective-permute-start | bytes 159752 | tf_op jit(solution)/shard_map/ppermute | solution.py:45
  100.4 3.6 %collective-permute-start.18 = (f32[104,128]{1,0:T(8,128)S(1)}, f32[104,128]{1,0:T(8,128)S(1)}, u32[]{:S(2)}, u32[]{:S(2)}) collective-permute-start(f32[104,128]{1,0:T(8,128)S(1)} %slice_add_fusion.6.refs_4_), channel_id=1, source_target_pairs={{0,1},{1,0},{2,3},{3,2},{4,5},{5,4},{6,7},{7,6},{8,9},{9,8},{10,11... | collective-permute-start | bytes 159752 | tf_op jit(solution)/shard_map/ppermute | solution.py:45
  (18 other events, 96.8 us)

commit v6 on v5

--- a/solution.py
+++ b/solution.py
@@ -12,7 +12,7 @@
 TILE = 1024
 SUB = 512
 WINDOW = 128
-SPAN = 512
+SPAN = 256
 RIGHT_CHUNK = 64
 THIRDS = 64
 
@@ -407,7 +407,7 @@
                 piece_step(k + shift, out_ref, shift)
                 return carry
 
-            lax.fori_loop(0, n_pieces // 2, each, 0)
+            lax.fori_loop(0, n_pieces // 2, each, 0, unroll=4)
 
 
 def right_kernel(tail, query_ref, c_hi_ref, c_lo_ref, out_ref, total):
@@ -448,7 +448,7 @@
     tiles = edges // tile
 
     smem = pl.BlockSpec(memory_space=pltpu.SMEM)
-    rows = left_share * 4
+    rows = left_share * 2
     where = jnp.stack([counts[0, 0], lax.axis_index("col"), lax.axis_index("row")])
 
     def prepare(where, left_ids, rel_ids, right_ids, neg_ids):

time: 108 us -> 106 us (0.981)
  Pallas kernels: 52.8 us -> 50.6 us
    pallas_call x1, Pallas kernels: 29.7 us -> 27.5 us  [body(): pl.pallas_call(functools.partial(edge_kernel, rows, chunk, tail), grid=(g...]
  transfers between devices with their start and end apart: 20 -> 20, of which waited for: 7 -> 7; matrix products, arithmetic and copies ran while one was open for 4% -> 4% of each run, Pallas kernels for 19% -> 20%
where the time goes in v6:
time: 106 us
  Pallas kernels  50.6 us (48%)
  starting transfers between devices  27.6 us (26%)
  waiting for transfers between devices  16 us (15%)
  local copies, waits for them, and re-layouts  5.1 us (5%)
  other arithmetic  4.85 us (5%)
  between operations  1.81 us (2%)
    ppermute x20, starting transfers between devices, swap(): return lax.ppermute(array, axis, [(i, i ^ bit) for i in range(size)])  27.6 us
    pallas_call x1, Pallas kernels, body(): pl.pallas_call(functools.partial(edge_kernel, rows, chunk, tail), grid=(g...  27.5 us
    ppermute x20, waiting for transfers between devices, swap(): return lax.ppermute(array, axis, [(i, i ^ bit) for i in range(size)])  16 us
    pallas_call x2, Pallas kernels, right_sum(): pl.pallas_call(functools.partial(right_kernel, tail), grid=(groups,), in_...  10.2 us
    pallas_call x1, Pallas kernels, prepare(): pl.pallas_call(functools.partial(prep_kernel, n_row, n_col, left_share, r...  7.88 us
    pallas_call x2, Pallas kernels, finish(): pl.pallas_call(functools.partial(finish_kernel, jobs, tail, len(grads)),...  5.01 us
    unnamed x44, local copies, waits for them, and re-layouts  3.82 us
  transfers between devices with their start and end apart: 20, of which 7 were waited for; matrix products, arithmetic and copies ran while one was open for 4% of the time, Pallas kernels for 20%

profile of v6, /device:TPU:0, one launch (start us, length us, event | category | flops | bytes accessed | tf_op | source)
XLA Modules:
  0.0 105.8 jit_solution(2806553903098061141)
XLA Ops:
  2.5 4.1 %collective-permute-start = (bf16[48,512]{1,0:T(8,128)(2,1)S(1)}, bf16[48,512]{1,0:T(8,128)(2,1)S(1)}, u32[]{:S(2)}, u32[]{:S(2)}) collective-permute-start(bf16[48,512]{1,0:T(8,128)(2,1)S(1)} %get-tuple-element.86), channel_id=1, source_target_pairs={{0,8},{1,9},{2,10},{3,11},{4,12},{5,13},{6,14},{7,15},{8,0},{9,1},... | collective-permute-start | bytes 147464 | tf_op jit(solution)/shard_map/ppermute | solution.py:45
  6.6 1.5 %collective-permute-start.1 = (bf16[48,512]{1,0:T(8,128)(2,1)S(1)}, bf16[48,512]{1,0:T(8,128)(2,1)S(1)}, u32[]{:S(2)}, u32[]{:S(2)}) collective-permute-start(bf16[48,512]{1,0:T(8,128)(2,1)S(1)} %get-tuple-element.87), channel_id=1, source_target_pairs={{0,2},{1,3},{2,0},{3,1},{4,6},{5,7},{6,4},{7,5},{8,10},{9,11},{10,... | collective-permute-start | bytes 147464 | tf_op jit(solution)/shard_map/ppermute | solution.py:45
  8.1 1.0 bitcast_convert_fusion
  9.3 1.6 %collective-permute-start.6 = (bf16[256,512]{0,1:T(8,128)(2,1)S(1)}, bf16[256,512]{0,1:T(8,128)(2,1)S(1)}, u32[]{:S(2)}, u32[]{:S(2)}) collective-permute-start(bf16[256,512]{0,1:T(8,128)(2,1)S(1)} %pad_maximum_fusion.2), channel_id=1, source_target_pairs={{0,16},{16,0},{1,17},{17,1},{2,18},{18,2},{3,19},{19,3},{4,20},{20... | collective-permute-start | bytes 786440 | tf_op jit(solution)/shard_map/ppermute | solution.py:45
  11.6 1.6 %collective-permute-start.2 = (bf16[96,512]{1,0:T(8,128)(2,1)S(1)}, bf16[96,512]{1,0:T(8,128)(2,1)S(1)}, u32[]{:S(2)}, u32[]{:S(2)}) collective-permute-start(bf16[96,512]{1,0:T(8,128)(2,1)S(1)} %get-tuple-element.92), channel_id=1, source_target_pairs={{0,4},{1,5},{2,6},{3,7},{4,0},{5,1},{6,2},{7,3},{8,12},{9,13},{10,... | collective-permute-start | bytes 294920 | tf_op jit(solution)/shard_map/ppermute | solution.py:45
  13.8 7.9 %prep.1 = (s32[4,8,1024]{2,1,0:T(8,128)S(1)}, f32[4,1,512]{2,1,0:T(1,128)S(1)}, s32[4,1,128]{2,1,0:T(1,128)S(1)}) custom-call(s32[3]{0:T(128)S(1)} %pad_add_fusion.where_ref, s32[1,4000]{1,0:T(1,128)S(1)} %bitcast.23, s32[1,4000]{1,0:T(1,128)S(1)} %bitcast.24, s32[1,4000]{1,0:T(1,128)S(1)} %bitcast.25, s32[4,1000]{1,0:T(4,128)S(1)} %bitcast.26), custom_call_target="tpu_custom_call" | custom-call | flops 67108864 | bytes 131072 | tf_op jit(solution)/shard_map/prep/pallas_call | solution.py:455
  21.8 1.6 %collective-permute-start.4 = (bf16[192,512]{1,0:T(8,128)(2,1)S(1)}, bf16[192,512]{1,0:T(8,128)(2,1)S(1)}, u32[]{:S(2)}, u32[]{:S(2)}) collective-permute-start(bf16[192,512]{1,0:T(8,128)(2,1)S(1)} %pad_maximum_fusion.4), channel_id=1, source_target_pairs={{0,2},{1,3},{2,0},{3,1},{4,6},{5,7},{6,4},{7,5},{8,10},{9,11},{10,... | collective-permute-start | bytes 589832 | tf_op jit(solution)/shard_map/ppermute | solution.py:45
  24.1 3.4 %collective-permute-done.4 = bf16[192,512]{1,0:T(8,128)(2,1)S(1)} collective-permute-done((bf16[192,512]{1,0:T(8,128)(2,1)S(1)}, bf16[192,512]{1,0:T(8,128)(2,1)S(1)}, u32[]{:S(2)}, u32[]{:S(2)}) %collective-permute-start.4) | collective-permute-done | bytes 196640 | tf_op jit(solution)/shard_map/ppermute | solution.py:45
  27.5 1.5 %collective-permute-done.5 = bf16[192,512]{1,0:T(8,128)(2,1)S(1)} collective-permute-done((bf16[192,512]{1,0:T(8,128)(2,1)S(1)}, bf16[192,512]{1,0:T(8,128)(2,1)S(1)}, u32[]{:S(2)}, u32[]{:S(2)}) %collective-permute-start.5) | collective-permute-done | bytes 196640 | tf_op jit(solution)/shard_map/ppermute | solution.py:45
  30.2 1.3 %collective-permute-done.7.other_ref = bf16[768,512]{1,0:T(8,128)(2,1)S(1)} collective-permute-done((bf16[768,512]{1,0:T(8,128)(2,1)S(1)}, bf16[768,512]{1,0:T(8,128)(2,1)S(1)}, u32[]{:S(2)}, u32[]{:S(2)}) %collective-permute-start.7) | collective-permute-done | bytes 786464 | tf_op jit(solution)/shard_map/ppermute | solution.py:45
  32.3 27.5 %edges.1 = (bf16[4096,512]{1,0:T(8,128)(2,1)}, bf16[4096,512]{1,0:T(8,128)(2,1)}, bf16[4096,512]{1,0:T(8,128)(2,1)}, f32[2536,128]{1,0:T(8,128)}, f32[2536,128]{1,0:T(8,128)}) custom-call(s32[3]{0:T(128)} %copy-done.3, s32[4,128]{1,0:T(4,128)} %bitcast.22, s32[4,8,1024]{2,1,0:T(8,128)} %copy-done.1, f32[4,1,512]{2,1,0:T(1,128)} %copy-done.2, ...), custom_call_target="tpu_custom_call" | custom-call | tf_op jit(solution)/shard_map/edges/pallas_call | solution.py:497
  60.3 2.2 %copy-done = bf16[4096,512]{1,0:T(8,128)(2,1)S(1)} copy-done((bf16[4096,512]{1,0:T(8,128)(2,1)S(1)}, bf16[4096,512]{1,0:T(8,128)(2,1)}, u32[]{:S(2)}) %copy-start) | copy-done | bytes 4194328
  62.4 5.2 %right_sum.2 = f32[800,128]{1,0:T(8,128)S(1)} custom-call(bf16[4096,512]{1,0:T(8,128)(2,1)S(1)} %copy-done, bf16[4096,512]{1,0:T(8,128)(2,1)} %get-tuple-element.135.c_hi_ref, bf16[4096,512]{1,0:T(8,128)(2,1)} %get-tuple-element.136.c_lo_ref), custom_call_target="tpu_custom_call" | custom-call | flops 2147483648 | bytes 8388608 | tf_op jit(solution)/shard_map/right_sum/pallas_call | solution.py:539
  67.9 5.3 %collective-permute-start.10 = (f32[608,128]{1,0:T(8,128)S(1)}, f32[608,128]{1,0:T(8,128)S(1)}, u32[]{:S(2)}, u32[]{:S(2)}) collective-permute-start(f32[608,128]{1,0:T(8,128)S(1)} %slice.97), channel_id=1, source_target_pairs={{0,4},{1,5},{2,6},{3,7},{4,0},{5,1},{6,2},{7,3},{8,12},{9,13},{10,... | collective-permute-start | bytes 933896 | tf_op jit(solution)/shard_map/ppermute | solution.py:45
  73.6 1.5 %collective-permute-start.11 = (f32[104,128]{1,0:T(8,128)S(1)}, f32[104,128]{1,0:T(8,128)S(1)}, u32[]{:S(2)}, u32[]{:S(2)}) collective-permute-start(f32[104,128]{1,0:T(8,128)S(1)} %slice_add_fusion.7), channel_id=1, source_target_pairs={{0,16},{16,0},{1,17},{17,1},{2,18},{18,2},{3,19},{19,3},{4,20},{20... | collective-permute-start | bytes 159752 | tf_op jit(solution)/shard_map/ppermute | solution.py:45
  75.7 2.7 %collective-permute-done.11 = f32[104,128]{1,0:T(8,128)S(1)} collective-permute-done((f32[104,128]{1,0:T(8,128)S(1)}, f32[104,128]{1,0:T(8,128)S(1)}, u32[]{:S(2)}, u32[]{:S(2)}) %collective-permute-start.11) | collective-permute-done | bytes 53280 | tf_op jit(solution)/shard_map/ppermute | solution.py:45
  78.3 2.8 %collective-permute-start.12 = (f32[104,128]{1,0:T(8,128)S(1)}, f32[104,128]{1,0:T(8,128)S(1)}, u32[]{:S(2)}, u32[]{:S(2)}) collective-permute-start(f32[104,128]{1,0:T(8,128)S(1)} %add.42), channel_id=1, source_target_pairs={{0,8},{1,9},{2,10},{3,11},{4,12},{5,13},{6,14},{7,15},{8,0},{9,1},... | collective-permute-start | bytes 159752 | tf_op jit(solution)/shard_map/ppermute | solution.py:45
  81.1 5.1 %right_sum.3 = f32[800,128]{1,0:T(8,128)S(1)} custom-call(bf16[4096,512]{1,0:T(8,128)(2,1)S(1)} %copy-done, bf16[4096,512]{1,0:T(8,128)(2,1)} %get-tuple-element.135.c_hi_ref, bf16[4096,512]{1,0:T(8,128)(2,1)} %get-tuple-element.136.c_lo_ref), custom_call_target="tpu_custom_call" | custom-call | flops 2147483648 | bytes 8388608 | tf_op jit(solution)/shard_map/right_sum/pallas_call | solution.py:539
  86.5 2.1 %collective-permute-start.14 = (f32[304,128]{1,0:T(8,128)S(1)}, f32[304,128]{1,0:T(8,128)S(1)}, u32[]{:S(2)}, u32[]{:S(2)}) collective-permute-start(f32[304,128]{1,0:T(8,128)S(1)} %slice.101), channel_id=1, source_target_pairs={{0,8},{1,9},{2,10},{3,11},{4,12},{5,13},{6,14},{7,15},{8,0},{9,1},... | collective-permute-start | bytes 466952 | tf_op jit(solution)/shard_map/ppermute | solution.py:45
  89.4 5.7 %collective-permute-done.14 = f32[304,128]{1,0:T(8,128)S(1)} collective-permute-done((f32[304,128]{1,0:T(8,128)S(1)}, f32[304,128]{1,0:T(8,128)S(1)}, u32[]{:S(2)}, u32[]{:S(2)}) %collective-permute-start.14) | collective-permute-done | bytes 155680 | tf_op jit(solution)/shard_map/ppermute | solution.py:45
  95.3 1.7 %collective-permute-start.17 = (f32[256,128]{1,0:T(8,128)S(1)}, f32[256,128]{1,0:T(8,128)S(1)}, u32[]{:S(2)}, u32[]{:S(2)}) collective-permute-start(f32[256,128]{1,0:T(8,128)S(1)} %pad_maximum_fusion.6), channel_id=1, source_target_pairs={{0,2},{1,3},{2,0},{3,1},{4,6},{5,7},{6,4},{7,5},{8,10},{9,11},{10,... | collective-permute-start | bytes 393224 | tf_op jit(solution)/shard_map/ppermute | solution.py:45
  97.0 1.3 %collective-permute-start.16 = (f32[152,128]{1,0:T(8,128)S(1)}, f32[152,128]{1,0:T(8,128)S(1)}, u32[]{:S(2)}, u32[]{:S(2)}) collective-permute-start(f32[152,128]{1,0:T(8,128)S(1)} %slice.105), channel_id=1, source_target_pairs={{0,8},{1,9},{2,10},{3,11},{4,12},{5,13},{6,14},{7,15},{8,0},{9,1},... | collective-permute-start | bytes 233480 | tf_op jit(solution)/shard_map/ppermute | solution.py:45
  98.7 2.6 %new_right.1 = (f32[400,256]{1,0:T(8,128)}, f32[1,256]{1,0:T(1,128)}) custom-call(s32[3]{0:T(128)} %copy-done.3, f32[800,128]{1,0:T(8,128)} %add.46.refs_0_, f32[400,256]{1,0:T(8,128)} %bitcast.28, f32[1,256]{1,0:T(1,128)} %refs_2_.1), custom_call_target="tpu_custom_call" | custom-call | tf_op jit(solution)/shard_map/new_right/pallas_call | solution.py:228
  103.4 2.4 %new_left_rel.1 = (f32[96,400]{1,0:T(8,128)}, f32[1,96]{1,0:T(1,128)}, f32[64,400]{1,0:T(8,128)}, f32[1,64]{1,0:T(1,128)}) custom-call(s32[3]{0:T(128)} %copy-done.3, f32[304,128]{1,0:T(8,128)} %copy-done.12, f32[152,128]{1,0:T(8,128)} %copy-done.18, f32[304,128]{1,0:T(8,128)} %copy-done.13, f32[256,128]{1,0:T(8,128)} %copy-done.17, f32[104,128]{1,0:T(8,128)} %copy-done.16, ...), custom_call_target="tpu_custom_call" | custom-call | tf_op jit(solution)/shard_map/new_left_rel/pallas_call | solution.py:228
  (104 shorter events, 10.5 us)
Async XLA Ops:
  0.6 13.0 %copy-start.15 = (f32[64,400]{1,0:T(8,128)S(1)}, f32[64,400]{1,0:T(8,128)}, u32[]{:S(2)}) copy-start(f32[64,400]{1,0:T(8,128)} %refs_9_.1) | copy-start | bytes 307204
  1.6 12.1 %copy-start.5 = (s32[1,1,4000]{2,1,0:T(1,128)S(1)}, s32[1,1,4000]{2,1,0:T(1,128)}, u32[]{:S(2)}) copy-start(s32[1,1,4000]{2,1,0:T(1,128)} %param.17) | copy-start | bytes 48004
  1.6 12.1 %copy-start.6 = (s32[1,1,4000]{2,1,0:T(1,128)S(1)}, s32[1,1,4000]{2,1,0:T(1,128)}, u32[]{:S(2)}) copy-start(s32[1,1,4000]{2,1,0:T(1,128)} %param.18) | copy-start | bytes 48004
  2.5 9.1 %collective-permute-start = (bf16[48,512]{1,0:T(8,128)(2,1)S(1)}, bf16[48,512]{1,0:T(8,128)(2,1)S(1)}, u32[]{:S(2)}, u32[]{:S(2)}) collective-permute-start(bf16[48,512]{1,0:T(8,128)(2,1)S(1)} %get-tuple-element.86), channel_id=1, source_target_pairs={{0,8},{1,9},{2,10},{3,11},{4,12},{5,13},{6,14},{7,15},{8,0},{9,1},... | collective-permute-start | bytes 147464 | tf_op jit(solution)/shard_map/ppermute | solution.py:45
  6.6 5.0 %collective-permute-start.1 = (bf16[48,512]{1,0:T(8,128)(2,1)S(1)}, bf16[48,512]{1,0:T(8,128)(2,1)S(1)}, u32[]{:S(2)}, u32[]{:S(2)}) collective-permute-start(bf16[48,512]{1,0:T(8,128)(2,1)S(1)} %get-tuple-element.87), channel_id=1, source_target_pairs={{0,2},{1,3},{2,0},{3,1},{4,6},{5,7},{6,4},{7,5},{8,10},{9,11},{10,... | collective-permute-start | bytes 147464 | tf_op jit(solution)/shard_map/ppermute | solution.py:45
  9.3 14.8 %collective-permute-start.6 = (bf16[256,512]{0,1:T(8,128)(2,1)S(1)}, bf16[256,512]{0,1:T(8,128)(2,1)S(1)}, u32[]{:S(2)}, u32[]{:S(2)}) collective-permute-start(bf16[256,512]{0,1:T(8,128)(2,1)S(1)} %pad_maximum_fusion.2), channel_id=1, source_target_pairs={{0,16},{16,0},{1,17},{17,1},{2,18},{18,2},{3,19},{19,3},{4,20},{20... | collective-permute-start | bytes 786440 | tf_op jit(solution)/shard_map/ppermute | solution.py:45
  11.6 17.4 %copy-start.3 = (s32[3]{0:T(128)}, s32[3]{0:T(128)S(1)}, u32[]{:S(2)}) copy-start(s32[3]{0:T(128)S(1)} %pad_add_fusion.where_ref) | copy-start | bytes 40
  11.6 10.1 %collective-permute-start.2 = (bf16[96,512]{1,0:T(8,128)(2,1)S(1)}, bf16[96,512]{1,0:T(8,128)(2,1)S(1)}, u32[]{:S(2)}, u32[]{:S(2)}) collective-permute-start(bf16[96,512]{1,0:T(8,128)(2,1)S(1)} %get-tuple-element.92), channel_id=1, source_target_pairs={{0,4},{1,5},{2,6},{3,7},{4,0},{5,1},{6,2},{7,3},{8,12},{9,13},{10,... | collective-permute-start | bytes 294920 | tf_op jit(solution)/shard_map/ppermute | solution.py:45
  13.3 8.4 %collective-permute-start.3 = (bf16[96,512]{1,0:T(8,128)(2,1)S(1)}, bf16[96,512]{1,0:T(8,128)(2,1)S(1)}, u32[]{:S(2)}, u32[]{:S(2)}) collective-permute-start(bf16[96,512]{1,0:T(8,128)(2,1)S(1)} %get-tuple-element.93), channel_id=1, source_target_pairs={{0,8},{1,9},{2,10},{3,11},{4,12},{5,13},{6,14},{7,15},{8,0},{9,1},... | collective-permute-start | bytes 294920 | tf_op jit(solution)/shard_map/ppermute | solution.py:45
  21.8 5.7 %collective-permute-start.4 = (bf16[192,512]{1,0:T(8,128)(2,1)S(1)}, bf16[192,512]{1,0:T(8,128)(2,1)S(1)}, u32[]{:S(2)}, u32[]{:S(2)}) collective-permute-start(bf16[192,512]{1,0:T(8,128)(2,1)S(1)} %pad_maximum_fusion.4), channel_id=1, source_target_pairs={{0,2},{1,3},{2,0},{3,1},{4,6},{5,7},{6,4},{7,5},{8,10},{9,11},{10,... | collective-permute-start | bytes 589832 | tf_op jit(solution)/shard_map/ppermute | solution.py:45
  23.3 5.7 %collective-permute-start.5 = (bf16[192,512]{1,0:T(8,128)(2,1)S(1)}, bf16[192,512]{1,0:T(8,128)(2,1)S(1)}, u32[]{:S(2)}, u32[]{:S(2)}) collective-permute-start(bf16[192,512]{1,0:T(8,128)(2,1)S(1)} %pad_maximum_fusion.5), channel_id=1, source_target_pairs={{0,4},{1,5},{2,6},{3,7},{4,0},{5,1},{6,2},{7,3},{8,12},{9,13},{10,... | collective-permute-start | bytes 589832 | tf_op jit(solution)/shard_map/ppermute | solution.py:45
  29.1 2.4 %collective-permute-start.7 = (bf16[768,512]{1,0:T(8,128)(2,1)S(1)}, bf16[768,512]{1,0:T(8,128)(2,1)S(1)}, u32[]{:S(2)}, u32[]{:S(2)}) collective-permute-start(bf16[768,512]{1,0:T(8,128)(2,1)S(1)} %pad_maximum_fusion.own_ref), channel_id=1, source_target_pairs={{0,1},{1,0},{2,3},{3,2},{4,5},{5,4},{6,7},{7,6},{8,9},{9,8},{10,11... | collective-permute-start | bytes 2359304 | tf_op jit(solution)/shard_map/ppermute | solution.py:45
  59.8 7.8 %collective-permute-start.8 = (f32[2536,128]{1,0:T(8,128)}, f32[2536,128]{1,0:T(8,128)S(1)}, u32[]{:S(2)}, u32[]{:S(2)}) collective-permute-start(f32[2536,128]{1,0:T(8,128)} %get-tuple-element.117), channel_id=1, source_target_pairs={{0,1},{1,0},{2,3},{3,2},{4,5},{5,4},{6,7},{7,6},{8,9},{9,8},{10,11... | collective-permute-start | bytes 3895304 | tf_op jit(solution)/shard_map/ppermute | solution.py:45
  67.9 18.3 %collective-permute-start.10 = (f32[608,128]{1,0:T(8,128)S(1)}, f32[608,128]{1,0:T(8,128)S(1)}, u32[]{:S(2)}, u32[]{:S(2)}) collective-permute-start(f32[608,128]{1,0:T(8,128)S(1)} %slice.97), channel_id=1, source_target_pairs={{0,4},{1,5},{2,6},{3,7},{4,0},{5,1},{6,2},{7,3},{8,12},{9,13},{10,... | collective-permute-start | bytes 933896 | tf_op jit(solution)/shard_map/ppermute | solution.py:45
  73.2 13.0 %collective-permute-start.9 = (f32[608,128]{1,0:T(8,128)S(1)}, f32[608,128]{1,0:T(8,128)S(1)}, u32[]{:S(2)}, u32[]{:S(2)}) collective-permute-start(f32[608,128]{1,0:T(8,128)S(1)} %slice.96), channel_id=1, source_target_pairs={{0,2},{1,3},{2,0},{3,1},{4,6},{5,7},{6,4},{7,5},{8,10},{9,11},{10,... | collective-permute-start | bytes 933896 | tf_op jit(solution)/shard_map/ppermute | solution.py:45
  73.6 4.7 %collective-permute-start.11 = (f32[104,128]{1,0:T(8,128)S(1)}, f32[104,128]{1,0:T(8,128)S(1)}, u32[]{:S(2)}, u32[]{:S(2)}) collective-permute-start(f32[104,128]{1,0:T(8,128)S(1)} %slice_add_fusion.7), channel_id=1, source_target_pairs={{0,16},{16,0},{1,17},{17,1},{2,18},{18,2},{3,19},{19,3},{4,20},{20... | collective-permute-start | bytes 159752 | tf_op jit(solution)/shard_map/ppermute | solution.py:45
  75.1 13.5 %collective-permute-start.15 = (f32[800,128]{1,0:T(8,128)S(1)}, f32[800,128]{1,0:T(8,128)S(1)}, u32[]{:S(2)}, u32[]{:S(2)}) collective-permute-start(f32[800,128]{1,0:T(8,128)S(1)} %right_sum.2), channel_id=1, source_target_pairs={{0,16},{16,0},{1,17},{17,1},{2,18},{18,2},{3,19},{19,3},{4,20},{20... | collective-permute-start | bytes 1228808 | tf_op jit(solution)/shard_map/ppermute | solution.py:45
  78.3 7.9 %collective-permute-start.12 = (f32[104,128]{1,0:T(8,128)S(1)}, f32[104,128]{1,0:T(8,128)S(1)}, u32[]{:S(2)}, u32[]{:S(2)}) collective-permute-start(f32[104,128]{1,0:T(8,128)S(1)} %add.42), channel_id=1, source_target_pairs={{0,8},{1,9},{2,10},{3,11},{4,12},{5,13},{6,14},{7,15},{8,0},{9,1},... | collective-permute-start | bytes 159752 | tf_op jit(solution)/shard_map/ppermute | solution.py:45
  86.4 8.7 %collective-permute-start.13 = (f32[408,128]{1,0:T(8,128)S(1)}, f32[408,128]{1,0:T(8,128)S(1)}, u32[]{:S(2)}, u32[]{:S(2)}) collective-permute-start(f32[408,128]{1,0:T(8,128)S(1)} %pad_maximum_fusion.3), channel_id=1, source_target_pairs={{0,4},{1,5},{2,6},{3,7},{4,0},{5,1},{6,2},{7,3},{8,12},{9,13},{10,... | collective-permute-start | bytes 626696 | tf_op jit(solution)/shard_map/ppermute | solution.py:45
  86.5 8.6 %collective-permute-start.14 = (f32[304,128]{1,0:T(8,128)S(1)}, f32[304,128]{1,0:T(8,128)S(1)}, u32[]{:S(2)}, u32[]{:S(2)}) collective-permute-start(f32[304,128]{1,0:T(8,128)S(1)} %slice.101), channel_id=1, source_target_pairs={{0,8},{1,9},{2,10},{3,11},{4,12},{5,13},{6,14},{7,15},{8,0},{9,1},... | collective-permute-start | bytes 466952 | tf_op jit(solution)/shard_map/ppermute | solution.py:45
  95.3 7.4 %collective-permute-start.17 = (f32[256,128]{1,0:T(8,128)S(1)}, f32[256,128]{1,0:T(8,128)S(1)}, u32[]{:S(2)}, u32[]{:S(2)}) collective-permute-start(f32[256,128]{1,0:T(8,128)S(1)} %pad_maximum_fusion.6), channel_id=1, source_target_pairs={{0,2},{1,3},{2,0},{3,1},{4,6},{5,7},{6,4},{7,5},{8,10},{9,11},{10,... | collective-permute-start | bytes 393224 | tf_op jit(solution)/shard_map/ppermute | solution.py:45
  97.0 5.7 %collective-permute-start.16 = (f32[152,128]{1,0:T(8,128)S(1)}, f32[152,128]{1,0:T(8,128)S(1)}, u32[]{:S(2)}, u32[]{:S(2)}) collective-permute-start(f32[152,128]{1,0:T(8,128)S(1)} %slice.105), channel_id=1, source_target_pairs={{0,8},{1,9},{2,10},{3,11},{4,12},{5,13},{6,14},{7,15},{8,0},{9,1},... | collective-permute-start | bytes 233480 | tf_op jit(solution)/shard_map/ppermute | solution.py:45
  98.3 3.6 %collective-permute-start.19 = (f32[104,128]{1,0:T(8,128)S(1)}, f32[104,128]{1,0:T(8,128)S(1)}, u32[]{:S(2)}, u32[]{:S(2)}) collective-permute-start(f32[104,128]{1,0:T(8,128)S(1)} %slice_add_fusion.6.refs_4_), channel_id=1, source_target_pairs={{0,3},{1,2},{2,1},{3,0},{4,7},{5,6},{6,5},{7,4},{8,11},{9,10},{10,... | collective-permute-start | bytes 159752 | tf_op jit(solution)/shard_map/ppermute | solution.py:45
  98.3 3.6 %collective-permute-start.18 = (f32[104,128]{1,0:T(8,128)S(1)}, f32[104,128]{1,0:T(8,128)S(1)}, u32[]{:S(2)}, u32[]{:S(2)}) collective-permute-start(f32[104,128]{1,0:T(8,128)S(1)} %slice_add_fusion.6.refs_4_), channel_id=1, source_target_pairs={{0,1},{1,0},{2,3},{3,2},{4,5},{5,4},{6,7},{7,6},{8,9},{9,8},{10,11... | collective-permute-start | bytes 159752 | tf_op jit(solution)/shard_map/ppermute | solution.py:45
  (18 other events, 98.4 us)

commit v7 on v6

--- a/solution.py
+++ b/solution.py
@@ -333,12 +333,13 @@
 
         fetched, weighed, rel_total = {}, {}, 0.0
         for turn in range(len(spans) + 2):
+            if 0 <= turn - 1 < len(spans):
+                weighed[turn - 1] = weigh(turn - 1, fetched[turn - 1][1])
             if turn < len(spans):
                 fetched[turn] = fetch(turn)
-            if 0 <= turn - 1 < len(spans):
-                weighed[turn - 1] = weigh(turn - 1, fetched[turn - 1][1])
             if 0 <= turn - 2 < len(spans):
                 rel_total += back(turn - 2, fetched[turn - 2][0], weighed[turn - 2])
+
         grad_rel_ref[...] += rel_total
 
     active = start < where_ref[0]
@@ -395,7 +396,14 @@
                 first = (span(g, piece) + SPAN) // WINDOW
                 return lax.fori_loop(first, (bound_ref[g, piece + 1] + WINDOW - 1) // WINDOW, window_step, carry)
 
-            lax.fori_loop(0, groups, rest_step, 0)
+            more = bound_ref[0, piece + 1] > span(0, piece) + SPAN
+            for g in range(1, groups):
+                more = more | (bound_ref[g, piece + 1] > span(g, piece) + SPAN)
+
+            @pl.when(more)
+            def _():
+                lax.fori_loop(0, groups, rest_step, 0)
+
             size = packed_rows(chunk)
             for k in range(rows // chunk):
                 there = pl.ds(pl.multiple_of((piece - shift) * (rows // chunk) * size + k * size, 8), size)

time: 106 us -> 106 us (level)
  Pallas kernels: 50.6 us -> 55.6 us
  starting transfers between devices: 27.6 us -> 22.6 us
    pallas_call x1, Pallas kernels: 27.5 us -> 32.5 us  [body(): pl.pallas_call(functools.partial(edge_kernel, rows, chunk, tail), grid=(g...]
    ppermute x20, starting transfers between devices: 27.6 us -> 22.6 us  [swap(): return lax.ppermute(array, axis, [(i, i ^ bit) for i in range(size)])]
  transfers between devices with their start and end apart: 20 -> 20, of which waited for: 7 -> 6; matrix products, arithmetic and copies ran while one was open for 4% -> 4% of each run, Pallas kernels for 20% -> 20%
where the time goes in v7:
time: 106 us
  Pallas kernels  55.6 us (52%)
  starting transfers between devices  22.6 us (21%)
  waiting for transfers between devices  15.9 us (15%)
  local copies, waits for them, and re-layouts  5.11 us (5%)
  other arithmetic  4.85 us (5%)
  between operations  1.82 us (2%)
    pallas_call x1, Pallas kernels, body(): pl.pallas_call(functools.partial(edge_kernel, rows, chunk, tail), grid=(g...  32.5 us
    ppermute x20, starting transfers between devices, swap(): return lax.ppermute(array, axis, [(i, i ^ bit) for i in range(size)])  22.6 us
    ppermute x20, waiting for transfers between devices, swap(): return lax.ppermute(array, axis, [(i, i ^ bit) for i in range(size)])  15.9 us
    pallas_call x2, Pallas kernels, right_sum(): pl.pallas_call(functools.partial(right_kernel, tail), grid=(groups,), in_...  10.2 us
    pallas_call x1, Pallas kernels, prepare(): pl.pallas_call(functools.partial(prep_kernel, n_row, n_col, left_share, r...  7.88 us
    pallas_call x2, Pallas kernels, finish(): pl.pallas_call(functools.partial(finish_kernel, jobs, tail, len(grads)),...  5.01 us
    unnamed x44, local copies, waits for them, and re-layouts  3.83 us
  transfers between devices with their start and end apart: 20, of which 6 were waited for; matrix products, arithmetic and copies ran while one was open for 4% of the time, Pallas kernels for 20%

profile of v7, /device:TPU:0, one launch (start us, length us, event | category | flops | bytes accessed | tf_op | source)
XLA Modules:
  0.0 105.8 jit_solution(6878087158064529196)
XLA Ops:
  2.5 4.1 %collective-permute-start = (bf16[48,512]{1,0:T(8,128)(2,1)S(1)}, bf16[48,512]{1,0:T(8,128)(2,1)S(1)}, u32[]{:S(2)}, u32[]{:S(2)}) collective-permute-start(bf16[48,512]{1,0:T(8,128)(2,1)S(1)} %get-tuple-element.86), channel_id=1, source_target_pairs={{0,8},{1,9},{2,10},{3,11},{4,12},{5,13},{6,14},{7,15},{8,0},{9,1},... | collective-permute-start | bytes 147464 | tf_op jit(solution)/shard_map/ppermute | solution.py:45
  6.6 1.5 %collective-permute-start.1 = (bf16[48,512]{1,0:T(8,128)(2,1)S(1)}, bf16[48,512]{1,0:T(8,128)(2,1)S(1)}, u32[]{:S(2)}, u32[]{:S(2)}) collective-permute-start(bf16[48,512]{1,0:T(8,128)(2,1)S(1)} %get-tuple-element.87), channel_id=1, source_target_pairs={{0,2},{1,3},{2,0},{3,1},{4,6},{5,7},{6,4},{7,5},{8,10},{9,11},{10,... | collective-permute-start | bytes 147464 | tf_op jit(solution)/shard_map/ppermute | solution.py:45
  8.1 1.0 bitcast_convert_fusion
  9.3 1.6 %collective-permute-start.6 = (bf16[256,512]{0,1:T(8,128)(2,1)S(1)}, bf16[256,512]{0,1:T(8,128)(2,1)S(1)}, u32[]{:S(2)}, u32[]{:S(2)}) collective-permute-start(bf16[256,512]{0,1:T(8,128)(2,1)S(1)} %pad_maximum_fusion.2), channel_id=1, source_target_pairs={{0,16},{16,0},{1,17},{17,1},{2,18},{18,2},{3,19},{19,3},{4,20},{20... | collective-permute-start | bytes 786440 | tf_op jit(solution)/shard_map/ppermute | solution.py:45
  11.6 1.6 %collective-permute-start.2 = (bf16[96,512]{1,0:T(8,128)(2,1)S(1)}, bf16[96,512]{1,0:T(8,128)(2,1)S(1)}, u32[]{:S(2)}, u32[]{:S(2)}) collective-permute-start(bf16[96,512]{1,0:T(8,128)(2,1)S(1)} %get-tuple-element.92), channel_id=1, source_target_pairs={{0,4},{1,5},{2,6},{3,7},{4,0},{5,1},{6,2},{7,3},{8,12},{9,13},{10,... | collective-permute-start | bytes 294920 | tf_op jit(solution)/shard_map/ppermute | solution.py:45
  13.8 7.9 %prep.1 = (s32[4,8,1024]{2,1,0:T(8,128)S(1)}, f32[4,1,512]{2,1,0:T(1,128)S(1)}, s32[4,1,128]{2,1,0:T(1,128)S(1)}) custom-call(s32[3]{0:T(128)S(1)} %pad_add_fusion.where_ref, s32[1,4000]{1,0:T(1,128)S(1)} %bitcast.23, s32[1,4000]{1,0:T(1,128)S(1)} %bitcast.24, s32[1,4000]{1,0:T(1,128)S(1)} %bitcast.25, s32[4,1000]{1,0:T(4,128)S(1)} %bitcast.26), custom_call_target="tpu_custom_call" | custom-call | flops 67108864 | bytes 131072 | tf_op jit(solution)/shard_map/prep/pallas_call | solution.py:463
  21.8 1.6 %collective-permute-start.4 = (bf16[192,512]{1,0:T(8,128)(2,1)S(1)}, bf16[192,512]{1,0:T(8,128)(2,1)S(1)}, u32[]{:S(2)}, u32[]{:S(2)}) collective-permute-start(bf16[192,512]{1,0:T(8,128)(2,1)S(1)} %pad_maximum_fusion.4), channel_id=1, source_target_pairs={{0,2},{1,3},{2,0},{3,1},{4,6},{5,7},{6,4},{7,5},{8,10},{9,11},{10,... | collective-permute-start | bytes 589832 | tf_op jit(solution)/shard_map/ppermute | solution.py:45
  24.1 3.4 %collective-permute-done.4 = bf16[192,512]{1,0:T(8,128)(2,1)S(1)} collective-permute-done((bf16[192,512]{1,0:T(8,128)(2,1)S(1)}, bf16[192,512]{1,0:T(8,128)(2,1)S(1)}, u32[]{:S(2)}, u32[]{:S(2)}) %collective-permute-start.4) | collective-permute-done | bytes 196640 | tf_op jit(solution)/shard_map/ppermute | solution.py:45
  27.5 1.5 %collective-permute-done.5 = bf16[192,512]{1,0:T(8,128)(2,1)S(1)} collective-permute-done((bf16[192,512]{1,0:T(8,128)(2,1)S(1)}, bf16[192,512]{1,0:T(8,128)(2,1)S(1)}, u32[]{:S(2)}, u32[]{:S(2)}) %collective-permute-start.5) | collective-permute-done | bytes 196640 | tf_op jit(solution)/shard_map/ppermute | solution.py:45
  29.2 1.0 copy.17.right_ref
  30.2 1.3 %collective-permute-done.7.other_ref = bf16[768,512]{1,0:T(8,128)(2,1)S(1)} collective-permute-done((bf16[768,512]{1,0:T(8,128)(2,1)S(1)}, bf16[768,512]{1,0:T(8,128)(2,1)S(1)}, u32[]{:S(2)}, u32[]{:S(2)}) %collective-permute-start.7) | collective-permute-done | bytes 786464 | tf_op jit(solution)/shard_map/ppermute | solution.py:45
  32.3 32.5 %edges.1 = (bf16[4096,512]{1,0:T(8,128)(2,1)}, bf16[4096,512]{1,0:T(8,128)(2,1)}, bf16[4096,512]{1,0:T(8,128)(2,1)}, f32[2536,128]{1,0:T(8,128)}, f32[2536,128]{1,0:T(8,128)}) custom-call(s32[3]{0:T(128)} %copy-done.3, s32[4,128]{1,0:T(4,128)} %bitcast.22, s32[4,8,1024]{2,1,0:T(8,128)} %copy-done.1, f32[4,1,512]{2,1,0:T(1,128)} %copy-done.2, ...), custom_call_target="tpu_custom_call" | custom-call | tf_op jit(solution)/shard_map/edges/pallas_call | solution.py:505
  65.0 2.2 %copy-done = bf16[4096,512]{1,0:T(8,128)(2,1)S(1)} copy-done((bf16[4096,512]{1,0:T(8,128)(2,1)S(1)}, bf16[4096,512]{1,0:T(8,128)(2,1)}, u32[]{:S(2)}) %copy-start) | copy-done | bytes 4194328
  67.1 5.2 %right_sum.2 = f32[800,128]{1,0:T(8,128)S(1)} custom-call(bf16[4096,512]{1,0:T(8,128)(2,1)S(1)} %copy-done, bf16[4096,512]{1,0:T(8,128)(2,1)} %get-tuple-element.135.c_hi_ref, bf16[4096,512]{1,0:T(8,128)(2,1)} %get-tuple-element.136.c_lo_ref), custom_call_target="tpu_custom_call" | custom-call | flops 2147483648 | bytes 8388608 | tf_op jit(solution)/shard_map/right_sum/pallas_call | solution.py:547
  72.7 2.0 %collective-permute-start.9 = (f32[608,128]{1,0:T(8,128)S(1)}, f32[608,128]{1,0:T(8,128)S(1)}, u32[]{:S(2)}, u32[]{:S(2)}) collective-permute-start(f32[608,128]{1,0:T(8,128)S(1)} %slice.96), channel_id=1, source_target_pairs={{0,2},{1,3},{2,0},{3,1},{4,6},{5,7},{6,4},{7,5},{8,10},{9,11},{10,... | collective-permute-start | bytes 933896 | tf_op jit(solution)/shard_map/ppermute | solution.py:45
  74.7 2.0 %collective-permute-start.15 = (f32[800,128]{1,0:T(8,128)S(1)}, f32[800,128]{1,0:T(8,128)S(1)}, u32[]{:S(2)}, u32[]{:S(2)}) collective-permute-start(f32[800,128]{1,0:T(8,128)S(1)} %right_sum.2), channel_id=1, source_target_pairs={{0,16},{16,0},{1,17},{17,1},{2,18},{18,2},{3,19},{19,3},{4,20},{20... | collective-permute-start | bytes 1228808 | tf_op jit(solution)/shard_map/ppermute | solution.py:45
  76.7 2.7 %collective-permute-done.11 = f32[104,128]{1,0:T(8,128)S(1)} collective-permute-done((f32[104,128]{1,0:T(8,128)S(1)}, f32[104,128]{1,0:T(8,128)S(1)}, u32[]{:S(2)}, u32[]{:S(2)}) %collective-permute-start.11) | collective-permute-done | bytes 53280 | tf_op jit(solution)/shard_map/ppermute | solution.py:45
  79.4 2.7 %collective-permute-start.12 = (f32[104,128]{1,0:T(8,128)S(1)}, f32[104,128]{1,0:T(8,128)S(1)}, u32[]{:S(2)}, u32[]{:S(2)}) collective-permute-start(f32[104,128]{1,0:T(8,128)S(1)} %add.42), channel_id=1, source_target_pairs={{0,8},{1,9},{2,10},{3,11},{4,12},{5,13},{6,14},{7,15},{8,0},{9,1},... | collective-permute-start | bytes 159752 | tf_op jit(solution)/shard_map/ppermute | solution.py:45
  82.0 5.0 %right_sum.3 = f32[800,128]{1,0:T(8,128)S(1)} custom-call(bf16[4096,512]{1,0:T(8,128)(2,1)S(1)} %copy-done, bf16[4096,512]{1,0:T(8,128)(2,1)} %get-tuple-element.135.c_hi_ref, bf16[4096,512]{1,0:T(8,128)(2,1)} %get-tuple-element.136.c_lo_ref), custom_call_target="tpu_custom_call" | custom-call | flops 2147483648 | bytes 8388608 | tf_op jit(solution)/shard_map/right_sum/pallas_call | solution.py:547
  89.5 6.8 %collective-permute-done.14 = f32[304,128]{1,0:T(8,128)S(1)} collective-permute-done((f32[304,128]{1,0:T(8,128)S(1)}, f32[304,128]{1,0:T(8,128)S(1)}, u32[]{:S(2)}, u32[]{:S(2)}) %collective-permute-start.14) | collective-permute-done | bytes 155680 | tf_op jit(solution)/shard_map/ppermute | solution.py:45
  96.8 1.3 %collective-permute-start.16 = (f32[152,128]{1,0:T(8,128)S(1)}, f32[152,128]{1,0:T(8,128)S(1)}, u32[]{:S(2)}, u32[]{:S(2)}) collective-permute-start(f32[152,128]{1,0:T(8,128)S(1)} %slice.105), channel_id=1, source_target_pairs={{0,8},{1,9},{2,10},{3,11},{4,12},{5,13},{6,14},{7,15},{8,0},{9,1},... | collective-permute-start | bytes 233480 | tf_op jit(solution)/shard_map/ppermute | solution.py:45
  98.2 1.6 %collective-permute-start.18 = (f32[104,128]{1,0:T(8,128)S(1)}, f32[104,128]{1,0:T(8,128)S(1)}, u32[]{:S(2)}, u32[]{:S(2)}) collective-permute-start(f32[104,128]{1,0:T(8,128)S(1)} %slice_add_fusion.6.refs_4_), channel_id=1, source_target_pairs={{0,1},{1,0},{2,3},{3,2},{4,5},{5,4},{6,7},{7,6},{8,9},{9,8},{10,11... | collective-permute-start | bytes 159752 | tf_op jit(solution)/shard_map/ppermute | solution.py:45
  99.8 2.6 %new_right.1 = (f32[400,256]{1,0:T(8,128)}, f32[1,256]{1,0:T(1,128)}) custom-call(s32[3]{0:T(128)} %copy-done.3, f32[800,128]{1,0:T(8,128)} %add.46.refs_0_, f32[400,256]{1,0:T(8,128)} %bitcast.28, f32[1,256]{1,0:T(1,128)} %refs_2_.1), custom_call_target="tpu_custom_call" | custom-call | tf_op jit(solution)/shard_map/new_right/pallas_call | solution.py:228
  103.4 2.4 %new_left_rel.1 = (f32[96,400]{1,0:T(8,128)}, f32[1,96]{1,0:T(1,128)}, f32[64,400]{1,0:T(8,128)}, f32[1,64]{1,0:T(1,128)}) custom-call(s32[3]{0:T(128)} %copy-done.3, f32[304,128]{1,0:T(8,128)} %copy-done.12, f32[152,128]{1,0:T(8,128)} %copy-done.18, f32[304,128]{1,0:T(8,128)} %copy-done.13, f32[256,128]{1,0:T(8,128)} %copy-done.17, f32[104,128]{1,0:T(8,128)} %copy-done.16, ...), custom_call_target="tpu_custom_call" | custom-call | tf_op jit(solution)/shard_map/new_left_rel/pallas_call | solution.py:228
  (104 shorter events, 8.6 us)
Async XLA Ops:
  0.6 13.0 %copy-start.15 = (f32[64,400]{1,0:T(8,128)S(1)}, f32[64,400]{1,0:T(8,128)}, u32[]{:S(2)}) copy-start(f32[64,400]{1,0:T(8,128)} %refs_9_.1) | copy-start | bytes 307204
  1.6 12.1 %copy-start.5 = (s32[1,1,4000]{2,1,0:T(1,128)S(1)}, s32[1,1,4000]{2,1,0:T(1,128)}, u32[]{:S(2)}) copy-start(s32[1,1,4000]{2,1,0:T(1,128)} %param.17) | copy-start | bytes 48004
  1.6 12.1 %copy-start.6 = (s32[1,1,4000]{2,1,0:T(1,128)S(1)}, s32[1,1,4000]{2,1,0:T(1,128)}, u32[]{:S(2)}) copy-start(s32[1,1,4000]{2,1,0:T(1,128)} %param.18) | copy-start | bytes 48004
  2.5 9.1 %collective-permute-start = (bf16[48,512]{1,0:T(8,128)(2,1)S(1)}, bf16[48,512]{1,0:T(8,128)(2,1)S(1)}, u32[]{:S(2)}, u32[]{:S(2)}) collective-permute-start(bf16[48,512]{1,0:T(8,128)(2,1)S(1)} %get-tuple-element.86), channel_id=1, source_target_pairs={{0,8},{1,9},{2,10},{3,11},{4,12},{5,13},{6,14},{7,15},{8,0},{9,1},... | collective-permute-start | bytes 147464 | tf_op jit(solution)/shard_map/ppermute | solution.py:45
  6.6 5.0 %collective-permute-start.1 = (bf16[48,512]{1,0:T(8,128)(2,1)S(1)}, bf16[48,512]{1,0:T(8,128)(2,1)S(1)}, u32[]{:S(2)}, u32[]{:S(2)}) collective-permute-start(bf16[48,512]{1,0:T(8,128)(2,1)S(1)} %get-tuple-element.87), channel_id=1, source_target_pairs={{0,2},{1,3},{2,0},{3,1},{4,6},{5,7},{6,4},{7,5},{8,10},{9,11},{10,... | collective-permute-start | bytes 147464 | tf_op jit(solution)/shard_map/ppermute | solution.py:45
  9.3 14.8 %collective-permute-start.6 = (bf16[256,512]{0,1:T(8,128)(2,1)S(1)}, bf16[256,512]{0,1:T(8,128)(2,1)S(1)}, u32[]{:S(2)}, u32[]{:S(2)}) collective-permute-start(bf16[256,512]{0,1:T(8,128)(2,1)S(1)} %pad_maximum_fusion.2), channel_id=1, source_target_pairs={{0,16},{16,0},{1,17},{17,1},{2,18},{18,2},{3,19},{19,3},{4,20},{20... | collective-permute-start | bytes 786440 | tf_op jit(solution)/shard_map/ppermute | solution.py:45
  11.6 17.4 %copy-start.3 = (s32[3]{0:T(128)}, s32[3]{0:T(128)S(1)}, u32[]{:S(2)}) copy-start(s32[3]{0:T(128)S(1)} %pad_add_fusion.where_ref) | copy-start | bytes 40
  11.6 10.1 %collective-permute-start.2 = (bf16[96,512]{1,0:T(8,128)(2,1)S(1)}, bf16[96,512]{1,0:T(8,128)(2,1)S(1)}, u32[]{:S(2)}, u32[]{:S(2)}) collective-permute-start(bf16[96,512]{1,0:T(8,128)(2,1)S(1)} %get-tuple-element.92), channel_id=1, source_target_pairs={{0,4},{1,5},{2,6},{3,7},{4,0},{5,1},{6,2},{7,3},{8,12},{9,13},{10,... | collective-permute-start | bytes 294920 | tf_op jit(solution)/shard_map/ppermute | solution.py:45
  13.3 8.4 %collective-permute-start.3 = (bf16[96,512]{1,0:T(8,128)(2,1)S(1)}, bf16[96,512]{1,0:T(8,128)(2,1)S(1)}, u32[]{:S(2)}, u32[]{:S(2)}) collective-permute-start(bf16[96,512]{1,0:T(8,128)(2,1)S(1)} %get-tuple-element.93), channel_id=1, source_target_pairs={{0,8},{1,9},{2,10},{3,11},{4,12},{5,13},{6,14},{7,15},{8,0},{9,1},... | collective-permute-start | bytes 294920 | tf_op jit(solution)/shard_map/ppermute | solution.py:45
  21.8 5.7 %collective-permute-start.4 = (bf16[192,512]{1,0:T(8,128)(2,1)S(1)}, bf16[192,512]{1,0:T(8,128)(2,1)S(1)}, u32[]{:S(2)}, u32[]{:S(2)}) collective-permute-start(bf16[192,512]{1,0:T(8,128)(2,1)S(1)} %pad_maximum_fusion.4), channel_id=1, source_target_pairs={{0,2},{1,3},{2,0},{3,1},{4,6},{5,7},{6,4},{7,5},{8,10},{9,11},{10,... | collective-permute-start | bytes 589832 | tf_op jit(solution)/shard_map/ppermute | solution.py:45
  23.3 5.7 %collective-permute-start.5 = (bf16[192,512]{1,0:T(8,128)(2,1)S(1)}, bf16[192,512]{1,0:T(8,128)(2,1)S(1)}, u32[]{:S(2)}, u32[]{:S(2)}) collective-permute-start(bf16[192,512]{1,0:T(8,128)(2,1)S(1)} %pad_maximum_fusion.5), channel_id=1, source_target_pairs={{0,4},{1,5},{2,6},{3,7},{4,0},{5,1},{6,2},{7,3},{8,12},{9,13},{10,... | collective-permute-start | bytes 589832 | tf_op jit(solution)/shard_map/ppermute | solution.py:45
  29.1 2.4 %collective-permute-start.7 = (bf16[768,512]{1,0:T(8,128)(2,1)S(1)}, bf16[768,512]{1,0:T(8,128)(2,1)S(1)}, u32[]{:S(2)}, u32[]{:S(2)}) collective-permute-start(bf16[768,512]{1,0:T(8,128)(2,1)S(1)} %pad_maximum_fusion.own_ref), channel_id=1, source_target_pairs={{0,1},{1,0},{2,3},{3,2},{4,5},{5,4},{6,7},{7,6},{8,9},{9,8},{10,11... | collective-permute-start | bytes 2359304 | tf_op jit(solution)/shard_map/ppermute | solution.py:45
  64.9 7.4 %collective-permute-start.8 = (f32[2536,128]{1,0:T(8,128)}, f32[2536,128]{1,0:T(8,128)S(1)}, u32[]{:S(2)}, u32[]{:S(2)}) collective-permute-start(f32[2536,128]{1,0:T(8,128)} %get-tuple-element.117), channel_id=1, source_target_pairs={{0,1},{1,0},{2,3},{3,2},{4,5},{5,4},{6,7},{7,6},{8,9},{9,8},{10,11... | collective-permute-start | bytes 3895304 | tf_op jit(solution)/shard_map/ppermute | solution.py:45
  72.6 14.5 %collective-permute-start.10 = (f32[608,128]{1,0:T(8,128)S(1)}, f32[608,128]{1,0:T(8,128)S(1)}, u32[]{:S(2)}, u32[]{:S(2)}) collective-permute-start(f32[608,128]{1,0:T(8,128)S(1)} %slice.97), channel_id=1, source_target_pairs={{0,4},{1,5},{2,6},{3,7},{4,0},{5,1},{6,2},{7,3},{8,12},{9,13},{10,... | collective-permute-start | bytes 933896 | tf_op jit(solution)/shard_map/ppermute | solution.py:45
  72.7 14.4 %collective-permute-start.9 = (f32[608,128]{1,0:T(8,128)S(1)}, f32[608,128]{1,0:T(8,128)S(1)}, u32[]{:S(2)}, u32[]{:S(2)}) collective-permute-start(f32[608,128]{1,0:T(8,128)S(1)} %slice.96), channel_id=1, source_target_pairs={{0,2},{1,3},{2,0},{3,1},{4,6},{5,7},{6,4},{7,5},{8,10},{9,11},{10,... | collective-permute-start | bytes 933896 | tf_op jit(solution)/shard_map/ppermute | solution.py:45
  74.7 4.7 %collective-permute-start.11 = (f32[104,128]{1,0:T(8,128)S(1)}, f32[104,128]{1,0:T(8,128)S(1)}, u32[]{:S(2)}, u32[]{:S(2)}) collective-permute-start(f32[104,128]{1,0:T(8,128)S(1)} %slice_add_fusion.7), channel_id=1, source_target_pairs={{0,16},{16,0},{1,17},{17,1},{2,18},{18,2},{3,19},{19,3},{4,20},{20... | collective-permute-start | bytes 159752 | tf_op jit(solution)/shard_map/ppermute | solution.py:45
  74.7 14.0 %collective-permute-start.15 = (f32[800,128]{1,0:T(8,128)S(1)}, f32[800,128]{1,0:T(8,128)S(1)}, u32[]{:S(2)}, u32[]{:S(2)}) collective-permute-start(f32[800,128]{1,0:T(8,128)S(1)} %right_sum.2), channel_id=1, source_target_pairs={{0,16},{16,0},{1,17},{17,1},{2,18},{18,2},{3,19},{19,3},{4,20},{20... | collective-permute-start | bytes 1228808 | tf_op jit(solution)/shard_map/ppermute | solution.py:45
  79.4 7.7 %collective-permute-start.12 = (f32[104,128]{1,0:T(8,128)S(1)}, f32[104,128]{1,0:T(8,128)S(1)}, u32[]{:S(2)}, u32[]{:S(2)}) collective-permute-start(f32[104,128]{1,0:T(8,128)S(1)} %add.42), channel_id=1, source_target_pairs={{0,8},{1,9},{2,10},{3,11},{4,12},{5,13},{6,14},{7,15},{8,0},{9,1},... | collective-permute-start | bytes 159752 | tf_op jit(solution)/shard_map/ppermute | solution.py:45
  87.3 9.0 %collective-permute-start.13 = (f32[408,128]{1,0:T(8,128)S(1)}, f32[408,128]{1,0:T(8,128)S(1)}, u32[]{:S(2)}, u32[]{:S(2)}) collective-permute-start(f32[408,128]{1,0:T(8,128)S(1)} %pad_maximum_fusion.3), channel_id=1, source_target_pairs={{0,4},{1,5},{2,6},{3,7},{4,0},{5,1},{6,2},{7,3},{8,12},{9,13},{10,... | collective-permute-start | bytes 626696 | tf_op jit(solution)/shard_map/ppermute | solution.py:45
  88.0 8.3 %collective-permute-start.14 = (f32[304,128]{1,0:T(8,128)S(1)}, f32[304,128]{1,0:T(8,128)S(1)}, u32[]{:S(2)}, u32[]{:S(2)}) collective-permute-start(f32[304,128]{1,0:T(8,128)S(1)} %slice.101), channel_id=1, source_target_pairs={{0,8},{1,9},{2,10},{3,11},{4,12},{5,13},{6,14},{7,15},{8,0},{9,1},... | collective-permute-start | bytes 466952 | tf_op jit(solution)/shard_map/ppermute | solution.py:45
  96.4 6.3 %collective-permute-start.17 = (f32[256,128]{1,0:T(8,128)S(1)}, f32[256,128]{1,0:T(8,128)S(1)}, u32[]{:S(2)}, u32[]{:S(2)}) collective-permute-start(f32[256,128]{1,0:T(8,128)S(1)} %pad_maximum_fusion.6), channel_id=1, source_target_pairs={{0,2},{1,3},{2,0},{3,1},{4,6},{5,7},{6,4},{7,5},{8,10},{9,11},{10,... | collective-permute-start | bytes 393224 | tf_op jit(solution)/shard_map/ppermute | solution.py:45
  96.8 5.9 %collective-permute-start.16 = (f32[152,128]{1,0:T(8,128)S(1)}, f32[152,128]{1,0:T(8,128)S(1)}, u32[]{:S(2)}, u32[]{:S(2)}) collective-permute-start(f32[152,128]{1,0:T(8,128)S(1)} %slice.105), channel_id=1, source_target_pairs={{0,8},{1,9},{2,10},{3,11},{4,12},{5,13},{6,14},{7,15},{8,0},{9,1},... | collective-permute-start | bytes 233480 | tf_op jit(solution)/shard_map/ppermute | solution.py:45
  98.2 4.2 %collective-permute-start.19 = (f32[104,128]{1,0:T(8,128)S(1)}, f32[104,128]{1,0:T(8,128)S(1)}, u32[]{:S(2)}, u32[]{:S(2)}) collective-permute-start(f32[104,128]{1,0:T(8,128)S(1)} %slice_add_fusion.6.refs_4_), channel_id=1, source_target_pairs={{0,3},{1,2},{2,1},{3,0},{4,7},{5,6},{6,5},{7,4},{8,11},{9,10},{10,... | collective-permute-start | bytes 159752 | tf_op jit(solution)/shard_map/ppermute | solution.py:45
  98.2 4.2 %collective-permute-start.18 = (f32[104,128]{1,0:T(8,128)S(1)}, f32[104,128]{1,0:T(8,128)S(1)}, u32[]{:S(2)}, u32[]{:S(2)}) collective-permute-start(f32[104,128]{1,0:T(8,128)S(1)} %slice_add_fusion.6.refs_4_), channel_id=1, source_target_pairs={{0,1},{1,0},{2,3},{3,2},{4,5},{5,4},{6,7},{7,6},{8,9},{9,8},{10,11... | collective-permute-start | bytes 159752 | tf_op jit(solution)/shard_map/ppermute | solution.py:45
  (18 other events, 94.7 us)
